TPU v7x, 32 devices: a whole 2x2x4 slice. The times are simulated.
32 devices in a mesh: dp: 8 (over y, x, core), space: 4 (over z).
Axes of the slice: x: 2, y: 2, z: 4, core: 2. Of those that a mesh axis runs over, the one named last changes fastest.
Arguments:
- frames: bfloat16 [64, 64, 64, 64], P('dp', 'space'), may hold values from -16 to 16
- cotangent: bfloat16 [64, 64, 64, 64], P('dp', 'space'), may hold values from -5 to 5
- actions: int32 [64], P('dp'), may hold values from 0 to 17
- noise_ids: int32 [64], P('dp'), may hold values from 0 to 63
- games: int32 [64], P('dp'), may hold values from 0 to 25
- live_counts: int32 [8], P('dp'), may hold values from 2 to 8, as said below
- conv_weight: float32 [4032, 64], replicated, may hold values from -0.25 to 0.25
- conv_moment: float32 [4032, 64], replicated
- conv_square: float32 [4032, 64], replicated, as said below
- norm_map: float32 [4, 257, 128], replicated, may hold values from -0.1875 to 0.1875
- norm_moment: float32 [4, 257, 128], replicated
- norm_square: float32 [4, 257, 128], replicated, as said below
- emb_table: float32 [108, 256], replicated, may hold values from -3 to 3
- table_moment: float32 [108, 256], replicated
- table_square: float32 [108, 256], replicated, as said below
Outputs:
- result: bfloat16 [64, 64, 64, 64], P('dp', 'space')
- frames_grad: float32 [64, 64, 64, 64], P('dp', 'space')
- conv_moment_new: float32 [4032, 64], replicated
- conv_square_new: float32 [4032, 64], replicated
- conv_weight_new: float32 [4032, 64], replicated
- conv_weight_low: bfloat16 [4032, 64], replicated
- norm_moment_new: float32 [4, 257, 128], replicated
- norm_square_new: float32 [4, 257, 128], replicated
- norm_map_new: float32 [4, 257, 128], replicated
- norm_map_low: bfloat16 [4, 257, 128], replicated
- table_moment_new: float32 [108, 256], replicated
- table_square_new: float32 [108, 256], replicated
- emb_table_new: float32 [108, 256], replicated
- emb_table_low: bfloat16 [108, 256], replicated
Inputs may be any that keep to these rules, and one draw needn't show every extreme that they name: `live_counts`: every group's live frames are its first slots; some group uses all 8 slots. `conv_square`: positive. `norm_square`: positive. `table_square`: positive.
All inputs are finite; a program needn't handle non-finite values.
Results may differ from a plain program's by a relative error of at most 0.0092.
Values may be sent and summed in bfloat16 or wider, within the bound.
A program may use at most 128 MiB of HBM per device.

v0:
```python
import jax
import jax.numpy as jnp
from jax import lax
from jax.sharding import PartitionSpec as P

GROUPS = 2
ACTIONS = 18
NOISE_LEVELS = 64
ADAM_STEP = 4


NORM_EPSILON = 1e-05
ADAM_EPS = 1e-08
BETA_ONE = 0.5
BETA_TWO = 0.5
DECAY = 0.01
HIGH = lax.Precision.HIGHEST
DIMS = ("NHWC", "HWIO", "NHWC")
TAP_DIMS = ("CHWN", "IHWO", "HWNC")


def with_halo(block, sides, width):
    for axis, dim in sides:
        count = lax.axis_size(axis)
        forward = [(i, i + 1) for i in range(count - 1)]
        backward = [(target, source) for source, target in forward]
        low = lax.ppermute(
            lax.slice_in_dim(block, block.shape[dim] - width, None, axis=dim), axis, forward
        )
        high = lax.ppermute(lax.slice_in_dim(block, 0, width, axis=dim), axis, backward)
        block = jnp.concatenate([low, block, high], axis=dim)
    return block


def kernels(conv_weight):
    channel_width = conv_weight.shape[1]
    pieces = [
        conv_weight[k * 9 * channel_width : (k + 1) * 9 * channel_width].reshape(
            3, 3, channel_width, channel_width
        )
        for k in range(5)
    ]
    pieces.append(conv_weight[45 * channel_width :].reshape(3, 3, 2 * channel_width, channel_width))
    return pieces


def conv_rows(padded, kernel):
    return lax.conv_general_dilated(
        padded,
        kernel,
        (1, 1),
        ((0, 0), (1, 1)),
        dimension_numbers=DIMS,
        preferred_element_type=jnp.float32,
    )


def conv_whole(input_value, kernel):
    return lax.conv_general_dilated(
        input_value,
        kernel,
        (1, 1),
        ((1, 1), (1, 1)),
        dimension_numbers=DIMS,
        preferred_element_type=jnp.float32,
    )


def conv_stride(source, kernel):
    return lax.conv_general_dilated(
        source,
        kernel,
        (2, 2),
        ((0, 0), (1, 1)),
        dimension_numbers=DIMS,
        preferred_element_type=jnp.float32,
    )


def flipped(kernel):
    return jnp.transpose(kernel[::-1, ::-1], (0, 1, 3, 2))


def kernel_grad(source, grad_value, stride, padding):
    taps = lax.conv_general_dilated(
        source,
        grad_value,
        (1, 1),
        padding,
        rhs_dilation=(stride, stride),
        dimension_numbers=TAP_DIMS,
        preferred_element_type=jnp.float32,
    )
    return taps.reshape(-1, grad_value.shape[-1])


def stride_back(grad_value, kernel, height):
    rows_out = grad_value.shape[1]
    return lax.conv_general_dilated(
        grad_value,
        flipped(kernel),
        (1, 1),
        ((2, height + 1 - 2 * rows_out), (1, 2)),
        lhs_dilation=(2, 2),
        dimension_numbers=DIMS,
        preferred_element_type=jnp.float32,
    )


def swish_derivative(input_value):
    gate = jax.nn.sigmoid(input_value)
    return gate * (1.0 + input_value * (1.0 - gate))


def group_norm_forward(input_value, adaptive_modulation, element_count, grid_cells):
    count, height, breadth, channel_width = input_value.shape
    group_split_input = input_value.reshape(
        count, height * breadth, GROUPS, channel_width // GROUPS
    )
    first = jnp.sum(group_split_input, axis=(1, 3))
    second = jnp.sum(group_split_input * group_split_input, axis=(1, 3))
    first, second = element_count((first, second))
    group_mean = first / grid_cells
    group_variance = second / grid_cells - group_mean * group_mean
    scaled_activation = lax.rsqrt(group_variance + NORM_EPSILON)
    centered_normalized = (
        (group_split_input - group_mean[:, None, :, None]) * scaled_activation[:, None, :, None]
    ).reshape(input_value.shape)
    modulated = (
        centered_normalized * (1.0 + adaptive_modulation[:, None, None, :channel_width])
        + adaptive_modulation[:, None, None, channel_width:]
    )
    return (modulated, centered_normalized, scaled_activation)


def group_norm_backward(
    grad_value,
    centered_normalized,
    scaled_activation,
    adaptive_modulation,
    element_count,
    grid_cells,
):
    count, height, breadth, channel_width = grad_value.shape
    scale_grad = jnp.sum(grad_value * centered_normalized, axis=(1, 2))
    shift_grad = jnp.sum(grad_value, axis=(1, 2))
    upper_value = (grad_value * (1.0 + adaptive_modulation[:, None, None, :channel_width])).reshape(
        count, height * breadth, GROUPS, channel_width // GROUPS
    )
    normalized_input = centered_normalized.reshape(upper_value.shape)
    first = jnp.sum(upper_value, axis=(1, 3))
    second = jnp.sum(upper_value * normalized_input, axis=(1, 3))
    first, second = element_count((first, second))
    inner = (
        upper_value
        - first[:, None, :, None] / grid_cells
        - normalized_input * (second[:, None, :, None] / grid_cells)
    )
    return (
        (inner * scaled_activation[:, None, :, None]).reshape(grad_value.shape),
        jnp.concatenate([scale_grad, shift_grad], 1),
    )


def adamw(weight, moment, square, grad_value, rate):
    fix_one = 1.0 - BETA_ONE**ADAM_STEP
    fix_two = 1.0 - BETA_TWO**ADAM_STEP
    moment_new = BETA_ONE * moment + (1.0 - BETA_ONE) * grad_value
    square_new = BETA_TWO * square + (1.0 - BETA_TWO) * grad_value * grad_value
    fixed_m = moment_new / fix_one
    fixed_v = square_new / fix_two
    weight_new = weight - rate * (fixed_m / (jnp.sqrt(fixed_v) + ADAM_EPS) + DECAY * weight)
    return (moment_new, square_new, weight_new, weight_new.astype(jnp.bfloat16))


def local(
    frames,
    cotangent,
    actions,
    noise_ids,
    games,
    live_counts,
    conv_weight,
    conv_moment,
    conv_square,
    norm_map,
    norm_moment,
    norm_square,
    emb_table,
    table_moment,
    table_square,
):
    count, strip, breadth, channel_width = frames.shape
    spread = lax.axis_size("space")
    share = count // spread
    start = lax.axis_index("space") * share
    full_grid_cells = strip * spread * breadth * (channel_width // GROUPS)
    coarse_grid_cells = strip * spread // 2 * (breadth // 2) * (channel_width // GROUPS)
    rows_pad = ((0, 0), (1, 1))
    both_pad = ((1, 1), (1, 1))
    stride_pad = ((0, 0), (1, 0))

    def widen(input_value):
        return with_halo(input_value, (("space", 1),), 1)

    def widen_back(input_value):
        return with_halo(input_value, (("space", 1),), 1)

    def forward_element_count(pair):
        return lax.psum(pair, "space")

    def backward_element_count(pair):
        return lax.psum(pair, "space")

    def local_element_count(pair):
        return pair

    entries = jnp.arange(emb_table.shape[0], dtype=jnp.int32)[None, :]
    hits = (
        (entries == actions[:, None])
        | (entries == noise_ids[:, None] + ACTIONS)
        | (entries == games[:, None] + ACTIONS + NOISE_LEVELS)
    )
    multihot = hits.astype(jnp.float32)
    embedded = jnp.dot(multihot, emb_table, precision=HIGH)
    augmented = jnp.concatenate([embedded, jnp.ones((count, 1), jnp.float32)], 1)
    own_aug = lax.dynamic_slice_in_dim(augmented, start, share, 0)
    own_hot = lax.dynamic_slice_in_dim(multihot, start, share, 0)
    modulation_first = jnp.dot(augmented, norm_map[0], precision=HIGH)
    modulation_second = jnp.dot(augmented, norm_map[1], precision=HIGH)
    modulation_third = jnp.dot(own_aug, norm_map[2], precision=HIGH)
    modulation_fourth = jnp.dot(own_aug, norm_map[3], precision=HIGH)
    kern = [piece.astype(jnp.bfloat16) for piece in kernels(conv_weight)]
    source_input = frames.astype(jnp.float32)
    preactivation_one, centered_normalized_one, scaled_activation_one = group_norm_forward(
        source_input, modulation_first, forward_element_count, full_grid_cells
    )
    h_one_pad = widen(jax.nn.silu(preactivation_one).astype(jnp.bfloat16))
    conv_first_output = conv_rows(h_one_pad, kern[0])
    preactivation_two, centered_normalized_two, scaled_activation_two = group_norm_forward(
        conv_first_output, modulation_second, forward_element_count, full_grid_cells
    )
    h_two_pad = widen(jax.nn.silu(preactivation_two).astype(jnp.bfloat16))
    y_one = source_input + conv_rows(h_two_pad, kern[1])
    skip = y_one.astype(jnp.bfloat16)
    whole = lax.all_to_all(skip, "space", split_axis=0, concat_axis=1, tiled=True)
    source = jnp.pad(whole, ((0, 0), (1, 0), (0, 0), (0, 0)))
    down_value = conv_stride(source, kern[2])
    preactivation_three, centered_normalized_three, scaled_activation_three = group_norm_forward(
        down_value, modulation_third, local_element_count, coarse_grid_cells
    )
    h_three = jax.nn.silu(preactivation_three).astype(jnp.bfloat16)
    conv_third_output = conv_whole(h_three, kern[3])
    preactivation_four, centered_normalized_four, scaled_activation_four = group_norm_forward(
        conv_third_output, modulation_fourth, local_element_count, coarse_grid_cells
    )
    h_four = jax.nn.silu(preactivation_four).astype(jnp.bfloat16)
    y_two = down_value + conv_whole(h_four, kern[4])
    coarse_rows = lax.all_to_all(
        y_two.astype(jnp.bfloat16), "space", split_axis=1, concat_axis=0, tiled=True
    )
    upsampled = jnp.repeat(jnp.repeat(coarse_rows, 2, 1), 2, 2)
    joined_pad = widen(jnp.concatenate([skip, upsampled], -1))
    result = conv_rows(joined_pad, kern[5]).astype(jnp.bfloat16)
    live = (jnp.arange(count, dtype=jnp.int32) < live_counts[0]).astype(jnp.bfloat16)
    g_out = cotangent * live[:, None, None, None]
    g_joined = conv_rows(widen_back(g_out), flipped(kern[5]))
    g_merge = kernel_grad(joined_pad, g_out, 1, rows_pad)
    g_skip = g_joined[..., :channel_width]
    pooled = (
        g_joined[..., channel_width:]
        .reshape(count, strip // 2, 2, breadth // 2, 2, channel_width)
        .sum(axis=(2, 4))
    )
    g_coarse = lax.all_to_all(
        pooled.astype(jnp.bfloat16), "space", split_axis=0, concat_axis=1, tiled=True
    )
    g_four = kernel_grad(h_four, g_coarse, 1, both_pad)
    hidden_four_gradient = conv_whole(g_coarse, flipped(kern[4]))
    g_c_three, dmod_four = group_norm_backward(
        hidden_four_gradient * swish_derivative(preactivation_four),
        centered_normalized_four,
        scaled_activation_four,
        modulation_fourth,
        local_element_count,
        coarse_grid_cells,
    )
    g_c_three = g_c_three.astype(jnp.bfloat16)
    g_three = kernel_grad(h_three, g_c_three, 1, both_pad)
    g_h_three = conv_whole(g_c_three, flipped(kern[3]))
    g_d_norm, dmod_three = group_norm_backward(
        g_h_three * swish_derivative(preactivation_three),
        centered_normalized_three,
        scaled_activation_three,
        modulation_third,
        local_element_count,
        coarse_grid_cells,
    )
    g_d = (g_coarse.astype(jnp.float32) + g_d_norm).astype(jnp.bfloat16)
    g_down = kernel_grad(source, g_d, 2, stride_pad)
    g_source = stride_back(g_d, kern[2], source.shape[1])
    g_skip_down = lax.all_to_all(
        g_source[:, 1:].astype(jnp.bfloat16), "space", split_axis=1, concat_axis=0, tiled=True
    )
    g_y_one = g_skip + g_skip_down.astype(jnp.float32)
    g_c_two = g_y_one.astype(jnp.bfloat16)
    g_two = kernel_grad(h_two_pad, g_c_two, 1, rows_pad)
    hidden_two_gradient = conv_rows(widen_back(g_c_two), flipped(kern[1]))
    g_c_one, dmod_two = group_norm_backward(
        hidden_two_gradient * swish_derivative(preactivation_two),
        centered_normalized_two,
        scaled_activation_two,
        modulation_second,
        backward_element_count,
        full_grid_cells,
    )
    g_c_one = g_c_one.astype(jnp.bfloat16)
    g_one = kernel_grad(h_one_pad, g_c_one, 1, rows_pad)
    hidden_one_gradient = conv_rows(widen_back(g_c_one), flipped(kern[0]))
    g_x_norm, dmod_one = group_norm_backward(
        hidden_one_gradient * swish_derivative(preactivation_one),
        centered_normalized_one,
        scaled_activation_one,
        modulation_first,
        backward_element_count,
        full_grid_cells,
    )
    frames_grad = g_y_one + g_x_norm
    grad_conv = jnp.concatenate([g_one, g_two, g_down, g_three, g_four, g_merge], 0)
    grad_map = jnp.stack(
        [
            jnp.dot(augmented.T, dmod_one, precision=HIGH),
            jnp.dot(augmented.T, dmod_two, precision=HIGH),
            jnp.dot(own_aug.T, dmod_three, precision=HIGH),
            jnp.dot(own_aug.T, dmod_four, precision=HIGH),
        ]
    )
    g_embed = jnp.dot(dmod_one, norm_map[0].T, precision=HIGH) + jnp.dot(
        dmod_two, norm_map[1].T, precision=HIGH
    )
    g_own = jnp.dot(dmod_three, norm_map[2].T, precision=HIGH) + jnp.dot(
        dmod_four, norm_map[3].T, precision=HIGH
    )
    grad_table = jnp.dot(multihot.T, g_embed[:, :-1], precision=HIGH) + jnp.dot(
        own_hot.T, g_own[:, :-1], precision=HIGH
    )
    grad_conv, grad_map, grad_table = lax.psum((grad_conv, grad_map, grad_table), ("dp", "space"))
    conv_out = adamw(conv_weight, conv_moment, conv_square, grad_conv, 0.05)
    norm_out = adamw(norm_map, norm_moment, norm_square, grad_map, 0.04)
    table_out = adamw(emb_table, table_moment, table_square, grad_table, 0.5)
    return (
        result,
        frames_grad,
        conv_out[0],
        conv_out[1],
        conv_out[2],
        conv_out[3],
        norm_out[0],
        norm_out[1],
        norm_out[2],
        norm_out[3],
        table_out[0],
        table_out[1],
        table_out[2],
        table_out[3],
    )


def solution(mesh):
    in_specs = (
        P("dp", "space", None, None),
        P("dp", "space", None, None),
        P("dp"),
        P("dp"),
        P("dp"),
        P("dp"),
        P(),
        P(),
        P(),
        P(),
        P(),
        P(),
        P(),
        P(),
        P(),
    )
    out_specs = (
        P("dp", "space", None, None),
        P("dp", "space", None, None),
        P(),
        P(),
        P(),
        P(),
        P(),
        P(),
        P(),
        P(),
        P(),
        P(),
        P(),
        P(),
    )
    return jax.shard_map(local, mesh=mesh, in_specs=in_specs, out_specs=out_specs, check_vma=False)
```

profile of v0, /device:TPU:0, one launch (start us, length us, event | category | flops | bytes accessed | tf_op | source)
XLA Modules:
  0.0 532.4 jit_solution(15660101598035099480)
XLA Ops:
  7.8 3.0 copy_multiply_fusion
  12.9 5.6 %collective-permute-start.6 = (bf16[8,1,64,64]{3,0,2,1:T(8,128)(2,1)}, bf16[8,1,64,64]{3,0,2,1:T(8,128)(2,1)}, u32[]{:S(2)}, u32[]{:S(2)}) collective-permute-start(bf16[8,1,64,64]{3,0,2,1:T(8,128)(2,1)} %get-tuple-element.179), channel_id=1, source_target_pairs={{0,1},{1,2},{2,3},{4,5},{5,6},{6,7},{8,9},{9,10},{10,11},{12,13},{... | collective-permute-start | bytes 196616 | tf_op jit(solution)/shard_map/ppermute | solution.py:27
  22.3 13.0 %all-reduce.5 = (f32[8,2]{0,1:T(2,128)S(1)}, f32[8,2]{0,1:T(2,128)S(1)}) all-reduce(f32[8,2]{0,1:T(2,128)S(1)} %copy.664, f32[8,2]{0,1:T(2,128)S(1)} %copy.663), channel_id=1, replica_groups=mesh['dp'=8,'space'=4] {'space'}, use_global_device_ids=true, to_apply=%region_5.6 | all-reduce | flops 32 | bytes 256 | tf_op jit(solution)/shard_map/psum | solution.py:210
  36.9 2.6 fusion.13
  45.2 4.3 collective-permute-done.1
  49.4 6.7 %fusion.161 = (f32[8,64]{1,0:T(8,128)S(1)}, f32[8,64]{1,0:T(8,128)S(1)}, f32[8,16,64,64]{3,0,2,1:T(8,128)}) fusion(bf16[3,3,64,64]{3,2,1,0:T(8,128)(2,1)S(1)} %bitcast.251, bf16[8,1,64,64]{3,0,2,1:T(8,128)(2,1)} %collective-permute-done.1, bf16[8,16,64,64]{3,0,2,1:T(8,128)(2,1)} %copy-done.41, bf16[8,1,64,64]{3,0,2,1:T(8,128)(2,1)} %collective-permute-done), kind=kOutput, calls=%fused_computation.278 | convolution fusion | flops 602799104 | bytes 3354624 | tf_op jit(solution)/shard_map/conv_general_dilated | solution.py:48
  56.6 8.8 %all-reduce.4 = (f32[8,2]{0,1:T(2,128)S(1)}, f32[8,2]{0,1:T(2,128)S(1)}) all-reduce(f32[8,2]{0,1:T(2,128)S(1)} %copy.666, f32[8,2]{0,1:T(2,128)S(1)} %copy.665), channel_id=1, replica_groups=mesh['dp'=8,'space'=4] {'space'}, use_global_device_ids=true, to_apply=%region_11.12 | all-reduce | flops 32 | bytes 256 | tf_op jit(solution)/shard_map/psum | solution.py:210
  65.9 3.7 multiply_convert_fusion.1
  70.4 4.4 collective-permute-start.2
  76.1 4.0 fusion.31
  80.1 3.2 slice.215
  83.3 2.6 reduce_sum.361
  89.0 3.9 all-to-all-start.2
  92.9 5.4 %fusion.23 = bf16[8,16,64,64]{3,0,2,1:T(8,128)(2,1)S(1)} fusion(bf16[3,3,64,64]{3,2,1,0:T(8,128)(2,1)} %bitcast.253, bf16[8,1,64,64]{3,0,2,1:T(8,128)(2,1)} %collective-permute-done.3, bf16[8,16,64,64]{3,0,2,1:T(8,128)(2,1)} %copy-done.38, bf16[8,1,64,64]{3,0,2,1:T(8,128)(2,1)} %collective-permute-done.2, bf16[8,16,64,64]{3,2,1,0:T(8,128)(2,1)S(1)} %copy-done.3), kind=kOutput, calls=%fused_computation.29 | convolution fusion | flops 602800128 | bytes 3350528 | tf_op jit(solution)/shard_map/conv_general_dilated | solution.py:48
  100.2 2.7 reshape.348
  102.8 5.1 all-to-all-start
  114.3 12.6 %all-to-all-done = bf16[4,2,65536]{2,1,0:T(2,128)(2,1)} async-done(((bf16[4,2,65536]{2,1,0:T(2,128)(2,1)}), bf16[4,2,65536]{2,1,0:T(2,128)(2,1)}, u32[]{:S(2)}, u32[]{:S(2)}) %all-to-all-start) | async-done | bytes 1048608 | tf_op jit(solution)/shard_map/all_to_all | solution.py:246
  126.9 11.8 %reshape.349 = bf16[8,16,64,64]{3,2,1,0:T(8,128)(2,1)S(1)} reshape(bf16[4,2,65536]{2,1,0:T(2,128)(2,1)} %all-to-all-done) | data formatting | bytes 2097152
  141.0 2.5 pad.3
  147.9 4.2 fusion.108
  161.7 4.2 fusion.109
  173.8 4.5 all-to-all-start.1
  182.5 7.8 %fusion.170 = (f32[32,16,5,64]{3,1,2,0:T(8,128)S(1)}, f32[32,16,5,64]{3,1,2,0:T(8,128)}, f32[32,16,5,64]{3,1,2,0:T(8,128)}, f32[32,16,5,64]{3,1,2,0:T(8,128)}) fusion(f32[32,16,5,64]{3,1,2,0:T(8,128)} %get-tuple-element.168, f32[32,16,5,64]{3,0,2,1:T(8,128)S(1)} %bitcast.208, f32[32,16,5,64]{3,0,2,1:T(8,128)S(1)} %bitcast.210, ...), kind=kOutput, calls=%fused_computation.283 | convolution fusion | flops 187105280 | bytes 5120080 | tf_op jit(solution)/shard_map/conv_general_dilated | solution.py:59
  200.7 5.8 %fusion.168 = (f32[32,16,5,64]{3,1,2,0:T(8,128)S(1)}, f32[32,16,5,64]{3,1,2,0:T(8,128)S(1)}, f32[32,16,5,64]{3,1,2,0:T(8,128)}, f32[32,16,5,64]{3,1,2,0:T(8,128)}) fusion(f32[32,16,5,64]{3,1,2,0:T(8,128)S(1)} %copy-done.26, f32[32,16,5,64]{3,0,2,1:T(8,128)S(1)} %bitcast.204, f32[32,16,5,64]{3,0,2,1:T(8,128)S(1)} %bitcast.206, ...), kind=kOutput, calls=%fused_computation.282 | convolution fusion | flops 189235200 | bytes 5103616 | tf_op jit(solution)/shard_map/conv_general_dilated | solution.py:59
  207.4 2.8 copy.649
  216.9 4.9 fusion.111
  222.7 2.9 select_convert_fusion
  228.5 2.4 fusion.49
  240.9 2.7 copy.784
  243.6 4.5 reshape.354
  250.1 5.1 all-to-all-start.3
  258.9 3.9 collective-permute-start.4
  265.1 6.1 %collective-permute-done.4 = bf16[8,1,64,128]{3,0,2,1:T(8,128)(2,1)S(1)} collective-permute-done((bf16[8,1,64,128]{3,0,2,1:T(8,128)(2,1)S(1)}, bf16[8,1,64,128]{3,0,2,1:T(8,128)(2,1)S(1)}, u32[]{:S(2)}, u32[]{:S(2)}) %collective-permute-start.4) | collective-permute-done | bytes 131104 | tf_op jit(solution)/shard_map/ppermute | solution.py:27
  271.2 5.7 %convolution_convert_fusion = bf16[8,16,64,64]{3,0,2,1:T(8,128)(2,1)S(1)} fusion(bf16[3,3,128,64]{2,1,0,3:T(4,128)(2,1)S(1)} %copy-done.69, bf16[8,1,64,128]{3,0,2,1:T(8,128)(2,1)S(1)} %collective-permute-done.5, bf16[8,16,64,64]{3,0,2,1:T(8,128)(2,1)S(1)} %bitcast.190, bf16[8,16,64,64]{3,0,2,1:T(8,128)(2,1)S(1)} %copy-done.8, ...), kind=kOutput, calls=%fused_computation.78 | convolution fusion | flops 1205338112 | bytes 3555328 | tf_op jit(solution)/shard_map/conv_general_dilated | solution.py:48
  278.8 3.2 fusion.160
  282.5 3.1 reshape.355
  286.2 3.3 copy.626
  292.3 11.8 %collective-permute-start.8 = (bf16[8,1,64,64]{3,0,2,1:T(8,128)(2,1)}, bf16[8,1,64,64]{3,0,2,1:T(8,128)(2,1)}, u32[]{:S(2)}, u32[]{:S(2)}) collective-permute-start(bf16[8,1,64,64]{3,0,2,1:T(8,128)(2,1)} %get-tuple-element.177), channel_id=1, source_target_pairs={{0,1},{1,2},{2,3},{4,5},{5,6},{6,7},{8,9},{9,10},{10,11},{12,13},{... | collective-permute-start | bytes 196616 | tf_op jit(solution)/shard_map/ppermute | solution.py:27
  305.7 6.1 %fusion.78 = f32[3,3,64,64]{3,2,1,0:T(8,128)S(1)} fusion(bf16[8,16,64,64]{3,0,2,1:T(8,128)(2,1)S(1)} %fusion.56, bf16[8,1,64,64]{3,0,2,1:T(8,128)(2,1)} %collective-permute-done.3, bf16[8,16,64,64]{3,0,2,1:T(8,128)(2,1)S(1)} %copy-done.39, bf16[8,1,64,64]{3,0,2,1:T(8,128)(2,1)} %collective-permute-done.2), kind=kOutput, calls=%fused_computation.140 | convolution fusion | flops 601227264 | bytes 2375680 | tf_op jit(solution)/shard_map/conv_general_dilated | solution.py:85
  312.7 11.2 %multiply_reduce_fusion = (f32[8,64]{1,0:T(8,128)S(1)}, f32[8,64]{1,0:T(8,128)S(1)}, f32[8,64]{1,0:T(8,128)S(1)}, f32[8,64]{1,0:T(8,128)}, f32[8,16,64,64]{3,0,2,1:T(8,128)}) fusion(f32[8,16,64,64]{3,0,2,1:T(8,128)} %get-tuple-element.218, f32[8,64]{1,0:T(8,128)S(1)} %copy-done.82, f32[8,64]{1,0:T(8,128)S(1)} %copy-done.80, f32[8,64]{1,0:T(8,128)S(1)} %copy-done.84, ...), kind=kOutput, calls=%fused_computation.32 | convolution fusion | flops 611186688 | bytes 5464064 | tf_op jit(solution)/shard_map/conv_general_dilated | solution.py:48
  324.4 11.0 %all-reduce.3 = (f32[8,2]{0,1:T(2,128)S(1)}, f32[8,2]{0,1:T(2,128)S(1)}) all-reduce(f32[8,2]{0,1:T(2,128)S(1)} %copy.668, f32[8,2]{0,1:T(2,128)S(1)} %copy.667), channel_id=1, replica_groups=mesh['dp'=8,'space'=4] {'space'}, use_global_device_ids=true, to_apply=%region_34.35 | all-reduce | flops 32 | bytes 256 | tf_op jit(solution)/shard_map/psum | solution.py:213
  335.9 4.7 multiply_convert_fusion
  344.9 6.8 %fusion.79 = f32[3,3,64,64]{3,2,1,0:T(8,128)} fusion(bf16[8,16,64,64]{3,0,2,1:T(8,128)(2,1)S(1)} %multiply_convert_fusion, bf16[8,1,64,64]{3,0,2,1:T(8,128)(2,1)} %collective-permute-done.1, bf16[8,16,64,64]{3,0,2,1:T(8,128)(2,1)S(1)} %copy-done.42, bf16[8,1,64,64]{3,0,2,1:T(8,128)(2,1)} %collective-permute-done), kind=kOutput, calls=%fused_computation.141 | convolution fusion | flops 601227264 | bytes 2375680 | tf_op jit(solution)/shard_map/conv_general_dilated | solution.py:85
  357.8 12.6 %fusion.21 = (f32[8,64]{1,0:T(8,128)S(1)}, f32[8,64]{1,0:T(8,128)S(1)}, f32[8,64]{1,0:T(8,128)S(1)}, f32[8,64]{1,0:T(8,128)S(1)}, f32[8,16,64,64]{3,0,2,1:T(8,128)}) fusion(f32[8,64]{1,0:T(8,128)S(1)} %copy-done.88, f32[8,64]{1,0:T(8,128)S(1)} %copy-done.86, bf16[8,16,64,64]{3,2,1,0:T(8,128)(2,1)S(1)} %copy-done.4, f32[8,64]{1,0:T(8,128)S(1)} %copy-done.90, ...), kind=kOutput, calls=%fused_computation.27 | convolution fusion | flops 611710976 | bytes 4415488 | tf_op jit(solution)/shard_map/conv_general_dilated | solution.py:48
  371.6 11.6 %all-reduce.2 = (f32[8,2]{0,1:T(2,128)S(1)}, f32[8,2]{0,1:T(2,128)S(1)}) all-reduce(f32[8,2]{0,1:T(2,128)S(1)} %copy.670, f32[8,2]{0,1:T(2,128)S(1)} %copy.669), channel_id=1, replica_groups=mesh['dp'=8,'space'=4] {'space'}, use_global_device_ids=true, to_apply=%region_40.41 | all-reduce | flops 32 | bytes 256 | tf_op jit(solution)/shard_map/psum | solution.py:213
  385.4 6.4 %fusion.20 = f32[8,16,64,64]{3,0,2,1:T(8,128)S(1)} fusion(f32[8,16,64,64]{3,0,2,1:T(8,128)} %get-tuple-element.226, f32[8,64]{1,0:T(8,128)S(1)} %mul.468, f32[8,64]{1,0:T(8,128)S(1)} %sub.209, f32[8,64]{1,0:T(8,128)S(1)} %copy-done.90, f32[8,64]{1,0:T(8,128)S(1)} %copy-done.88, f32[8,64]{1,0:T(8,128)S(1)} %copy-done.86, f32[8,16,64,64]{3,0,2,1:T(8,128)} %bitcast.178, ...), kind=kLoop, calls=%fused_computation.26 | loop fusion | flops 5242880 | bytes 9447424 | tf_op jit(solution)/shard_map/add | solution.py:328
  391.9 2.8 copy.657
  394.6 122.0 %all-reduce.8.cloned.1.call-done = (f32[4032,64]{0,1:T(8,128)}, f32[4,257,128]{2,1,0:T(8,128)}, f32[108,256]{1,0:T(8,128)}) async-done(((f32[4032,64]{0,1:T(8,128)}, f32[4,257,128]{2,1,0:T(8,128)}, f32[108,256]{1,0:T(8,128)}), (f32[4032,64]{0,1:T(8,128)}, f32[4,257,128]{2,1,0:T(8,128)}, f32[108,256]{1,0:T(8,128)})) %all-reduce.8.cloned.1.call-update) | async-done | bytes 1669136 | tf_op jit(solution)/shard_map/psum | solution.py:347
  (478 shorter events, 125.7 us)
Async XLA Ops:
  7.8 11.9 %copy-start.3 = (bf16[8,16,64,64]{3,2,1,0:T(8,128)(2,1)S(1)}, bf16[8,16,64,64]{3,2,1,0:T(8,128)(2,1)}, u32[]{:S(2)}) copy-start(bf16[8,16,64,64]{3,2,1,0:T(8,128)(2,1)} %param.15) | copy-start | bytes 3145732
  12.2 23.6 %copy-start.47 = (f32[4,257,128]{2,0,1:T(4,128)S(1)}, f32[4,257,128]{2,0,1:T(4,128)}, u32[]{:S(2)}) copy-start(f32[4,257,128]{2,0,1:T(4,128)} %param.24) | copy-start | bytes 1579012
  12.2 23.7 %copy-start.106 = (s32[8]{0:T(128)S(1)}, s32[8]{0:T(128)}, u32[]{:S(2)}) copy-start(s32[8]{0:T(128)} %param.19) | copy-start | bytes 100
  12.2 23.7 %copy-start.107 = (s32[8]{0:T(128)S(1)}, s32[8]{0:T(128)}, u32[]{:S(2)}) copy-start(s32[8]{0:T(128)} %param.18) | copy-start | bytes 100
  12.2 23.7 %copy-start.105 = (s32[8]{0:T(128)S(1)}, s32[8]{0:T(128)}, u32[]{:S(2)}) copy-start(s32[8]{0:T(128)} %param.17) | copy-start | bytes 100
  12.2 23.8 %copy-start.66 = (f32[108,256]{1,0:T(8,128)S(1)}, f32[108,256]{1,0:T(8,128)}, u32[]{:S(2)}) copy-start(f32[108,256]{1,0:T(8,128)} %param.27) | copy-start | bytes 331780
  12.9 63.2 %collective-permute-start.6 = (bf16[8,1,64,64]{3,0,2,1:T(8,128)(2,1)}, bf16[8,1,64,64]{3,0,2,1:T(8,128)(2,1)}, u32[]{:S(2)}, u32[]{:S(2)}) collective-permute-start(bf16[8,1,64,64]{3,0,2,1:T(8,128)(2,1)} %get-tuple-element.179), channel_id=1, source_target_pairs={{0,1},{1,2},{2,3},{4,5},{5,6},{6,7},{8,9},{9,10},{10,11},{12,13},{... | collective-permute-start | bytes 196616 | tf_op jit(solution)/shard_map/ppermute | solution.py:27
  18.5 57.6 %collective-permute-start.7 = (bf16[8,1,64,64]{3,0,2,1:T(8,128)(2,1)S(1)}, bf16[8,1,64,64]{3,0,2,1:T(8,128)(2,1)}, u32[]{:S(2)}, u32[]{:S(2)}) collective-permute-start(bf16[8,1,64,64]{3,0,2,1:T(8,128)(2,1)S(1)} %get-tuple-element.180), channel_id=1, source_target_pairs={{1,0},{2,1},{3,2},{5,4},{6,5},{7,6},{9,8},{10,9},{11,10},{13,12},{... | collective-permute-start | bytes 196616 | tf_op jit(solution)/shard_map/ppermute | solution.py:30
  35.9 74.1 %copy-start.30 = (f32[4,257,128]{2,1,0:T(8,128)}, f32[4,257,128]{2,1,0:T(8,128)S(1)}, u32[]{:S(2)}) copy-start(f32[4,257,128]{2,1,0:T(8,128)S(1)} %copy.566) | copy-start | bytes 1579012
  40.4 4.8 collective-permute-start
  42.3 7.2 %collective-permute-start.1 = (bf16[8,1,64,64]{3,0,2,1:T(8,128)(2,1)}, bf16[8,1,64,64]{3,0,2,1:T(8,128)(2,1)}, u32[]{:S(2)}, u32[]{:S(2)}) collective-permute-start(bf16[8,1,64,64]{3,0,2,1:T(8,128)(2,1)} %get-tuple-element.184), channel_id=1, source_target_pairs={{1,0},{2,1},{3,2},{5,4},{6,5},{7,6},{9,8},{10,9},{11,10},{13,12},{... | collective-permute-start | bytes 196616 | tf_op jit(solution)/shard_map/ppermute | solution.py:30
  44.0 21.8 %copy-start.83 = (f32[8,64]{1,0:T(8,128)}, f32[8,64]{1,0:T(8,128)S(1)}, u32[]{:S(2)}) copy-start(f32[8,64]{1,0:T(8,128)S(1)} %get-tuple-element.202) | copy-start | bytes 6148
  44.0 21.8 %copy-start.92 = (f32[8,64]{1,0:T(8,128)}, f32[8,64]{1,0:T(8,128)S(1)}, u32[]{:S(2)}) copy-start(f32[8,64]{1,0:T(8,128)S(1)} %get-tuple-element.203) | copy-start | bytes 6148
  44.2 31.9 %copy-start.68 = (bf16[3,3,128,64]{2,1,0,3:T(4,128)(2,1)}, bf16[3,3,128,64]{2,1,0,3:T(4,128)(2,1)S(1)}, u32[]{:S(2)}) copy-start(bf16[3,3,128,64]{2,1,0,3:T(4,128)(2,1)S(1)} %convert_element_type.112) | copy-start | bytes 442372
  45.2 11.0 %copy-start.70 = (bf16[576,64]{1,0:T(8,128)(2,1)}, bf16[576,64]{1,0:T(8,128)(2,1)S(1)}, u32[]{:S(2)}) copy-start(bf16[576,64]{1,0:T(8,128)(2,1)S(1)} %copy.567) | copy-start | bytes 221188
  65.9 10.2 %copy-start.44 = (bf16[8,16,64,64]{3,0,2,1:T(8,128)(2,1)S(1)}, bf16[8,16,64,64]{3,0,2,1:T(8,128)(2,1)}, u32[]{:S(2)}) copy-start(bf16[8,16,64,64]{3,0,2,1:T(8,128)(2,1)} %copy-done.43) | copy-start | bytes 3145732
  70.4 22.5 %collective-permute-start.2 = (bf16[8,1,64,64]{3,0,2,1:T(8,128)(2,1)}, bf16[8,1,64,64]{3,0,2,1:T(8,128)(2,1)}, u32[]{:S(2)}, u32[]{:S(2)}) collective-permute-start(bf16[8,1,64,64]{3,0,2,1:T(8,128)(2,1)} %get-tuple-element.181), channel_id=1, source_target_pairs={{0,1},{1,2},{2,3},{4,5},{5,6},{6,7},{8,9},{9,10},{10,11},{12,13},{... | collective-permute-start | bytes 196616 | tf_op jit(solution)/shard_map/ppermute | solution.py:27
  74.8 18.1 %collective-permute-start.3 = (bf16[8,1,64,64]{3,0,2,1:T(8,128)(2,1)}, bf16[8,1,64,64]{3,0,2,1:T(8,128)(2,1)}, u32[]{:S(2)}, u32[]{:S(2)}) collective-permute-start(bf16[8,1,64,64]{3,0,2,1:T(8,128)(2,1)} %get-tuple-element.182), channel_id=1, source_target_pairs={{1,0},{2,1},{3,2},{5,4},{6,5},{7,6},{9,8},{10,9},{11,10},{13,12},{... | collective-permute-start | bytes 196616 | tf_op jit(solution)/shard_map/ppermute | solution.py:30
  89.0 13.9 %all-to-all-start.2 = ((bf16[4,2,16384]{2,1,0:T(2,128)(2,1)}), bf16[4,2,16384]{2,1,0:T(2,128)(2,1)S(1)}, u32[]{:S(2)}, u32[]{:S(2)}) async-start(bf16[4,2,16384]{2,1,0:T(2,128)(2,1)} %reshape.352), calls=%async_computation.2 | async-start | bytes 524288 | tf_op jit(solution)/shard_map/all_to_all | solution.py:275
  102.8 24.1 %all-to-all-start = ((bf16[4,2,65536]{2,1,0:T(2,128)(2,1)}), bf16[4,2,65536]{2,1,0:T(2,128)(2,1)}, u32[]{:S(2)}, u32[]{:S(2)}) async-start(bf16[4,2,65536]{2,1,0:T(2,128)(2,1)} %reshape.348), calls=%async_computation | async-start | bytes 2097152 | tf_op jit(solution)/shard_map/all_to_all | solution.py:246
  109.7 34.4 %copy-start.71 = (bf16[576,64]{1,0:T(8,128)(2,1)}, bf16[576,64]{1,0:T(8,128)(2,1)S(1)}, u32[]{:S(2)}) copy-start(bf16[576,64]{1,0:T(8,128)(2,1)S(1)} %copy.578) | copy-start | bytes 221188
  173.8 76.2 %all-to-all-start.1 = ((bf16[4,2,16384]{2,1,0:T(2,128)(2,1)}), bf16[4,2,16384]{2,1,0:T(2,128)(2,1)}, u32[]{:S(2)}, u32[]{:S(2)}) async-start(bf16[4,2,16384]{2,1,0:T(2,128)(2,1)} %reshape.350), calls=%async_computation.1 | async-start | bytes 524288 | tf_op jit(solution)/shard_map/all_to_all | solution.py:259
  193.8 54.2 %copy-start.100 = (f32[2,64]{1,0:T(2,128)}, f32[2,64]{1,0:T(2,128)S(1)}, u32[]{:S(2)}) copy-start(f32[2,64]{1,0:T(2,128)S(1)} %slice_reduce_fusion) | copy-start | bytes 1540
  250.1 32.4 %all-to-all-start.3 = ((bf16[4,2,65536]{2,1,0:T(2,128)(2,1)}), bf16[4,2,65536]{2,1,0:T(2,128)(2,1)}, u32[]{:S(2)}, u32[]{:S(2)}) async-start(bf16[4,2,65536]{2,1,0:T(2,128)(2,1)} %reshape.354), calls=%async_computation.3 | async-start | bytes 2097152 | tf_op jit(solution)/shard_map/all_to_all | solution.py:302
  255.1 261.6 %all-reduce.8.cloned.1.call-start = ((), (), s32[]{:S(2)}) async-start(), calls=%async_computation.4 | async-start | bytes 3407872 | tf_op jit(solution)/shard_map/psum | solution.py:347
  258.8 12.4 %copy-start.69 = (bf16[3,3,128,64]{2,1,0,3:T(4,128)(2,1)S(1)}, bf16[3,3,128,64]{2,1,0,3:T(4,128)(2,1)}, u32[]{:S(2)}) copy-start(bf16[3,3,128,64]{2,1,0,3:T(4,128)(2,1)} %copy-done.68) | copy-start | bytes 442372
  258.9 12.3 %collective-permute-start.4 = (bf16[8,1,64,128]{3,0,2,1:T(8,128)(2,1)S(1)}, bf16[8,1,64,128]{3,0,2,1:T(8,128)(2,1)S(1)}, u32[]{:S(2)}, u32[]{:S(2)}) collective-permute-start(bf16[8,1,64,128]{3,0,2,1:T(8,128)(2,1)S(1)} %get-tuple-element.171), channel_id=1, source_target_pairs={{0,1},{1,2},{2,3},{4,5},{5,6},{6,7},{8,9},{9,10},{10,11},{12,13},{... | collective-permute-start | bytes 393224 | tf_op jit(solution)/shard_map/ppermute | solution.py:27
  262.9 8.3 %collective-permute-start.5 = (bf16[8,1,64,128]{3,0,2,1:T(8,128)(2,1)S(1)}, bf16[8,1,64,128]{3,0,2,1:T(8,128)(2,1)S(1)}, u32[]{:S(2)}, u32[]{:S(2)}) collective-permute-start(bf16[8,1,64,128]{3,0,2,1:T(8,128)(2,1)S(1)} %get-tuple-element.172), channel_id=1, source_target_pairs={{1,0},{2,1},{3,2},{5,4},{6,5},{7,6},{9,8},{10,9},{11,10},{13,12},{... | collective-permute-start | bytes 393224 | tf_op jit(solution)/shard_map/ppermute | solution.py:30
  289.5 16.2 %copy-start.39 = (bf16[8,16,64,64]{3,0,2,1:T(8,128)(2,1)S(1)}, bf16[8,16,64,64]{3,0,2,1:T(8,128)(2,1)}, u32[]{:S(2)}) copy-start(bf16[8,16,64,64]{3,0,2,1:T(8,128)(2,1)} %copy-done.38) | copy-start | bytes 3145732
  292.3 20.3 %collective-permute-start.8 = (bf16[8,1,64,64]{3,0,2,1:T(8,128)(2,1)}, bf16[8,1,64,64]{3,0,2,1:T(8,128)(2,1)}, u32[]{:S(2)}, u32[]{:S(2)}) collective-permute-start(bf16[8,1,64,64]{3,0,2,1:T(8,128)(2,1)} %get-tuple-element.177), channel_id=1, source_target_pairs={{0,1},{1,2},{2,3},{4,5},{5,6},{6,7},{8,9},{9,10},{10,11},{12,13},{... | collective-permute-start | bytes 196616 | tf_op jit(solution)/shard_map/ppermute | solution.py:27
  304.1 8.5 %copy-start.80 = (f32[8,64]{1,0:T(8,128)S(1)}, f32[8,64]{1,0:T(8,128)}, u32[]{:S(2)}) copy-start(f32[8,64]{1,0:T(8,128)} %copy-done.79) | copy-start | bytes 6148
  304.1 8.5 %copy-start.82 = (f32[8,64]{1,0:T(8,128)S(1)}, f32[8,64]{1,0:T(8,128)}, u32[]{:S(2)}) copy-start(f32[8,64]{1,0:T(8,128)} %copy-done.81) | copy-start | bytes 6148
  304.1 8.5 %copy-start.84 = (f32[8,64]{1,0:T(8,128)S(1)}, f32[8,64]{1,0:T(8,128)}, u32[]{:S(2)}) copy-start(f32[8,64]{1,0:T(8,128)} %copy-done.83) | copy-start | bytes 6148
  304.1 8.6 %copy-start.93 = (f32[8,64]{1,0:T(8,128)S(1)}, f32[8,64]{1,0:T(8,128)}, u32[]{:S(2)}) copy-start(f32[8,64]{1,0:T(8,128)} %copy-done.92) | copy-start | bytes 6148
  304.1 8.5 %collective-permute-start.9 = (bf16[8,1,64,64]{3,0,2,1:T(8,128)(2,1)}, bf16[8,1,64,64]{3,0,2,1:T(8,128)(2,1)}, u32[]{:S(2)}, u32[]{:S(2)}) collective-permute-start(bf16[8,1,64,64]{3,0,2,1:T(8,128)(2,1)} %get-tuple-element.178), channel_id=1, source_target_pairs={{1,0},{2,1},{3,2},{5,4},{6,5},{7,6},{9,8},{10,9},{11,10},{13,12},{... | collective-permute-start | bytes 196616 | tf_op jit(solution)/shard_map/ppermute | solution.py:30
  335.8 9.1 %copy-start.42 = (bf16[8,16,64,64]{3,0,2,1:T(8,128)(2,1)S(1)}, bf16[8,16,64,64]{3,0,2,1:T(8,128)(2,1)}, u32[]{:S(2)}) copy-start(bf16[8,16,64,64]{3,0,2,1:T(8,128)(2,1)} %copy-done.41) | copy-start | bytes 3145732
  340.6 11.2 %copy-start.40 = (bf16[8,16,64,64]{3,0,2,1:T(8,128)(2,1)}, bf16[8,16,64,64]{3,0,2,1:T(8,128)(2,1)S(1)}, u32[]{:S(2)}) copy-start(bf16[8,16,64,64]{3,0,2,1:T(8,128)(2,1)S(1)} %multiply_convert_fusion) | copy-start | bytes 3145732
  341.4 16.3 %collective-permute-start.10 = (bf16[8,1,64,64]{3,0,2,1:T(8,128)(2,1)}, bf16[8,1,64,64]{3,0,2,1:T(8,128)(2,1)}, u32[]{:S(2)}, u32[]{:S(2)}) collective-permute-start(bf16[8,1,64,64]{3,0,2,1:T(8,128)(2,1)} %get-tuple-element.175), channel_id=1, source_target_pairs={{0,1},{1,2},{2,3},{4,5},{5,6},{6,7},{8,9},{9,10},{10,11},{12,13},{... | collective-permute-start | bytes 196616 | tf_op jit(solution)/shard_map/ppermute | solution.py:27
  343.3 8.5 %copy-start.94 = (f32[8,64]{1,0:T(8,128)S(1)}, f32[8,64]{1,0:T(8,128)}, u32[]{:S(2)}) copy-start(f32[8,64]{1,0:T(8,128)} %get-tuple-element.133) | copy-start | bytes 6148
  343.3 11.2 %copy-start.56 = (f32[576,64]{0,1:T(8,128)S(1)}, f32[576,64]{0,1:T(8,128)}, u32[]{:S(2)}) copy-start(f32[576,64]{0,1:T(8,128)} %copy.647) | copy-start | bytes 442372
  343.3 11.2 %copy-start.57 = (f32[576,64]{0,1:T(8,128)S(1)}, f32[576,64]{0,1:T(8,128)}, u32[]{:S(2)}) copy-start(f32[576,64]{0,1:T(8,128)} %copy.646) | copy-start | bytes 442372
  343.3 14.4 %collective-permute-start.11 = (bf16[8,1,64,64]{3,0,2,1:T(8,128)(2,1)}, bf16[8,1,64,64]{3,0,2,1:T(8,128)(2,1)}, u32[]{:S(2)}, u32[]{:S(2)}) collective-permute-start(bf16[8,1,64,64]{3,0,2,1:T(8,128)(2,1)} %get-tuple-element.176), channel_id=1, source_target_pairs={{1,0},{2,1},{3,2},{5,4},{6,5},{7,6},{9,8},{10,9},{11,10},{13,12},{... | collective-permute-start | bytes 196616 | tf_op jit(solution)/shard_map/ppermute | solution.py:30
  357.7 25.5 %copy-start.65 = (f32[108,256]{1,0:T(8,128)S(1)}, f32[108,256]{1,0:T(8,128)}, u32[]{:S(2)}) copy-start(f32[108,256]{1,0:T(8,128)} %fusion.132) | copy-start | bytes 331780
  357.7 25.5 %copy-start.91 = (f32[8,257]{1,0:T(8,128)S(1)}, f32[8,257]{1,0:T(8,128)}, u32[]{:S(2)}) copy-start(f32[8,257]{1,0:T(8,128)} %fusion.116) | copy-start | bytes 24676
  357.7 25.5 %copy-start.98 = (pred[8,108]{1,0:T(8,128)(4,1)S(1)}, pred[8,108]{1,0:T(8,128)(4,1)}, u32[]{:S(2)}) copy-start(pred[8,108]{1,0:T(8,128)(4,1)} %copy-done.96) | copy-start | bytes 2596
  391.8 124.8 %copy-start.48 = (f32[4,257,128]{2,0,1:T(4,128)S(1)}, f32[4,257,128]{2,0,1:T(4,128)}, u32[]{:S(2)}) copy-start(f32[4,257,128]{2,0,1:T(4,128)} %param.24) | copy-start | bytes 1579012
  391.8 124.8 %copy-start.63 = (f32[4,257,128]{2,0,1:T(4,128)S(1)}, f32[4,257,128]{2,0,1:T(4,128)}, u32[]{:S(2)}) copy-start(f32[4,257,128]{2,0,1:T(4,128)} %param.26) | copy-start | bytes 1579012
  391.9 124.8 %copy-start.64 = (f32[4,257,128]{2,0,1:T(4,128)S(1)}, f32[4,257,128]{2,0,1:T(4,128)}, u32[]{:S(2)}) copy-start(f32[4,257,128]{2,0,1:T(4,128)} %param.25) | copy-start | bytes 1579012
  (78 other events, 237.1 us)
Sparse Core Ops, SparseCore 0:
  385.1 131.5 all-reduce.7
where the time goes:
time: 542 us; the launch traced here: 532 us
  waiting for transfers between devices  145 us (27%)
  local copies, waits for them, and re-layouts  112 us (21%)
  matrix products  98.7 us (18%)
  other arithmetic  59 us (11%)
  starting transfers between devices  56.4 us (10%)
  blocking collectives  44.4 us (8%)
  between operations  16.8 us (3%)
    psum x1, waiting for transfers between devices, local(): lax.psum((grad_conv, grad_map, grad_table), ('dp', 'space'))  122 us
    unnamed x243, local copies, waits for them, and re-layouts  51.2 us
    conv_general_dilated x6, matrix products, conv_rows(): lax.conv_general_dilated(padded, kernel, (1, 1), ((0, 0), (1, 1)), dimens...  45.5 us
    ppermute x6, starting transfers between devices, with_halo(): lax.ppermute(lax.slice_in_dim(block, block.shape[dim] - width, None, axis...  29.5 us
    conv_general_dilated x6, matrix products, kernel_grad(): lax.conv_general_dilated(source, grad_value, (1, 1), padding, rhs_dilatio...  25.9 us
    psum x2, blocking collectives, backward_element_count(): return lax.psum(pair, 'space')  22.6 us
    psum x2, blocking collectives, forward_element_count(): return lax.psum(pair, 'space')  21.8 us
    conv_general_dilated x4, matrix products, conv_whole(): lax.conv_general_dilated(input_value, kernel, (1, 1), ((1, 1), (1, 1)), d...  15.7 us
  transfers between devices with their start and end apart: 17, of which 4 were waited for; matrix products, arithmetic and copies ran while one was open for 29% of the time, Pallas kernels for 0%

commit v1 on v0

v1 whole, which is shorter than its diff:
```python
import functools

import jax
import jax.numpy as jnp
from jax import lax
from jax.experimental import pallas as pl
from jax.experimental.pallas import tpu as pltpu
from jax.sharding import PartitionSpec as P

ACTIONS = 18
NOISE_LEVELS = 64
ADAM_STEP = 4
NORM_EPSILON = 1e-05
ADAM_EPS = 1e-08
BETA_ONE = 0.5
BETA_TWO = 0.5
DECAY = 0.01
HIGH = lax.Precision.HIGHEST
F32 = jnp.float32
BF16 = jnp.bfloat16
MESH = pl.DeviceIdType.MESH
VM = pltpu.VMEM

ALPHA, BETA, RSTD, NMR, GAIN, SHIFT, COEF, BIAS = range(8)


def dot_nn(a, b):
    return lax.dot_general(a, b, (((1,), (0,)), ((), ())), preferred_element_type=F32)


def dot_nt(a, b):
    return lax.dot_general(a, b, (((1,), (1,)), ((), ())), preferred_element_type=F32)


def dot_tn(a, b):
    return lax.dot_general(a, b, (((0,), (0,)), ((), ())), preferred_element_type=F32)


def dot_high(a, b):
    return lax.dot_general(
        a, b, (((1,), (0,)), ((), ())), precision=HIGH, preferred_element_type=F32
    )


def logistic(z):
    return 0.5 * jnp.tanh(0.5 * z) + 0.5


def lane_iota(shape):
    return lax.broadcasted_iota(jnp.int32, shape, len(shape) - 1)


def swap(v):
    return pltpu.roll(v, 64, len(v.shape) - 1)


def join(lo, hi):
    return jnp.where(lane_iota(lo.shape) < 64, lo, hi)


def twice(row):
    return jnp.concatenate([row, row], axis=-1)


def step_kernel(
    n,
    x_hbm,
    cot_hbm,
    act_ref,
    noise_ref,
    game_ref,
    live_ref,
    cw_ref,
    nm_ref,
    tab_ref,
    res_hbm,
    fg_hbm,
    gt_ref,
    pack_ref,
    raw,
    xh,
    tmp,
    fst,
    xs,
    e1,
    e2,
    esk,
    eg,
    eg2,
    c1,
    gsa,
    gz,
    dv,
    c3,
    gh4,
    gz4,
    gz3,
    gco,
    ec3,
    ec4,
    ecg,
    ecg3,
    ecy,
    ed,
    w1f,
    w1b,
    w2f,
    w2b,
    wsf,
    wsb,
    wup,
    wco,
    wdf,
    wdb,
    w3f,
    w3b,
    w4f,
    w4b,
    acc,
    prm,
    tabp,
    stat,
    hal,
    hout,
    hfull,
    hfout,
    local_sem,
    out_sem,
    fg_sem,
    stat_send,
    stat_recv,
    halo_send,
    halo_recv,
):
    frames, strip = raw.shape[0], raw.shape[1]
    breadth = raw.shape[2]
    half = frames // 2
    rows = strip // 2
    cols = breadth // 2
    me = lax.axis_index("space")
    full_cells = float(strip * n * breadth * 32)
    coarse_cells = full_cells / 4.0
    owned = rows * cols
    ext = (rows + 2) * cols

    barrier = pltpu.get_barrier_semaphore()
    for off in range(1, n):
        pl.semaphore_signal(
            barrier,
            inc=1,
            device_id={"space": lax.rem(me + off, n)},
            device_id_type=MESH,
        )

    x_copy = pltpu.make_async_copy(x_hbm, raw, local_sem.at[0])
    x_copy.start()
    pl.semaphore_wait(barrier, n - 1)

    def halo_copies(k, first, last, to_up, to_down):
        up = pltpu.make_async_remote_copy(
            src_ref=first,
            dst_ref=to_up,
            send_sem=halo_send.at[k, 0],
            recv_sem=halo_recv.at[k, 0],
            device_id={"space": lax.rem(me + n - 1, n)},
            device_id_type=MESH,
        )
        down = pltpu.make_async_remote_copy(
            src_ref=last,
            dst_ref=to_down,
            send_sem=halo_send.at[k, 1],
            recv_sem=halo_recv.at[k, 1],
            device_id={"space": lax.rem(me + 1, n)},
            device_id_type=MESH,
        )
        return up, down

    def halo_start(copies):
        @pl.when(me > 0)
        def _():
            copies[0].start()

        @pl.when(me < n - 1)
        def _():
            copies[1].start()

    def halo_wait(copies):
        @pl.when(me < n - 1)
        def _():
            copies[0].wait_recv()

        @pl.when(me > 0)
        def _():
            copies[1].wait_recv()

    def halo_finish(copies):
        @pl.when(me > 0)
        def _():
            copies[0].wait_send()

        @pl.when(me < n - 1)
        def _():
            copies[1].wait_send()

    def stat_copy(k, off, slot):
        return pltpu.make_async_remote_copy(
            src_ref=stat.at[k, slot],
            dst_ref=stat.at[k, slot],
            send_sem=stat_send.at[k, off - 1],
            recv_sem=stat_recv.at[k, off - 1],
            device_id={"space": lax.rem(me + off, n)},
            device_id_type=MESH,
        )

    def stat_start(k, value):
        stat[k, me] = value
        for off in range(1, n):
            stat_copy(k, off, me).start()

    def stat_total(k):
        for off in range(1, n):
            stat_copy(k, off, lax.rem(me + n - off, n)).wait_recv()
        total = stat[k, 0]
        for i in range(1, n):
            total = total + stat[k, i]
        for off in range(1, n):
            stat_copy(k, off, me).wait_send()
        return total

    x_halo = halo_copies(
        0, x_hbm.at[:, pl.ds(0, 3)], x_hbm.at[:, pl.ds(strip - 3, 3)], xh.at[0, 1], xh.at[0, 0]
    )
    g_halo = halo_copies(
        1, cot_hbm.at[:, pl.ds(0, 3)], cot_hbm.at[:, pl.ds(strip - 3, 3)], xh.at[1, 1], xh.at[1, 0]
    )
    for side in range(2):

        @pl.when((me == 0) if side == 0 else (me == n - 1))
        def _():
            for which in range(2):
                xh[which, side] = jnp.zeros(xh.shape[2:], BF16)
            for which in range(hal.shape[0]):
                hal[which, side] = jnp.zeros(hal.shape[2:], BF16)
            hfull[side] = jnp.zeros(hfull.shape[1:], BF16)

    halo_start(x_halo)

    def coarse_halo(k):
        return halo_copies(
            k, hout.at[k - 2, 0], hout.at[k - 2, 1], hal.at[k - 2, 1], hal.at[k - 2, 0]
        )

    g_h4_halo, d_halo, c3_halo, y_halo, g_h3_halo = [coarse_halo(k) for k in range(2, 7)]
    g_h2_halo = halo_copies(7, hfout.at[0], hfout.at[1], hfull.at[1], hfull.at[0])

    def block_mask(shape, pad):
        blocks = shape[0]
        b = lax.broadcasted_iota(jnp.int32, shape, 0)
        low = jnp.where(me > 0, 0, pad)
        high = jnp.where(me < n - 1, blocks, blocks - pad)
        return (b >= low) & (b < high)

    def param(k, which, f):
        return prm[k * 8 + which, pl.ds(f, 1), :]

    def wide(k, which, f):
        return twice(param(k, which, f))

    def put_row(carry, f, value):
        row = lax.broadcasted_iota(jnp.int32, carry.shape, 0)
        return jnp.where(row == f, value, carry)

    def full_sum(v):
        s = jnp.sum(v.reshape(-1, 256), axis=0, keepdims=True)
        return s[:, :128] + s[:, 128:]

    def paired(raw_rows):
        count = raw_rows.shape[0]
        tmp[0:count, :, 0:64] = raw_rows.astype(F32)
        even = tmp[0:count, pl.ds(0, cols, stride=2), :]
        odd = tmp[0:count, pl.ds(1, cols, stride=2), :]
        return join(even, swap(odd))

    def pair_halves(p):
        count = p.shape[0] // 2
        p = p.reshape(count, 2, cols, 128)
        return p[:, 0], p[:, 1]

    def neighbours(v):
        count = v.shape[0]
        flat = v.reshape(count * cols, 128)
        up = pltpu.roll(flat, count * cols - 1, 0).reshape(v.shape)
        down = pltpu.roll(flat, 1, 0).reshape(v.shape)
        return up, down

    def put_e(e, f, start, h):
        count = h.shape[0]
        for part in range(2):
            v = h[:, :, part * 128 : (part + 1) * 128]
            up, down = neighbours(v)
            lane = lane_iota(v.shape)
            q = lax.broadcasted_iota(jnp.int32, v.shape, 1)
            near = jnp.where(
                lane < 64, jnp.where(q == cols - 1, 0.0, up), jnp.where(q == 0, 0.0, down)
            )
            e[f, start : start + count, :, part * 256 : part * 256 + 128] = v.astype(BF16)
            e[f, start : start + count, :, part * 256 + 128 : part * 256 + 256] = near.astype(BF16)

    def window(e, f, start, count):
        return jnp.concatenate(
            [
                e[f, start - 1 : start - 1 + count, :, 256:512],
                e[f, start : start + count, :, :],
                e[f, start + 1 : start + 1 + count, :, 0:256],
            ],
            axis=-1,
        ).reshape(count * cols, 1024)

    def own_pixels(e, f, start, count):
        return jnp.concatenate(
            [
                e[f, start : start + count, :, 0:128],
                e[f, start : start + count, :, 256:384],
            ],
            axis=-1,
        ).reshape(count * cols, 256)

    def put_ec(ec, hf, v):
        up, down = neighbours(v)
        q = lax.broadcasted_iota(jnp.int32, v.shape, 1)
        ec[hf, :, :, 0:128] = jnp.where(q == 0, 0.0, down).astype(BF16)
        ec[hf, :, :, 128:256] = v.astype(BF16)
        ec[hf, :, :, 256:384] = jnp.where(q == cols - 1, 0.0, up).astype(BF16)

    def coarse_window(ec, hf):
        return jnp.concatenate([ec[hf, a : a + rows] for a in range(3)], axis=-1).reshape(
            owned, 1152
        )

    def coarse_sum(v):
        return jnp.sum(v.reshape(-1, 128), axis=0, keepdims=True)

    def with_halo(ref, hf, k):
        ref[hf, 0] = hal[k, 0, hf].astype(F32)
        ref[hf, rows + 1] = hal[k, 1, hf].astype(F32)

    def border(ref_out, k, hf, v):
        ref_out[k, 0, hf] = v[0].astype(BF16)
        ref_out[k, 1, hf] = v[rows - 1].astype(BF16)

    def group_matrix(coarse):
        r = lax.broadcasted_iota(jnp.int32, (128, 128), 0) // 32
        c = lax.broadcasted_iota(jnp.int32, (128, 128), 1) // 32
        same = (r == c) if coarse else (r % 2 == c % 2)
        return jnp.where(same, 1.0, 0.0)

    def norm_forward(k, total, coarse):
        cells = coarse_cells if coarse else full_cells
        count = half if coarse else frames
        moments = dot_high(total, group_matrix(coarse)) / cells
        mean = moments[0:count]
        var = moments[count : 2 * count] - mean * mean
        rstd = lax.rsqrt(var + NORM_EPSILON)
        gain = prm[k * 8 + GAIN, 0:count, :]
        alpha = rstd * gain
        prm[k * 8 + ALPHA, 0:count, :] = alpha
        prm[k * 8 + BETA, 0:count, :] = prm[k * 8 + SHIFT, 0:count, :] - mean * alpha
        prm[k * 8 + RSTD, 0:count, :] = rstd
        prm[k * 8 + NMR, 0:count, :] = -mean * rstd

    def norm_backward(k, total, coarse):
        cells = coarse_cells if coarse else full_cells
        count = half if coarse else frames
        gain = prm[k * 8 + GAIN, 0:count, :]
        shift_grad = total[0:count]
        scale_grad = total[count : 2 * count]
        means = (
            dot_high(
                jnp.concatenate([shift_grad * gain, scale_grad * gain], axis=0),
                group_matrix(coarse),
            )
            / cells
        )
        rstd = prm[k * 8 + RSTD, 0:count, :]
        factor = -rstd * means[count : 2 * count]
        prm[k * 8 + COEF, 0:count, :] = rstd * factor
        prm[k * 8 + BIAS, 0:count, :] = (
            prm[k * 8 + NMR, 0:count, :] * factor - rstd * means[0:count]
        )
        if coarse:
            scale_all = jnp.concatenate([scale_grad, swap(scale_grad)], axis=0)
            shift_all = jnp.concatenate([shift_grad, swap(shift_grad)], axis=0)
        else:
            scale_all = scale_grad + swap(scale_grad)
            shift_all = shift_grad + swap(shift_grad)
        pack_ref[:, k * 128 : (k + 1) * 128] = join(scale_all, swap(shift_all))

    x_copy.wait()

    def load_x(f, carry):
        total, square = carry
        even, odd = pair_halves(paired(raw[f]))
        both = jnp.concatenate([even, odd], axis=-1)
        xs[f, 2 : 2 + rows] = both.astype(BF16)
        return put_row(total, f, full_sum(both)), put_row(square, f, full_sum(both * both))

    zero_rows = jnp.zeros((frames, 128), F32)
    sums = lax.fori_loop(0, frames, load_x, (zero_rows, zero_rows))
    stat_start(0, jnp.concatenate(sums, axis=0))
    g_copy = pltpu.make_async_copy(cot_hbm, raw, local_sem.at[1])
    g_copy.start()
    halo_start(g_halo)

    def conditioning():
        entry = lax.broadcasted_iota(jnp.int32, (frames, 128), 1)
        row = lax.broadcasted_iota(jnp.int32, (frames, 128), 0)
        hot = jnp.zeros((frames, 128), F32)
        for f in range(frames):
            hit = (
                (entry == act_ref[f])
                | (entry == noise_ref[f] + ACTIONS)
                | (entry == game_ref[f] + ACTIONS + NOISE_LEVELS)
            )
            hot = jnp.where((row == f) & hit, 1.0, hot)
        table_rows = tab_ref.shape[0]
        tabp[...] = jnp.zeros(tabp.shape, F32)
        tabp[0:table_rows, :] = tab_ref[...]
        embedded = dot_high(hot, tabp[...])
        pack_ref[:, 512:768] = embedded
        pack_ref[:, 768:896] = hot
        for k in range(4):
            mod = dot_high(embedded, nm_ref[pl.ds(k, 256, stride=4), :]) + nm_ref[
                1024 + k : 1025 + k, :
            ]
            scale = join(mod, swap(mod)) + 1.0
            shift = join(swap(mod), mod)
            if k < 2:
                prm[k * 8 + GAIN] = scale
                prm[k * 8 + SHIFT] = shift
            else:
                prm[k * 8 + GAIN, 0:half, :] = join(scale[0:half], scale[half:])
                prm[k * 8 + SHIFT, 0:half, :] = join(shift[0:half], shift[half:])

    conditioning()

    def tap(index):
        first = (index // 2) * 128
        last = min(first + 128, cw_ref.shape[1])
        tile = cw_ref[:, first:last].astype(BF16).astype(F32)
        if last - first < 128:
            tile = jnp.concatenate([tile, jnp.zeros((64, 128 - last + first), F32)], axis=-1)
        return tile, index % 2

    def low_half(index):
        tile, odd = tap(index)
        return swap(tile) if odd else tile

    def high_half(index):
        tile, odd = tap(index)
        return tile if odd else swap(tile)

    def lane_pair(low_index, high_index):
        zero = jnp.zeros((64, 128), F32)
        low = zero if low_index is None else low_half(low_index)
        high = zero if high_index is None else high_half(high_index)
        return join(low, high).astype(BF16)

    def fine_weights(index, forward_w, backward_w):
        zero = jnp.zeros((64, 128), BF16)
        pairs = []
        for t in range(3):
            p12 = lane_pair(index(t, 1), index(t, 2))
            p01 = lane_pair(index(t, 0), index(t, 1))
            pz0 = lane_pair(None, index(t, 0))
            p2z = lane_pair(index(t, 2), None)
            pairs.append((p12, p01, pz0, p2z))
        for a in range(4):
            for dr in range(2):
                t = a - dr
                ok = 0 <= t <= 2
                for dq in range(2):
                    r = (dr * 2 + dq) * 64
                    first = pairs[t][0 if dq == 0 else 1] if ok else zero
                    second = pairs[t][2 if dq == 0 else 3] if ok else zero
                    forward_w[r : r + 64, a * 256 : a * 256 + 128] = first
                    forward_w[r : r + 64, a * 256 + 128 : a * 256 + 256] = second
                t = 2 - a + dr
                ok = 0 <= t <= 2
                for g in range(4):
                    r = a * 256 + g * 64
                    backward_w[r : r + 64, dr * 128 : dr * 128 + 128] = (
                        pairs[t][g] if ok else zero
                    )

    def coarse_weights(index, forward_w, backward_w):
        for a in range(3):
            for j in range(3):
                lane = (a * 3 + j) * 128
                low = lane_pair(index(a, j), None)
                high = lane_pair(None, index(a, j))
                forward_w[0:64, lane : lane + 128] = low
                forward_w[64:128, lane : lane + 128] = high
                lane = ((2 - a) * 3 + (2 - j)) * 128
                backward_w[lane : lane + 64, :] = low
                backward_w[lane + 64 : lane + 128, :] = high

    def down_weights(index):
        zero = jnp.zeros((64, 128), BF16)
        wdf[...] = jnp.zeros(wdf.shape, BF16)
        wdb[...] = jnp.zeros(wdb.shape, BF16)
        for t in range(3):
            p12 = lane_pair(index(t, 1), index(t, 2))
            pz0 = lane_pair(None, index(t, 0))
            for hi in range(2):
                lane = hi * 768 + t * 256
                wdf[hi * 64 : hi * 64 + 64, lane : lane + 128] = p12
                wdf[hi * 64 : hi * 64 + 64, lane + 128 : lane + 256] = pz0
                i, dr = ((1, 1), (0, 0), (0, 1))[t]
                lane = hi * 256 + dr * 128
                for j in range(2):
                    r = (i * 2 + j) * 128 + hi * 64
                    wdb[r : r + 64, lane : lane + 128] = p12 if j == 0 else pz0

    def up_weights():
        def up_tap(ta, tb):
            return low_half(45 + (ta * 3 + tb) * 2 + 1)

        taps = [[up_tap(ta, tb) for tb in range(3)] for ta in range(3)]
        members = {(0, 0): (0,), (0, 1): (1, 2), (1, 1): (0, 1), (1, 2): (2,)}
        wup[...] = jnp.zeros(wup.shape, BF16)
        for (dr, i), in_rows in members.items():
            for (dq, j), in_cols in members.items():
                total = sum(taps[ta][tb] for ta in in_rows for tb in in_cols)
                zero = jnp.zeros_like(total)
                r = (dr * 2 + dq) * 64
                lane = (i * 3 + j) * 128
                wup[r : r + 64, lane : lane + 128] = join(total, zero).astype(BF16)
                wup[256 + r : 256 + r + 64, lane : lane + 128] = join(zero, swap(total)).astype(
                    BF16
                )
        for a in range(4):
            for g, off in enumerate((0, 1, 2, -1)):
                chosen = [
                    taps[2 - a + dr][1 - off + dq]
                    for dr in range(2)
                    for dq in range(2)
                    if 0 <= 2 - a + dr <= 2 and 0 <= 1 - off + dq <= 2
                ]
                total = sum(chosen[1:], chosen[0])
                zero = jnp.zeros_like(total)
                r = a * 256 + g * 64
                wco[0, r : r + 64, :] = join(total, zero).astype(BF16)
                wco[1, r : r + 64, :] = join(zero, swap(total)).astype(BF16)

    def stacked(k):
        return lambda t, s: k * 9 + t * 3 + s

    fine_weights(stacked(0), w1f, w1b)
    fine_weights(stacked(1), w2f, w2b)
    fine_weights(lambda t, s: 45 + (t * 3 + s) * 2, wsf, wsb)
    up_weights()
    down_weights(stacked(2))
    coarse_weights(stacked(3), w3f, w3b)
    coarse_weights(stacked(4), w4f, w4b)

    halo_wait(x_halo)

    def load_x_halo(f, carry):
        zero = jnp.zeros((1, cols, 128), F32)
        top = paired(xh[0, 0, f])
        low = paired(xh[0, 1, f])
        xs[f, 0] = jnp.concatenate([zero, top[0:1]], axis=-1)[0].astype(BF16)
        xs[f, 1] = jnp.concatenate([top[1:2], top[2:3]], axis=-1)[0].astype(BF16)
        xs[f, rows + 2] = jnp.concatenate([low[0:1], low[1:2]], axis=-1)[0].astype(BF16)
        xs[f, rows + 3] = jnp.concatenate([low[2:3], zero], axis=-1)[0].astype(BF16)
        return carry

    lax.fori_loop(0, frames, load_x_halo, 0)
    norm_forward(0, stat_total(0), False)

    def first_layer(f, carry):
        total, square = carry
        x = xs[f].astype(F32)
        z = x * wide(0, ALPHA, f) + wide(0, BETA, f)
        h = z * logistic(z)
        h = jnp.where(block_mask(h.shape, 2), h, 0.0)
        put_e(e1, f, 0, h)
        out = dot_nt(window(e1, f, 1, rows + 2), w1f[...]).reshape(rows + 2, cols, 256)
        c1[f] = out
        own = out[1 : rows + 1]
        return put_row(total, f, full_sum(own)), put_row(square, f, full_sum(own * own))

    sums = lax.fori_loop(0, frames, first_layer, (zero_rows, zero_rows))
    stat_start(1, jnp.concatenate(sums, axis=0))

    g_copy.wait()
    halo_wait(g_halo)

    def load_g(f, carry):
        live = jnp.where(f < live_ref[0], 1.0, 0.0)
        even, odd = pair_halves(paired(raw[f]))
        own = jnp.concatenate([even, odd], axis=-1)
        zero = jnp.zeros((1, cols, 128), F32)
        top = paired(xh[1, 0, f])
        low = paired(xh[1, 1, f])
        g = jnp.concatenate(
            [
                jnp.concatenate([zero, top[0:1]], axis=-1),
                jnp.concatenate([top[1:2], top[2:3]], axis=-1),
                own,
                jnp.concatenate([low[0:1], low[1:2]], axis=-1),
                jnp.concatenate([low[2:3], zero], axis=-1),
            ],
            axis=0,
        )
        g = jnp.where(block_mask(g.shape, 2), g * live, 0.0)
        put_e(eg, f, 0, g)
        gsa[f] = dot_nn(window(eg, f, 1, rows + 2), wsb[...]).reshape(rows + 2, cols, 256)
        return carry

    lax.fori_loop(0, frames, load_g, 0)

    def coarse_gradient(hf, carry):
        g = dot_nn(window(eg, hf, 1, rows + 2), wco[0]) + dot_nn(
            window(eg, hf + half, 1, rows + 2), wco[1]
        )
        g = g.reshape(rows + 2, cols, 128)
        g = jnp.where(block_mask(g.shape, 1), g, 0.0).astype(BF16).astype(F32)
        gco[hf] = g
        put_ec(ecg, hf, g)
        back = dot_nn(coarse_window(ecg, hf), w4b[...]).reshape(rows, cols, 128)
        gh4[hf, 1 : rows + 1] = back
        border(hout, 0, hf, back)
        return carry

    lax.fori_loop(0, half, coarse_gradient, 0)
    halo_start(g_h4_halo)

    norm_forward(1, stat_total(1), False)

    def second_layer(f, carry):
        z = c1[f] * wide(1, ALPHA, f) + wide(1, BETA, f)
        h = z * logistic(z)
        h = jnp.where(block_mask(h.shape, 1), h, 0.0)
        edge = jnp.zeros((cols, 512), BF16)
        e2[f, 0] = edge
        e2[f, rows + 3] = edge
        put_e(e2, f, 1, h)
        out = dot_nt(window(e2, f, 1, rows + 2), w2f[...]).reshape(rows + 2, cols, 256)
        skip = out + xs[f, 1 : rows + 3].astype(F32)
        skip = jnp.where(block_mask(skip.shape, 1), skip, 0.0)
        put_e(esk, f, 1, skip)
        return carry

    lax.fori_loop(0, frames, second_layer, 0)

    def down_window(f):
        return jnp.concatenate(
            [esk[f, 1 : 1 + rows, :, 256:512], esk[f, 2 : 2 + rows]], axis=-1
        ).reshape(owned, 768)

    zero_coarse = jnp.zeros((half, 128), F32)
    pad_rows = [jnp.zeros((2 * frames - 2 * half, 128), F32)]

    def down_layer(hf, carry):
        total, square = carry
        d = dot_nt(down_window(hf), wdf[:, 0:768]) + dot_nt(
            down_window(hf + half), wdf[:, 768:1536]
        )
        d = d.reshape(rows, cols, 128)
        dv[hf, 1 : rows + 1] = d
        border(hout, 1, hf, d)
        return put_row(total, hf, coarse_sum(d)), put_row(square, hf, coarse_sum(d * d))

    sums = lax.fori_loop(0, half, down_layer, (zero_coarse, zero_coarse))
    stat_start(2, jnp.concatenate(list(sums) + pad_rows, axis=0))
    halo_start(d_halo)

    def put_half(index, value):
        tile = index // 2
        current = gt_ref[tile].astype(F32)
        value = join(current, swap(value)) if index % 2 else join(value, current)
        gt_ref[tile] = value.astype(BF16)

    gt_ref[...] = jnp.zeros(gt_ref.shape, BF16)

    def fine_kernel_grad(index, e, start, gradient, gradient_start):
        acc[0, :, 0:1024] = jnp.zeros((256, 1024), F32)

        def add(f, carry):
            g = own_pixels(gradient, f, gradient_start, rows)
            acc[0, :, 0:1024] += dot_tn(g, window(e, f, start, rows))
            return carry

        lax.fori_loop(0, frames, add, 0)
        for t in range(3):
            u = []
            for dq in range(2):
                parts = [
                    acc[0, (dr * 2 + dq) * 64 : (dr * 2 + dq) * 64 + 64, pl.ds((t + dr) * 256, 256)]
                    for dr in range(2)
                ]
                u.append(parts[0] + parts[1])
            near, far = [v[:, 0:128] for v in u], [v[:, 128:256] for v in u]
            put_half(index(t, 0), swap(far[0]) + near[1])
            put_half(index(t, 1), near[0] + swap(near[1]))
            put_half(index(t, 2), swap(near[0]) + far[1])

    def coarse_kernel_grad(index, ec, gradient):
        acc[0, 0:128, :] = jnp.zeros((128, 1152), F32)

        def add(hf, carry):
            g = gradient[hf, 1 : rows + 1, :, 128:256].reshape(owned, 128)
            acc[0, 0:128, :] += dot_tn(g, coarse_window(ec, hf))
            return carry

        lax.fori_loop(0, half, add, 0)
        for a in range(3):
            for j in range(3):
                lanes = pl.ds((a * 3 + j) * 128, 128)
                put_half(index(a, j), acc[0, 0:64, lanes] + swap(acc[0, 64:128, lanes]))

    def down_kernel_grad(index):
        acc[:, 0:128, 0:768] = jnp.zeros((2, 128, 768), F32)

        def add(hf, carry):
            g = ed[hf, 1 : rows + 1, :, 0:128].reshape(owned, 128)
            acc[0, 0:128, 0:768] += dot_tn(g, down_window(hf))
            acc[1, 0:128, 0:768] += dot_tn(g, down_window(hf + half))
            return carry

        lax.fori_loop(0, half, add, 0)
        for a in range(3):
            near = acc[0, 0:64, pl.ds(a * 256, 128)] + acc[1, 64:128, pl.ds(a * 256, 128)]
            far = (
                acc[0, 0:64, pl.ds(a * 256 + 128, 128)] + acc[1, 64:128, pl.ds(a * 256 + 128, 128)]
            )
            put_half(index(a, 0), swap(far))
            put_half(index(a, 1), near)
            put_half(index(a, 2), swap(near))

    def up_kernel_grad():
        acc[...] = jnp.zeros(acc.shape, F32)

        def add(hf, carry):
            v = coarse_window(ecy, hf)
            acc[0] += dot_tn(own_pixels(eg, hf, 2, rows), v)
            acc[1] += dot_tn(own_pixels(eg, hf + half, 2, rows), v)
            return carry

        lax.fori_loop(0, half, add, 0)

        def block(dr, dq, i, j):
            r = (dr * 2 + dq) * 64
            lanes = pl.ds((i * 3 + j) * 128, 128)
            return acc[0, r : r + 64, lanes] + swap(acc[1, r : r + 64, lanes])

        place = {(0, 0): 0, (0, 1): 1, (0, 2): 1, (1, 0): 1, (1, 1): 1, (1, 2): 2}
        for ta in range(3):
            for tb in range(3):
                total = sum(
                    block(dr, dq, place[dr, ta], place[dq, tb])
                    for dr in range(2)
                    for dq in range(2)
                )
                put_half(45 + (ta * 3 + tb) * 2 + 1, total)

    fine_kernel_grad(lambda t, s: 45 + (t * 3 + s) * 2, esk, 2, eg, 2)

    halo_wait(d_halo)
    norm_forward(2, stat_total(2), True)

    def third_layer(hf, carry):
        total, square = carry
        with_halo(dv, hf, 1)
        z = dv[hf] * param(2, ALPHA, hf) + param(2, BETA, hf)
        h = z * logistic(z)
        put_ec(ec3, hf, jnp.where(block_mask(h.shape, 1), h, 0.0))
        out = dot_nt(coarse_window(ec3, hf), w3f[...]).reshape(rows, cols, 128)
        c3[hf, 1 : rows + 1] = out
        border(hout, 2, hf, out)
        return put_row(total, hf, coarse_sum(out)), put_row(square, hf, coarse_sum(out * out))

    sums = lax.fori_loop(0, half, third_layer, (zero_coarse, zero_coarse))
    stat_start(3, jnp.concatenate(list(sums) + pad_rows, axis=0))
    halo_start(c3_halo)

    halo_wait(c3_halo)
    halo_wait(g_h4_halo)
    norm_forward(3, stat_total(3), True)

    def fourth_layer(hf, carry):
        shift, scale = carry
        with_halo(c3, hf, 2)
        with_halo(gh4, hf, 0)
        v = c3[hf]
        z = v * param(3, ALPHA, hf) + param(3, BETA, hf)
        gate = logistic(z)
        h = z * gate
        put_ec(ec4, hf, jnp.where(block_mask(h.shape, 1), h, 0.0))
        g = gh4[hf] * (gate + h * (1.0 - gate))
        gz4[hf] = g
        own = g[1 : rows + 1]
        xhat = v[1 : rows + 1] * param(3, RSTD, hf) + param(3, NMR, hf)
        return put_row(shift, hf, coarse_sum(own)), put_row(scale, hf, coarse_sum(own * xhat))

    sums = lax.fori_loop(0, half, fourth_layer, (zero_coarse, zero_coarse))
    stat_start(4, jnp.concatenate(list(sums) + pad_rows, axis=0))

    def coarse_output(hf, carry):
        out = dot_nt(coarse_window(ec4, hf), w4f[...]).reshape(rows, cols, 128)
        y = dv[hf, 1 : rows + 1] + out
        border(hout, 3, hf, y)
        edge = jnp.zeros((1, cols, 128), F32)
        put_ec(ecy, hf, jnp.concatenate([edge, y, edge], axis=0))
        return carry

    lax.fori_loop(0, half, coarse_output, 0)
    halo_start(y_halo)
    coarse_kernel_grad(stacked(4), ec4, ecg)

    norm_backward(3, stat_total(4), True)

    def third_back(hf, carry):
        shift, scale = carry
        g = (
            gz4[hf] * param(3, ALPHA, hf)
            + c3[hf] * param(3, COEF, hf)
            + param(3, BIAS, hf)
        )
        put_ec(ecg3, hf, jnp.where(block_mask(g.shape, 1), g, 0.0))
        back = dot_nn(coarse_window(ecg3, hf), w3b[...]).reshape(rows, cols, 128)
        border(hout, 4, hf, back)
        v = dv[hf, 1 : rows + 1]
        z = v * param(2, ALPHA, hf) + param(2, BETA, hf)
        gate = logistic(z)
        own = back * (gate + z * gate * (1.0 - gate))
        gz3[hf, 1 : rows + 1] = own
        xhat = v * param(2, RSTD, hf) + param(2, NMR, hf)
        return put_row(shift, hf, coarse_sum(own)), put_row(scale, hf, coarse_sum(own * xhat))

    sums = lax.fori_loop(0, half, third_back, (zero_coarse, zero_coarse))
    stat_start(5, jnp.concatenate(list(sums) + pad_rows, axis=0))
    halo_start(g_h3_halo)

    halo_wait(y_halo)

    def result_copy(f):
        return pltpu.make_async_copy(raw.at[f], res_hbm.at[f], out_sem.at[f])

    def unpair(lo, hi):
        count = lo.shape[0]
        both = jnp.stack([lo, hi], axis=1).reshape(count * 2, cols, 128)
        tmp[0 : 2 * count, pl.ds(0, cols, stride=2), :] = both
        tmp[0 : 2 * count, pl.ds(1, cols, stride=2), :] = swap(both)

    def merge(hf, carry):
        for side, row in ((0, 0), (1, rows + 1)):
            line = hal[3, side, hf].astype(F32)[None]
            up, down = neighbours(line)
            q = lax.broadcasted_iota(jnp.int32, line.shape, 1)
            ecy[hf, row, :, 0:128] = jnp.where(q == 0, 0.0, down)[0].astype(BF16)
            ecy[hf, row, :, 128:256] = line[0].astype(BF16)
            ecy[hf, row, :, 256:384] = jnp.where(q == cols - 1, 0.0, up)[0].astype(BF16)
        both = dot_nt(coarse_window(ecy, hf), wup[...])
        for hi in range(2):
            f = hf + hi * half
            out = dot_nt(window(esk, f, 2, rows), wsf[...]) + both[:, hi * 256 : hi * 256 + 256]
            out = out.reshape(rows, cols, 256)
            unpair(out[:, :, 0:128], out[:, :, 128:256])
            raw[f] = tmp[:, :, 0:64].astype(BF16)
            result_copy(f).start()
        return carry

    lax.fori_loop(0, half, merge, 0)
    coarse_kernel_grad(stacked(3), ec3, ecg3)

    halo_wait(g_h3_halo)
    norm_backward(2, stat_total(5), True)

    def down_back(hf, carry):
        for side, row in ((0, 0), (1, rows + 1)):
            v = dv[hf, row]
            z = v * param(2, ALPHA, hf) + param(2, BETA, hf)
            gate = logistic(z)
            gz3[hf, row] = hal[4, side, hf].astype(F32) * (gate + z * gate * (1.0 - gate))
        g = (
            gco[hf]
            + gz3[hf] * param(2, ALPHA, hf)
            + dv[hf] * param(2, COEF, hf)
            + param(2, BIAS, hf)
        )
        g = jnp.where(block_mask(g.shape, 1), g, 0.0)
        up, _ = neighbours(g)
        q = lax.broadcasted_iota(jnp.int32, g.shape, 1)
        ed[hf, 0 : rows + 2, :, 0:128] = g.astype(BF16)
        ed[hf, 0 : rows + 2, :, 128:256] = jnp.where(q == cols - 1, 0.0, up).astype(BF16)
        ed[hf, rows + 2] = jnp.zeros((cols, 256), BF16)
        lhs = jnp.concatenate([ed[hf, 0 : rows + 2], ed[hf, 1 : rows + 3]], axis=-1)
        back = dot_nn(lhs.reshape(ext, 512), wdb[...])
        back = back.astype(BF16).astype(F32).reshape(rows + 2, cols, 512)
        for hi in range(2):
            f = hf + hi * half
            total = gsa[f] + back[:, :, hi * 256 : hi * 256 + 256]
            gsa[f] = total
            put_e(eg2, f, 0, jnp.where(block_mask(total.shape, 1), total, 0.0))
        return carry

    lax.fori_loop(0, half, down_back, 0)

    def second_back(f, carry):
        shift, scale = carry
        back = dot_nn(window(eg2, f, 1, rows), w2b[...]).reshape(rows, cols, 256)
        hfout[0, f] = back[0, :, 0:128].astype(BF16)
        hfout[1, f] = back[rows - 1, :, 128:256].astype(BF16)
        v = c1[f, 1 : rows + 1]
        z = v * wide(1, ALPHA, f) + wide(1, BETA, f)
        gate = logistic(z)
        own = back * (gate + z * gate * (1.0 - gate))
        gz[f, 1 : rows + 1] = own
        xhat = v * wide(1, RSTD, f) + wide(1, NMR, f)
        return put_row(shift, f, full_sum(own)), put_row(scale, f, full_sum(own * xhat))

    sums = lax.fori_loop(0, frames, second_back, (zero_rows, zero_rows))
    stat_start(6, jnp.concatenate(sums, axis=0))
    halo_start(g_h2_halo)
    up_kernel_grad()
    down_kernel_grad(stacked(2))
    fine_kernel_grad(stacked(1), e2, 2, eg2, 1)
    halo_wait(g_h2_halo)
    norm_backward(1, stat_total(6), False)

    def first_back(f, carry):
        shift, scale = carry
        for side, row in ((0, 0), (1, rows + 1)):
            v = c1[f, row]
            lanes = slice(128, 256) if side == 0 else slice(0, 128)
            z = v[:, lanes] * param(1, ALPHA, f) + param(1, BETA, f)
            gate = logistic(z)
            g = hfull[side, f].astype(F32) * (gate + z * gate * (1.0 - gate))
            blank = jnp.zeros_like(g)
            gz[f, row] = jnp.concatenate([blank, g] if side == 0 else [g, blank], axis=-1)
        g = gz[f] * wide(1, ALPHA, f) + c1[f] * wide(1, COEF, f) + wide(1, BIAS, f)
        put_e(eg, f, 0, jnp.where(block_mask(g.shape, 1), g, 0.0))
        back = dot_nn(window(eg, f, 1, rows), w1b[...]).reshape(rows, cols, 256)
        v = xs[f, 2 : rows + 2].astype(F32)
        z = v * wide(0, ALPHA, f) + wide(0, BETA, f)
        gate = logistic(z)
        own = back * (gate + z * gate * (1.0 - gate))
        gz[f, 1 : rows + 1] = own
        xhat = v * wide(0, RSTD, f) + wide(0, NMR, f)
        return put_row(shift, f, full_sum(own)), put_row(scale, f, full_sum(own * xhat))

    sums = lax.fori_loop(0, frames, first_back, (zero_rows, zero_rows))
    stat_start(7, jnp.concatenate(sums, axis=0))
    fine_kernel_grad(stacked(0), e1, 2, eg, 1)
    norm_backward(0, stat_total(7), False)

    def frames_copy(f):
        slot = lax.rem(f, 2)
        return pltpu.make_async_copy(fst.at[slot], fg_hbm.at[f], fg_sem.at[slot])

    def frames_back(f, carry):
        g = (
            gsa[f, 1 : rows + 1]
            + gz[f, 1 : rows + 1] * wide(0, ALPHA, f)
            + xs[f, 2 : rows + 2].astype(F32) * wide(0, COEF, f)
            + wide(0, BIAS, f)
        )
        unpair(g[:, :, 0:128], g[:, :, 128:256])

        @pl.when(f >= 2)
        def _():
            frames_copy(f - 2).wait()

        fst[lax.rem(f, 2)] = tmp[:, :, 0:64]
        frames_copy(f).start()
        return carry

    lax.fori_loop(0, frames, frames_back, 0)

    frames_copy(frames - 2).wait()
    frames_copy(frames - 1).wait()
    for f in range(frames):
        result_copy(f).wait()
    for copies in (x_halo, g_halo, g_h4_halo, d_halo, c3_halo, y_halo, g_h3_halo, g_h2_halo):
        halo_finish(copies)


def run_step(n, frames, cotangent, actions, noise_ids, games, live_counts, cw, nm, table):
    count, strip, breadth, _ = frames.shape
    half, rows, cols = count // 2, strip // 2, breadth // 2
    fine = (count, rows + 4, cols, 512)
    coarse = (half, rows + 2, cols, 128)
    coarse_e = (half, rows + 2, cols, 384)
    scratch = [
        VM((count, strip, breadth, 64), BF16),
        VM((2, 2, count, 3, breadth, 64), BF16),
        VM((strip, breadth, 128), F32),
        VM((2, strip, breadth, 64), F32),
        VM((count, rows + 4, cols, 256), BF16),
        VM(fine, BF16),
        VM(fine, BF16),
        VM(fine, BF16),
        VM(fine, BF16),
        VM((count, rows + 2, cols, 512), BF16),
        VM((count, rows + 2, cols, 256), F32),
        VM((count, rows + 2, cols, 256), F32),
        VM((count, rows + 2, cols, 256), F32),
        VM(coarse, F32),
        VM(coarse, F32),
        VM(coarse, F32),
        VM(coarse, F32),
        VM(coarse, F32),
        VM(coarse, F32),
        VM(coarse_e, BF16),
        VM(coarse_e, BF16),
        VM(coarse_e, BF16),
        VM(coarse_e, BF16),
        VM(coarse_e, BF16),
        VM((half, rows + 3, cols, 256), BF16),
        VM((256, 1024), BF16),
        VM((1024, 256), BF16),
        VM((256, 1024), BF16),
        VM((1024, 256), BF16),
        VM((256, 1024), BF16),
        VM((1024, 256), BF16),
        VM((512, 1152), BF16),
        VM((2, 1024, 128), BF16),
        VM((128, 1536), BF16),
        VM((512, 512), BF16),
        VM((128, 1152), BF16),
        VM((1152, 128), BF16),
        VM((128, 1152), BF16),
        VM((1152, 128), BF16),
        VM((2, 256, 1152), F32),
        VM((32, count, 128), F32),
        VM((128, 256), F32),
        VM((8, n, 2 * count, 128), F32),
        VM((5, 2, half, cols, 128), BF16),
        VM((5, 2, half, cols, 128), BF16),
        VM((2, count, cols, 128), BF16),
        VM((2, count, cols, 128), BF16),
        pltpu.SemaphoreType.DMA((2,)),
        pltpu.SemaphoreType.DMA((count,)),
        pltpu.SemaphoreType.DMA((2,)),
        pltpu.SemaphoreType.DMA((8, n - 1)),
        pltpu.SemaphoreType.DMA((8, n - 1)),
        pltpu.SemaphoreType.DMA((8, 2)),
        pltpu.SemaphoreType.DMA((8, 2)),
    ]
    smem = pl.BlockSpec(memory_space=pltpu.SMEM)
    vmem = pl.BlockSpec(memory_space=pltpu.VMEM)
    hbm = pl.BlockSpec(memory_space=pl.ANY)
    return pl.pallas_call(
        functools.partial(step_kernel, n),
        out_shape=(
            jax.ShapeDtypeStruct(frames.shape, BF16),
            jax.ShapeDtypeStruct(frames.shape, F32),
            jax.ShapeDtypeStruct((32, 64, 128), BF16),
            jax.ShapeDtypeStruct((count, 896), F32),
        ),
        in_specs=[hbm, hbm, smem, smem, smem, smem, vmem, vmem, vmem],
        out_specs=(hbm, hbm, vmem, vmem),
        scratch_shapes=scratch,
        compiler_params=pltpu.CompilerParams(
            collective_id=0, has_side_effects=True, vmem_limit_bytes=62 * 1024 * 1024
        ),
        name="step",
    )(frames, cotangent, actions, noise_ids, games, live_counts, cw, nm, table)


def adamw(weight, moment, square, grad_value, rate):
    fix_one = 1.0 - BETA_ONE**ADAM_STEP
    fix_two = 1.0 - BETA_TWO**ADAM_STEP
    moment_new = BETA_ONE * moment + (1.0 - BETA_ONE) * grad_value
    square_new = BETA_TWO * square + (1.0 - BETA_TWO) * grad_value * grad_value
    fixed_m = moment_new / fix_one
    fixed_v = square_new / fix_two
    weight_new = weight - rate * (fixed_m / (jnp.sqrt(fixed_v) + ADAM_EPS) + DECAY * weight)
    return (moment_new, square_new, weight_new, weight_new.astype(BF16))


def reduce_kernel(
    nd, ns, gt, pk, out, packs, rbuf, part, zbuf, own, sem_a, sem_b, sem_c, sem_d, sem_p, bar_unused
):
    dp = lax.axis_index("dp")
    sp = lax.axis_index("space")
    barrier = pltpu.get_barrier_semaphore()
    for off in range(1, nd):
        pl.semaphore_signal(
            barrier, inc=1, device_id={"dp": lax.rem(dp + off, nd)}, device_id_type=MESH
        )
    for off in range(1, ns):
        pl.semaphore_signal(
            barrier, inc=1, device_id={"space": lax.rem(sp + off, ns)}, device_id_type=MESH
        )
    pl.semaphore_wait(barrier, nd + ns - 2)

    def copy(src, dst, sems, off, axis):
        here, size = (dp, nd) if axis == "dp" else (sp, ns)
        return pltpu.make_async_remote_copy(
            src_ref=src,
            dst_ref=dst,
            send_sem=sems.at[0, off - 1],
            recv_sem=sems.at[1, off - 1],
            device_id={axis: lax.rem(here + off, size)},
            device_id_type=MESH,
        )

    def before(off, axis):
        here, size = (dp, nd) if axis == "dp" else (sp, ns)
        return lax.rem(here + size - off, size)

    def after(off, axis):
        here, size = (dp, nd) if axis == "dp" else (sp, ns)
        return lax.rem(here + off, size)

    packs[dp] = pk[...]
    for off in range(1, nd):
        copy(gt.at[after(off, "dp")], rbuf.at[dp], sem_a, off, "dp").start()
    for off in range(1, nd):
        copy(packs.at[dp], packs.at[dp], sem_p, off, "dp").start()
    rbuf[dp] = gt[dp]
    for off in range(1, nd):
        copy(gt.at[0], rbuf.at[before(off, "dp")], sem_a, off, "dp").wait_recv()
    total = rbuf[0].astype(F32)
    for i in range(1, nd):
        total = total + rbuf[i].astype(F32)
    part[...] = total
    for off in range(1, ns):
        copy(part.at[after(off, "space")], zbuf.at[sp], sem_b, off, "space").start()
    zbuf[sp] = part[sp]
    for off in range(1, ns):
        copy(part.at[0], zbuf.at[before(off, "space")], sem_b, off, "space").wait_recv()
    total = zbuf[0]
    for i in range(1, ns):
        total = total + zbuf[i]
    out[dp, sp] = total.astype(BF16)
    for off in range(1, ns):
        copy(out.at[dp, sp], out.at[dp, sp], sem_c, off, "space").start()
    for off in range(1, ns):
        slot = before(off, "space")
        copy(out.at[dp, slot], out.at[dp, slot], sem_c, off, "space").wait_recv()
    for off in range(1, nd):
        copy(out.at[dp], out.at[dp], sem_d, off, "dp").start()
    for off in range(1, nd):
        slot = before(off, "dp")
        copy(out.at[slot], out.at[slot], sem_d, off, "dp").wait_recv()
        copy(packs.at[slot], packs.at[slot], sem_p, off, "dp").wait_recv()
    for off in range(1, nd):
        copy(gt.at[0], rbuf.at[dp], sem_a, off, "dp").wait_send()
        copy(packs.at[dp], packs.at[dp], sem_p, off, "dp").wait_send()
        copy(out.at[dp], out.at[dp], sem_d, off, "dp").wait_send()
    for off in range(1, ns):
        copy(part.at[0], zbuf.at[sp], sem_b, off, "space").wait_send()
        copy(out.at[dp, sp], out.at[dp, sp], sem_c, off, "space").wait_send()


def run_reduce(nd, ns, gt, pack):
    rpd = 2048 // (nd * ns)
    shape = (nd, ns, rpd, 128)
    vmem = pl.BlockSpec(memory_space=pltpu.VMEM)
    sems = lambda k: pltpu.SemaphoreType.DMA((2, k - 1))
    return pl.pallas_call(
        functools.partial(reduce_kernel, nd, ns),
        out_shape=(
            jax.ShapeDtypeStruct(shape, BF16),
            jax.ShapeDtypeStruct((nd,) + pack.shape, F32),
        ),
        in_specs=[vmem, vmem],
        out_specs=(vmem, vmem),
        scratch_shapes=[
            VM(shape, BF16),
            VM(shape[1:], F32),
            VM(shape[1:], F32),
            VM(shape[2:], F32),
            sems(nd),
            sems(ns),
            sems(ns),
            sems(nd),
            sems(nd),
            pltpu.SemaphoreType.REGULAR,
        ],
        compiler_params=pltpu.CompilerParams(
            collective_id=1, has_side_effects=True, vmem_limit_bytes=32 * 1024 * 1024
        ),
        name="reduce",
    )(gt.reshape(shape), pack)


def local(
    nd,
    ns,
    frames,
    cotangent,
    actions,
    noise_ids,
    games,
    live_counts,
    conv_weight,
    conv_moment,
    conv_square,
    norm_map,
    norm_moment,
    norm_square,
    emb_table,
    table_moment,
    table_square,
):
    cw = conv_weight.T
    nm = jnp.transpose(norm_map, (1, 0, 2)).reshape(-1, 128)
    result, frames_grad, gt, pack = run_step(
        ns, frames, cotangent, actions, noise_ids, games, live_counts, cw, nm, emb_table
    )
    grads, packs = run_reduce(nd, ns, gt, pack)
    conv_rows = conv_weight.shape[0]
    grad_t = (
        grads.reshape(32, 64, 128).transpose(1, 0, 2).reshape(64, 4096)[:, :conv_rows].astype(F32)
    )
    conv_out = [v.T for v in adamw(cw, conv_moment.T, conv_square.T, grad_t, 0.05)]
    packs = packs.reshape(-1, 896)
    dmods = packs[:, 0:512]
    embedded = packs[:, 512:768]
    hot = packs[:, 768 : 768 + emb_table.shape[0]]
    top = jnp.dot(embedded.T, dmods, precision=HIGH).reshape(256, 4, 128)
    last = jnp.sum(dmods, axis=0).reshape(1, 4, 128)
    grad_map = jnp.concatenate([top, last], axis=0).transpose(1, 0, 2)
    norm_out = adamw(norm_map, norm_moment, norm_square, grad_map, 0.04)
    g_embed = jnp.dot(
        dmods, norm_map[:, :-1].transpose(0, 2, 1).reshape(512, 256), precision=HIGH
    )
    grad_table = jnp.dot(hot.T, g_embed, precision=HIGH)
    table_out = adamw(emb_table, table_moment, table_square, grad_table, 0.5)
    return (result, frames_grad, *conv_out, *norm_out, *table_out)


def solution(mesh):
    split = P("dp", "space", None, None)
    in_specs = (split, split) + (P("dp"),) * 4 + (P(),) * 9
    out_specs = (split, split) + (P(),) * 12
    sizes = dict(mesh.shape)
    return jax.shard_map(
        functools.partial(local, sizes["dp"], sizes["space"]),
        mesh=mesh,
        in_specs=in_specs,
        out_specs=out_specs,
        check_vma=False,
    )
```

time: 542 us -> 129 us (0.24); the launches traced: 532 us -> 128 us
  waiting for transfers between devices: 145 us -> 0 us
  Pallas kernels: 0 us -> 109 us
  local copies, waits for them, and re-layouts: 112 us -> 9.59 us
  matrix products: 98.7 us -> 2.34 us
  starting transfers between devices: 56.4 us -> 0 us
  other arithmetic: 59 us -> 5.97 us
  blocking collectives: 44.4 us -> 0 us
  between operations: 16.8 us -> 1.4 us
    psum x1 -> x0, waiting for transfers between devices: 122 us -> none  [local(): lax.psum((grad_conv, grad_map, grad_table), ('dp', 'space'))]
    pallas_call x0 -> x2, Pallas kernels: none -> 109 us  [the longest x1 83.7 us: run_step(): pl.pallas_call(functools.partial(step_kernel, n), out_shape=(jax.ShapeDty...]
    conv_general_dilated x17 -> x0, matrix products: 88.4 us -> none  [the longest x6 45.5 us: conv_rows(): lax.conv_general_dilated(padded, kernel, (1, 1), ((0, 0), (1, 1)), dimens...]
    psum x4 -> x0, blocking collectives: 44.4 us -> none  [the longest x2 22.6 us: backward_element_count(): return lax.psum(pair, 'space')]
    unnamed x243 -> x26, local copies, waits for them, and re-layouts: 51.2 us -> 7.27 us
    ppermute x12 -> x0, starting transfers between devices: 37.9 us -> none  [the longest x6 29.5 us: with_halo(): lax.ppermute(lax.slice_in_dim(block, block.shape[dim] - width, None, axis...]
    convert_element_type x18 -> x1, other arithmetic: 34.4 us -> 2.09 us  [adamw(): return (moment_new, square_new, weight_new, weight_new.astype(BF16))]
    all_to_all x4 -> x0, starting transfers between devices: 18.5 us -> none  [the longest x1 5.09 us: local(): lax.all_to_all(skip, 'space', split_axis=0, concat_axis=1, tiled=True)]
  transfers between devices with their start and end apart: 17 -> 0, of which waited for: 4 -> 0; matrix products, arithmetic and copies ran while one was open for 29% -> 0% of each run, Pallas kernels for 0% -> 0%
where the time goes in v1:
time: 129 us; the launch traced here: 128 us
  Pallas kernels  109 us (84%)
  local copies, waits for them, and re-layouts  9.59 us (7%)
  other arithmetic  5.97 us (5%)
  matrix products  2.34 us (2%)
  between operations  1.4 us (1%)
    pallas_call x1, Pallas kernels, run_step(): pl.pallas_call(functools.partial(step_kernel, n), out_shape=(jax.ShapeDty...  83.7 us
    pallas_call x1, Pallas kernels, run_reduce(): pl.pallas_call(functools.partial(reduce_kernel, nd, ns), out_shape=(jax.S...  25.4 us
    unnamed x26, local copies, waits for them, and re-layouts  7.27 us
    transpose x1, other arithmetic, local(): conv_out = [v.T for v in adamw(cw, conv_moment.T, conv_square.T, grad_t,...  3.86 us

profile of v1, /device:TPU:0, one launch (start us, length us, event | category | flops | bytes accessed | tf_op | source)
XLA Modules:
  0.0 128.4 jit_solution(2662640867194212674)
XLA Ops:
  1.3 2.0 %reshape.52.nm_ref = f32[1028,128]{1,0:T(8,128)} reshape(f32[257,4,128]{2,1,0:T(4,128)} %bitcast.57) | data formatting | bytes 1052672 | tf_op jit(solution)/shard_map/reshape | solution.py:1212
  3.3 0.0 copy-start.4
  3.3 83.7 %step.1 = (bf16[8,16,64,64]{3,2,1,0:T(8,128)(2,1)}, f32[8,16,64,64]{3,2,1,0:T(8,128)}, bf16[32,64,128]{2,1,0:T(8,128)(2,1)}, f32[8,896]{1,0:T(8,128)}) custom-call(bf16[8,16,64,64]{3,2,1,0:T(8,128)(2,1)} %x_hbm.1, bf16[8,16,64,64]{3,2,1,0:T(8,128)(2,1)} %cot_hbm.1, s32[8]{0:T(128)} %act_ref.1, s32[8]{0:T(128)} %noise_ref.1, s32[8]{0:T(128)} %game_ref.1, ...), custom_call_target="tpu_custom_call" | custom-call | tf_op jit(solution)/shard_map/step/pallas_call | solution.py:1055
  87.0 0.0 copy-start
  87.0 1.0 copy-done
  88.1 0.0 copy-start.1
  88.1 0.7 copy-done.1
  88.8 0.0 copy-start.6
  88.8 25.4 %reduce.1 = (bf16[8,4,64,128]{3,2,1,0:T(8,128)(2,1)S(1)}, f32[8,8,896]{2,1,0:T(8,128)S(1)}) custom-call(bf16[8,4,64,128]{3,2,1,0:T(8,128)(2,1)S(1)} %bitcast.55, f32[8,896]{1,0:T(8,128)S(1)} %copy-done.1), custom_call_target="tpu_custom_call" | custom-call | tf_op jit(solution)/shard_map/reduce/pallas_call | solution.py:1165
  114.3 0.1 copy.37
  114.4 0.0 copy-done.4
  114.4 0.0 copy-done.6
  114.4 3.9 %convert_bitcast_fusion = (bf16[4032,64]{0,1:T(8,128)(2,1)}, f32[64,4032]{1,0:T(8,128)}, f32[4032,64]{0,1:T(8,128)}, f32[4032,64]{0,1:T(8,128)}) fusion(f32[4032,64]{0,1:T(8,128)S(1)} %copy-done.6, bf16[64,4096]{1,0:T(8,128)(2,1)S(1)} %bitcast.59, f32[4032,64]{0,1:T(8,128)} %param.22, f32[4032,64]{0,1:T(8,128)S(1)} %copy-done.4), kind=kLoop, calls=%fused_computation.15 | loop fusion | flops 4128768 | bytes 7225344 | tf_op jit(solution)/shard_map/transpose | solution.py:1221
  118.2 0.0 copy-start.2
  118.3 0.0 copy-start.7
  118.3 0.0 copy-start.8
  118.3 0.6 fusion.8
  118.9 0.2 reshape.57
  119.1 0.2 copy-done.2
  119.3 0.2 copy-done.7
  119.5 0.2 copy-done.8
  119.6 0.0 copy-start.9
  119.6 0.0 copy-start.10
  119.6 0.0 copy-start.11
  119.6 2.1 %fusion.16 = (bf16[4,257,128]{2,0,1:T(4,128)(2,1)}, f32[4,257,128]{2,0,1:T(4,128)}, f32[4,257,128]{2,0,1:T(4,128)}, f32[4,257,128]{2,0,1:T(4,128)}) fusion(f32[4,257,128]{2,0,1:T(4,128)S(1)} %copy-done.2, f32[1,4,128]{2,1,0:T(4,128)S(1)} %bitcast.62, f32[256,4,128]{2,1,0:T(4,128)S(1)} %reshape.57, f32[4,257,128]{2,0,1:T(4,128)S(1)} %copy-done.7, ...), kind=kLoop, calls=%fused_computation.28 | loop fusion | flops 2105344 | bytes 3947520 | tf_op jit(solution)/shard_map/convert_element_type | solution.py:1081
  121.7 0.0 copy-start.5
  121.7 0.6 fusion.4
  122.4 0.0 copy-done.9
  122.4 0.0 copy-done.10
  122.4 0.0 copy-done.11
  122.4 1.1 fusion.14
  123.5 0.0 copy-done.5
  123.5 0.0 copy-start.3
  123.5 1.3 %copy.41 = bf16[8,16,64,64]{3,2,1,0:T(8,128)(2,1)} copy(bf16[8,16,64,64]{3,2,1,0:T(8,128)(2,1)S(1)} %copy-done.5) | data formatting | bytes 2097152
  124.8 1.6 %copy-done.3 = f32[8,16,64,64]{3,2,1,0:T(8,128)S(1)} copy-done((f32[8,16,64,64]{3,2,1,0:T(8,128)S(1)}, f32[8,16,64,64]{3,2,1,0:T(8,128)}, u32[]{:S(2)}) %copy-start.3) | copy-done | bytes 2097176
  126.4 2.0 %copy.42 = f32[8,16,64,64]{3,2,1,0:T(8,128)} copy(f32[8,16,64,64]{3,2,1,0:T(8,128)S(1)} %copy-done.3) | data formatting | bytes 4194304
  (2 shorter events, 0.1 us)
Async XLA Ops:
  3.3 111.1 %copy-start.4 = (f32[4032,64]{0,1:T(8,128)S(1)}, f32[4032,64]{0,1:T(8,128)}, u32[]{:S(2)}) copy-start(f32[4032,64]{0,1:T(8,128)} %param.21) | copy-start | bytes 3096580
  87.0 1.0 copy-start
  88.1 0.7 copy-start.1
  88.8 25.6 %copy-start.6 = (f32[4032,64]{0,1:T(8,128)S(1)}, f32[4032,64]{0,1:T(8,128)}, u32[]{:S(2)}) copy-start(f32[4032,64]{0,1:T(8,128)} %param.23) | copy-start | bytes 3096580
  118.2 1.0 copy-start.2
  118.3 1.2 copy-start.7
  118.3 1.4 %copy-start.8 = (f32[4,257,128]{2,0,1:T(4,128)S(1)}, f32[4,257,128]{2,0,1:T(4,128)}, u32[]{:S(2)}) copy-start(f32[4,257,128]{2,0,1:T(4,128)} %param.25) | copy-start | bytes 1579012
  119.6 2.7 %copy-start.9 = (f32[108,256]{1,0:T(8,128)S(1)}, f32[108,256]{1,0:T(8,128)}, u32[]{:S(2)}) copy-start(f32[108,256]{1,0:T(8,128)} %tab_ref.1) | copy-start | bytes 331780
  119.6 2.8 %copy-start.10 = (f32[108,256]{1,0:T(8,128)S(1)}, f32[108,256]{1,0:T(8,128)}, u32[]{:S(2)}) copy-start(f32[108,256]{1,0:T(8,128)} %param.29) | copy-start | bytes 331780
  119.6 2.8 %copy-start.11 = (f32[108,256]{1,0:T(8,128)S(1)}, f32[108,256]{1,0:T(8,128)}, u32[]{:S(2)}) copy-start(f32[108,256]{1,0:T(8,128)} %param.28) | copy-start | bytes 331780
  121.7 1.8 %copy-start.5 = (bf16[8,16,64,64]{3,2,1,0:T(8,128)(2,1)S(1)}, bf16[8,16,64,64]{3,2,1,0:T(8,128)(2,1)}, u32[]{:S(2)}) copy-start(bf16[8,16,64,64]{3,2,1,0:T(8,128)(2,1)} %get-tuple-element.52) | copy-start | bytes 3145732
  123.5 2.9 %copy-start.3 = (f32[8,16,64,64]{3,2,1,0:T(8,128)S(1)}, f32[8,16,64,64]{3,2,1,0:T(8,128)}, u32[]{:S(2)}) copy-start(f32[8,16,64,64]{3,2,1,0:T(8,128)} %get-tuple-element.53) | copy-start | bytes 6291460

commit v2 on v1

--- a/solution.py
+++ b/solution.py
@@ -63,6 +63,7 @@
 
 
 def step_kernel(
+    nd,
     n,
     x_hbm,
     cot_hbm,
@@ -71,12 +72,12 @@
     game_ref,
     live_ref,
     cw_ref,
-    nm_ref,
+    nm_hbm,
     tab_ref,
     res_hbm,
     fg_hbm,
-    gt_ref,
-    pack_ref,
+    gout_ref,
+    packs,
     raw,
     xh,
     tmp,
@@ -124,6 +125,14 @@
     hout,
     hfull,
     hfout,
+    nmv,
+    nmb,
+    gt_ref,
+    rbuf,
+    part,
+    zbuf,
+    zfull,
+    gall,
     local_sem,
     out_sem,
     fg_sem,
@@ -131,6 +140,10 @@
     stat_recv,
     halo_send,
     halo_recv,
+    dp_send,
+    dp_recv,
+    sp_send,
+    sp_recv,
 ):
     frames, strip = raw.shape[0], raw.shape[1]
     breadth = raw.shape[2]
@@ -138,6 +151,7 @@
     rows = strip // 2
     cols = breadth // 2
     me = lax.axis_index("space")
+    dp = lax.axis_index("dp")
     full_cells = float(strip * n * breadth * 32)
     coarse_cells = full_cells / 4.0
     owned = rows * cols
@@ -151,10 +165,24 @@
             device_id={"space": lax.rem(me + off, n)},
             device_id_type=MESH,
         )
+    for off in range(1, nd):
+        pl.semaphore_signal(
+            barrier,
+            inc=1,
+            device_id={"dp": lax.rem(dp + off, nd)},
+            device_id_type=MESH,
+        )
 
     x_copy = pltpu.make_async_copy(x_hbm, raw, local_sem.at[0])
     x_copy.start()
-    pl.semaphore_wait(barrier, n - 1)
+    map_copies = [
+        pltpu.make_async_copy(nm_hbm.at[pl.ds(0, 256), k], nmv.at[k], local_sem.at[2 + k])
+        for k in range(4)
+    ]
+    map_copies.append(pltpu.make_async_copy(nm_hbm.at[256], nmb, local_sem.at[6]))
+    for copy in map_copies:
+        copy.start()
+    pl.semaphore_wait(barrier, n + nd - 2)
 
     def halo_copies(k, first, last, to_up, to_down):
         up = pltpu.make_async_remote_copy(
@@ -393,7 +421,132 @@
         else:
             scale_all = scale_grad + swap(scale_grad)
             shift_all = shift_grad + swap(shift_grad)
-        pack_ref[:, k * 128 : (k + 1) * 128] = join(scale_all, swap(shift_all))
+        packs[dp, :, k * 128 : (k + 1) * 128] = join(scale_all, swap(shift_all))
+
+    slots = 32 // nd
+    share = 64 // n
+    first_slots = [
+        [i for i in range(slots) if i * nd >= 16],
+        [i for i in range(slots) if 8 <= i * nd < 16],
+        [0],
+    ]
+
+    def dp_before(off):
+        return lax.rem(dp + nd - off, nd)
+
+    def dp_after(off):
+        return lax.rem(dp + off, nd)
+
+    def sp_before(off):
+        return lax.rem(me + n - off, n)
+
+    def sp_after(off):
+        return lax.rem(me + off, n)
+
+    def stage_slots(stage):
+        chosen = first_slots[stage]
+        return pl.ds(chosen[0], len(chosen))
+
+    def dp_copy(stage, phase, src, dst, off):
+        return pltpu.make_async_remote_copy(
+            src_ref=src,
+            dst_ref=dst,
+            send_sem=dp_send.at[stage, phase, off - 1],
+            recv_sem=dp_recv.at[stage, phase, off - 1],
+            device_id={"dp": dp_after(off)},
+            device_id_type=MESH,
+        )
+
+    def sp_copy(stage, phase, src, dst, off):
+        return pltpu.make_async_remote_copy(
+            src_ref=src,
+            dst_ref=dst,
+            send_sem=sp_send.at[stage, phase, off - 1],
+            recv_sem=sp_recv.at[stage, phase, off - 1],
+            device_id={"space": sp_after(off)},
+            device_id_type=MESH,
+        )
+
+    def first_copy(stage, off, owner, slot):
+        where = stage_slots(stage)
+        return dp_copy(stage, 0, gt_ref.at[where, owner], rbuf.at[slot, where], off)
+
+    def second_copy(stage, off, row, slot):
+        where = stage_slots(stage)
+        return sp_copy(stage, 0, part.at[row, where], zbuf.at[slot, where], off)
+
+    def third_copy(stage, off, slot):
+        where = stage_slots(stage)
+        return sp_copy(stage, 1, zfull.at[slot, where], zfull.at[slot, where], off)
+
+    def fourth_copy(stage, off, slot):
+        where = stage_slots(stage)
+        return dp_copy(stage, 1, gall.at[slot, where], gall.at[slot, where], off)
+
+    def pack_copy(which, off, slot):
+        lanes = pl.ds(0, 128) if which else pl.ds(128, 768)
+        return dp_copy(3, which, packs.at[slot, :, lanes], packs.at[slot, :, lanes], off)
+
+    def pack_start(which):
+        for off in range(1, nd):
+            pack_copy(which, off, dp).start()
+
+    def gather_start(stage):
+        if not first_slots[stage]:
+            return
+        for off in range(1, nd):
+            first_copy(stage, off, dp_after(off), dp).start()
+
+    def gather_space(stage):
+        if not first_slots[stage]:
+            return
+        where = stage_slots(stage)
+        for off in range(1, nd):
+            first_copy(stage, off, dp, dp_before(off)).wait_recv()
+        rbuf[dp, where] = gt_ref[where, dp]
+        total = rbuf[0, where].astype(F32)
+        for i in range(1, nd):
+            total = total + rbuf[i, where].astype(F32)
+        for z in range(n):
+            part[z, where] = total[:, z * share : (z + 1) * share]
+        for off in range(1, n):
+            second_copy(stage, off, sp_after(off), me).start()
+
+    def gather_spread(stage):
+        if not first_slots[stage]:
+            return
+        where = stage_slots(stage)
+        for off in range(1, n):
+            second_copy(stage, off, me, sp_before(off)).wait_recv()
+        zbuf[me, where] = part[me, where]
+        total = zbuf[0, where]
+        for i in range(1, n):
+            total = total + zbuf[i, where]
+        zfull[me, where] = total
+        for off in range(1, n):
+            third_copy(stage, off, me).start()
+
+    def gather_all(stage):
+        if not first_slots[stage]:
+            return
+        where = stage_slots(stage)
+        for off in range(1, n):
+            third_copy(stage, off, sp_before(off)).wait_recv()
+        whole = jnp.concatenate([zfull[z, where] for z in range(n)], axis=1)
+        gall[dp, where] = whole.astype(BF16)
+        for off in range(1, nd):
+            fourth_copy(stage, off, dp).start()
+
+    def gather_finish(stage):
+        if not first_slots[stage]:
+            return
+        for off in range(1, nd):
+            fourth_copy(stage, off, dp_before(off)).wait_recv()
+            first_copy(stage, off, dp_after(off), dp).wait_send()
+            fourth_copy(stage, off, dp).wait_send()
+        for off in range(1, n):
+            second_copy(stage, off, sp_after(off), me).wait_send()
+            third_copy(stage, off, me).wait_send()
 
     x_copy.wait()
 
@@ -426,12 +579,12 @@
         tabp[...] = jnp.zeros(tabp.shape, F32)
         tabp[0:table_rows, :] = tab_ref[...]
         embedded = dot_high(hot, tabp[...])
-        pack_ref[:, 512:768] = embedded
-        pack_ref[:, 768:896] = hot
+        packs[dp, :, 512:768] = embedded
+        packs[dp, :, 768:896] = hot
+        for copy in map_copies:
+            copy.wait()
         for k in range(4):
-            mod = dot_high(embedded, nm_ref[pl.ds(k, 256, stride=4), :]) + nm_ref[
-                1024 + k : 1025 + k, :
-            ]
+            mod = dot_high(embedded, nmv[k]) + nmb[k : k + 1, :]
             scale = join(mod, swap(mod)) + 1.0
             shift = join(swap(mod), mod)
             if k < 2:
@@ -620,22 +773,6 @@
 
     lax.fori_loop(0, frames, load_g, 0)
 
-    def coarse_gradient(hf, carry):
-        g = dot_nn(window(eg, hf, 1, rows + 2), wco[0]) + dot_nn(
-            window(eg, hf + half, 1, rows + 2), wco[1]
-        )
-        g = g.reshape(rows + 2, cols, 128)
-        g = jnp.where(block_mask(g.shape, 1), g, 0.0).astype(BF16).astype(F32)
-        gco[hf] = g
-        put_ec(ecg, hf, g)
-        back = dot_nn(coarse_window(ecg, hf), w4b[...]).reshape(rows, cols, 128)
-        gh4[hf, 1 : rows + 1] = back
-        border(hout, 0, hf, back)
-        return carry
-
-    lax.fori_loop(0, half, coarse_gradient, 0)
-    halo_start(g_h4_halo)
-
     norm_forward(1, stat_total(1), False)
 
     def second_layer(f, carry):
@@ -676,11 +813,27 @@
     stat_start(2, jnp.concatenate(list(sums) + pad_rows, axis=0))
     halo_start(d_halo)
 
+    def coarse_gradient(hf, carry):
+        g = dot_nn(window(eg, hf, 1, rows + 2), wco[0]) + dot_nn(
+            window(eg, hf + half, 1, rows + 2), wco[1]
+        )
+        g = g.reshape(rows + 2, cols, 128)
+        g = jnp.where(block_mask(g.shape, 1), g, 0.0).astype(BF16).astype(F32)
+        gco[hf] = g
+        put_ec(ecg, hf, g)
+        back = dot_nn(coarse_window(ecg, hf), w4b[...]).reshape(rows, cols, 128)
+        gh4[hf, 1 : rows + 1] = back
+        border(hout, 0, hf, back)
+        return carry
+
+    lax.fori_loop(0, half, coarse_gradient, 0)
+    halo_start(g_h4_halo)
+
     def put_half(index, value):
-        tile = index // 2
-        current = gt_ref[tile].astype(F32)
+        slot, owner = index // 2 // nd, index // 2 % nd
+        current = gt_ref[slot, owner].astype(F32)
         value = join(current, swap(value)) if index % 2 else join(value, current)
-        gt_ref[tile] = value.astype(BF16)
+        gt_ref[slot, owner] = value.astype(BF16)
 
     gt_ref[...] = jnp.zeros(gt_ref.shape, BF16)
 
@@ -765,7 +918,6 @@
                 )
                 put_half(45 + (ta * 3 + tb) * 2 + 1, total)
 
-    fine_kernel_grad(lambda t, s: 45 + (t * 3 + s) * 2, esk, 2, eg, 2)
 
     halo_wait(d_halo)
     norm_forward(2, stat_total(2), True)
@@ -784,6 +936,7 @@
     sums = lax.fori_loop(0, half, third_layer, (zero_coarse, zero_coarse))
     stat_start(3, jnp.concatenate(list(sums) + pad_rows, axis=0))
     halo_start(c3_halo)
+    fine_kernel_grad(lambda t, s: 45 + (t * 3 + s) * 2, esk, 2, eg, 2)
 
     halo_wait(c3_halo)
     halo_wait(g_h4_halo)
@@ -874,6 +1027,8 @@
 
     lax.fori_loop(0, half, merge, 0)
     coarse_kernel_grad(stacked(3), ec3, ecg3)
+    up_kernel_grad()
+    gather_start(0)
 
     halo_wait(g_h3_halo)
     norm_backward(2, stat_total(5), True)
@@ -924,9 +1079,10 @@
     sums = lax.fori_loop(0, frames, second_back, (zero_rows, zero_rows))
     stat_start(6, jnp.concatenate(sums, axis=0))
     halo_start(g_h2_halo)
-    up_kernel_grad()
     down_kernel_grad(stacked(2))
     fine_kernel_grad(stacked(1), e2, 2, eg2, 1)
+    gather_start(1)
+    gather_space(0)
     halo_wait(g_h2_halo)
     norm_backward(1, stat_total(6), False)
 
@@ -951,10 +1107,17 @@
         xhat = v * wide(0, RSTD, f) + wide(0, NMR, f)
         return put_row(shift, f, full_sum(own)), put_row(scale, f, full_sum(own * xhat))
 
+    pack_start(0)
     sums = lax.fori_loop(0, frames, first_back, (zero_rows, zero_rows))
     stat_start(7, jnp.concatenate(sums, axis=0))
+    gather_spread(0)
+    gather_space(1)
     fine_kernel_grad(stacked(0), e1, 2, eg, 1)
+    gather_start(2)
     norm_backward(0, stat_total(7), False)
+    pack_start(1)
+    gather_all(0)
+    gather_spread(1)
 
     def frames_copy(f):
         slot = lax.rem(f, 2)
@@ -978,6 +1141,20 @@
         return carry
 
     lax.fori_loop(0, frames, frames_back, 0)
+    gather_space(2)
+    gather_all(1)
+    gather_spread(2)
+    gather_all(2)
+    for stage in range(3):
+        gather_finish(stage)
+    for off in range(1, nd):
+        for which in range(2):
+            pack_copy(which, off, dp_before(off)).wait_recv()
+            pack_copy(which, off, dp).wait_send()
+    for slot in range(slots):
+        for owner in range(nd):
+            lane = (slot * nd + owner) * 128
+            gout_ref[:, lane : lane + 128] = gall[owner, slot]
 
     frames_copy(frames - 2).wait()
     frames_copy(frames - 1).wait()
@@ -987,7 +1164,7 @@
         halo_finish(copies)
 
 
-def run_step(n, frames, cotangent, actions, noise_ids, games, live_counts, cw, nm, table):
+def run_step(nd, n, frames, cotangent, actions, noise_ids, games, live_counts, cw, nm, table):
     count, strip, breadth, _ = frames.shape
     half, rows, cols = count // 2, strip // 2, breadth // 2
     fine = (count, rows + 4, cols, 512)
@@ -1041,26 +1218,38 @@
         VM((5, 2, half, cols, 128), BF16),
         VM((2, count, cols, 128), BF16),
         VM((2, count, cols, 128), BF16),
-        pltpu.SemaphoreType.DMA((2,)),
+        VM((4, 256, 128), F32),
+        VM((4, 128), F32),
+        VM((32 // nd, nd, 64, 128), BF16),
+        VM((nd, 32 // nd, 64, 128), BF16),
+        VM((n, 32 // nd, 64 // n, 128), F32),
+        VM((n, 32 // nd, 64 // n, 128), F32),
+        VM((n, 32 // nd, 64 // n, 128), F32),
+        VM((nd, 32 // nd, 64, 128), BF16),
+        pltpu.SemaphoreType.DMA((7,)),
         pltpu.SemaphoreType.DMA((count,)),
         pltpu.SemaphoreType.DMA((2,)),
         pltpu.SemaphoreType.DMA((8, n - 1)),
         pltpu.SemaphoreType.DMA((8, n - 1)),
         pltpu.SemaphoreType.DMA((8, 2)),
         pltpu.SemaphoreType.DMA((8, 2)),
+        pltpu.SemaphoreType.DMA((4, 2, nd - 1)),
+        pltpu.SemaphoreType.DMA((4, 2, nd - 1)),
+        pltpu.SemaphoreType.DMA((3, 2, n - 1)),
+        pltpu.SemaphoreType.DMA((3, 2, n - 1)),
     ]
     smem = pl.BlockSpec(memory_space=pltpu.SMEM)
     vmem = pl.BlockSpec(memory_space=pltpu.VMEM)
     hbm = pl.BlockSpec(memory_space=pl.ANY)
     return pl.pallas_call(
-        functools.partial(step_kernel, n),
+        functools.partial(step_kernel, nd, n),
         out_shape=(
             jax.ShapeDtypeStruct(frames.shape, BF16),
             jax.ShapeDtypeStruct(frames.shape, F32),
-            jax.ShapeDtypeStruct((32, 64, 128), BF16),
-            jax.ShapeDtypeStruct((count, 896), F32),
+            jax.ShapeDtypeStruct((64, 4096), BF16),
+            jax.ShapeDtypeStruct((nd, count, 896), F32),
         ),
-        in_specs=[hbm, hbm, smem, smem, smem, smem, vmem, vmem, vmem],
+        in_specs=[hbm, hbm, smem, smem, smem, smem, vmem, hbm, vmem],
         out_specs=(hbm, hbm, vmem, vmem),
         scratch_shapes=scratch,
         compiler_params=pltpu.CompilerParams(
@@ -1079,114 +1268,6 @@
     fixed_v = square_new / fix_two
     weight_new = weight - rate * (fixed_m / (jnp.sqrt(fixed_v) + ADAM_EPS) + DECAY * weight)
     return (moment_new, square_new, weight_new, weight_new.astype(BF16))
-
-
-def reduce_kernel(
-    nd, ns, gt, pk, out, packs, rbuf, part, zbuf, own, sem_a, sem_b, sem_c, sem_d, sem_p, bar_unused
-):
-    dp = lax.axis_index("dp")
-    sp = lax.axis_index("space")
-    barrier = pltpu.get_barrier_semaphore()
-    for off in range(1, nd):
-        pl.semaphore_signal(
-            barrier, inc=1, device_id={"dp": lax.rem(dp + off, nd)}, device_id_type=MESH
-        )
-    for off in range(1, ns):
-        pl.semaphore_signal(
-            barrier, inc=1, device_id={"space": lax.rem(sp + off, ns)}, device_id_type=MESH
-        )
-    pl.semaphore_wait(barrier, nd + ns - 2)
-
-    def copy(src, dst, sems, off, axis):
-        here, size = (dp, nd) if axis == "dp" else (sp, ns)
-        return pltpu.make_async_remote_copy(
-            src_ref=src,
-            dst_ref=dst,
-            send_sem=sems.at[0, off - 1],
-            recv_sem=sems.at[1, off - 1],
-            device_id={axis: lax.rem(here + off, size)},
-            device_id_type=MESH,
-        )
-
-    def before(off, axis):
-        here, size = (dp, nd) if axis == "dp" else (sp, ns)
-        return lax.rem(here + size - off, size)
-
-    def after(off, axis):
-        here, size = (dp, nd) if axis == "dp" else (sp, ns)
-        return lax.rem(here + off, size)
-
-    packs[dp] = pk[...]
-    for off in range(1, nd):
-        copy(gt.at[after(off, "dp")], rbuf.at[dp], sem_a, off, "dp").start()
-    for off in range(1, nd):
-        copy(packs.at[dp], packs.at[dp], sem_p, off, "dp").start()
-    rbuf[dp] = gt[dp]
-    for off in range(1, nd):
-        copy(gt.at[0], rbuf.at[before(off, "dp")], sem_a, off, "dp").wait_recv()
-    total = rbuf[0].astype(F32)
-    for i in range(1, nd):
-        total = total + rbuf[i].astype(F32)
-    part[...] = total
-    for off in range(1, ns):
-        copy(part.at[after(off, "space")], zbuf.at[sp], sem_b, off, "space").start()
-    zbuf[sp] = part[sp]
-    for off in range(1, ns):
-        copy(part.at[0], zbuf.at[before(off, "space")], sem_b, off, "space").wait_recv()
-    total = zbuf[0]
-    for i in range(1, ns):
-        total = total + zbuf[i]
-    out[dp, sp] = total.astype(BF16)
-    for off in range(1, ns):
-        copy(out.at[dp, sp], out.at[dp, sp], sem_c, off, "space").start()
-    for off in range(1, ns):
-        slot = before(off, "space")
-        copy(out.at[dp, slot], out.at[dp, slot], sem_c, off, "space").wait_recv()
-    for off in range(1, nd):
-        copy(out.at[dp], out.at[dp], sem_d, off, "dp").start()
-    for off in range(1, nd):
-        slot = before(off, "dp")
-        copy(out.at[slot], out.at[slot], sem_d, off, "dp").wait_recv()
-        copy(packs.at[slot], packs.at[slot], sem_p, off, "dp").wait_recv()
-    for off in range(1, nd):
-        copy(gt.at[0], rbuf.at[dp], sem_a, off, "dp").wait_send()
-        copy(packs.at[dp], packs.at[dp], sem_p, off, "dp").wait_send()
-        copy(out.at[dp], out.at[dp], sem_d, off, "dp").wait_send()
-    for off in range(1, ns):
-        copy(part.at[0], zbuf.at[sp], sem_b, off, "space").wait_send()
-        copy(out.at[dp, sp], out.at[dp, sp], sem_c, off, "space").wait_send()
-
-
-def run_reduce(nd, ns, gt, pack):
-    rpd = 2048 // (nd * ns)
-    shape = (nd, ns, rpd, 128)
-    vmem = pl.BlockSpec(memory_space=pltpu.VMEM)
-    sems = lambda k: pltpu.SemaphoreType.DMA((2, k - 1))
-    return pl.pallas_call(
-        functools.partial(reduce_kernel, nd, ns),
-        out_shape=(
-            jax.ShapeDtypeStruct(shape, BF16),
-            jax.ShapeDtypeStruct((nd,) + pack.shape, F32),
-        ),
-        in_specs=[vmem, vmem],
-        out_specs=(vmem, vmem),
-        scratch_shapes=[
-            VM(shape, BF16),
-            VM(shape[1:], F32),
-            VM(shape[1:], F32),
-            VM(shape[2:], F32),
-            sems(nd),
-            sems(ns),
-            sems(ns),
-            sems(nd),
-            sems(nd),
-            pltpu.SemaphoreType.REGULAR,
-        ],
-        compiler_params=pltpu.CompilerParams(
-            collective_id=1, has_side_effects=True, vmem_limit_bytes=32 * 1024 * 1024
-        ),
-        name="reduce",
-    )(gt.reshape(shape), pack)
 
 
 def local(
@@ -1209,15 +1290,11 @@
     table_square,
 ):
     cw = conv_weight.T
-    nm = jnp.transpose(norm_map, (1, 0, 2)).reshape(-1, 128)
-    result, frames_grad, gt, pack = run_step(
-        ns, frames, cotangent, actions, noise_ids, games, live_counts, cw, nm, emb_table
+    nm = jnp.transpose(norm_map, (1, 0, 2))
+    result, frames_grad, grads, packs = run_step(
+        nd, ns, frames, cotangent, actions, noise_ids, games, live_counts, cw, nm, emb_table
     )
-    grads, packs = run_reduce(nd, ns, gt, pack)
-    conv_rows = conv_weight.shape[0]
-    grad_t = (
-        grads.reshape(32, 64, 128).transpose(1, 0, 2).reshape(64, 4096)[:, :conv_rows].astype(F32)
-    )
+    grad_t = grads[:, : conv_weight.shape[0]].astype(F32)
     conv_out = [v.T for v in adamw(cw, conv_moment.T, conv_square.T, grad_t, 0.05)]
     packs = packs.reshape(-1, 896)
     dmods = packs[:, 0:512]

time: 129 us -> 110 us (0.85)
  Pallas kernels: 109 us -> 93.9 us
  local copies, waits for them, and re-layouts: 9.59 us -> 5.69 us
    pallas_call x2 -> x1, Pallas kernels: 109 us -> 93.9 us  [run_step(): pl.pallas_call(functools.partial(step_kernel, nd, n), out_shape=(jax.Shap...]
    reshape x2 -> x0, local copies, waits for them, and re-layouts: 2.11 us -> none  [the longest x1 2.02 us: local(): nm = jnp.transpose(norm_map, (1, 0, 2)).reshape(-1, 128)]
    unnamed x26 -> x22, local copies, waits for them, and re-layouts: 7.27 us -> 5.47 us
where the time goes in v2:
time: 110 us
  Pallas kernels  93.9 us (85%)
  other arithmetic  6.48 us (6%)
  local copies, waits for them, and re-layouts  5.69 us (5%)
  matrix products  2.34 us (2%)
  between operations  1.39 us (1%)
    pallas_call x1, Pallas kernels, run_step(): pl.pallas_call(functools.partial(step_kernel, nd, n), out_shape=(jax.Shap...  93.9 us
    unnamed x22, local copies, waits for them, and re-layouts  5.47 us
    transpose x1, other arithmetic, local(): conv_out = [v.T for v in adamw(cw, conv_moment.T, conv_square.T, grad_t,...  4.36 us

profile of v2, /device:TPU:0, one launch (start us, length us, event | category | flops | bytes accessed | tf_op | source)
XLA Modules:
  0.0 109.8 jit_solution(1076955830890694797)
XLA Ops:
  1.3 0.0 copy-start.1
  1.3 93.9 %step.1 = (bf16[8,16,64,64]{3,2,1,0:T(8,128)(2,1)}, f32[8,16,64,64]{3,2,1,0:T(8,128)}, bf16[64,4096]{1,0:T(8,128)(2,1)}, f32[8,8,896]{2,1,0:T(8,128)}) custom-call(bf16[8,16,64,64]{3,2,1,0:T(8,128)(2,1)} %x_hbm.1, bf16[8,16,64,64]{3,2,1,0:T(8,128)(2,1)} %cot_hbm.1, s32[8]{0:T(128)} %act_ref.1, s32[8]{0:T(128)} %noise_ref.1, s32[8]{0:T(128)} %game_ref.1, ...), custom_call_target="tpu_custom_call" | custom-call | tf_op jit(solution)/shard_map/step/pallas_call | solution.py:1244
  95.3 0.0 copy-done.1
  95.3 0.0 copy-start.4
  95.3 4.4 %convert_bitcast_fusion = (bf16[4032,64]{0,1:T(8,128)(2,1)}, f32[64,4032]{1,0:T(8,128)}, f32[4032,64]{0,1:T(8,128)}, f32[4032,64]{0,1:T(8,128)}) fusion(f32[4032,64]{0,1:T(8,128)} %param.23, bf16[64,4096]{1,0:T(8,128)(2,1)} %get-tuple-element.20, f32[4032,64]{0,1:T(8,128)} %param.22, f32[4032,64]{0,1:T(8,128)S(1)} %copy-done.1), kind=kLoop, calls=%fused_computation.14 | loop fusion | flops 4128768 | bytes 7225344 | tf_op jit(solution)/shard_map/transpose | solution.py:1298
  99.6 0.0 copy-start
  99.6 0.0 copy-start.5
  99.6 0.0 copy-start.6
  99.6 0.0 copy-done.4
  99.7 0.6 fusion.8
  100.3 0.2 reshape.41
  100.5 0.2 copy-done
  100.7 0.2 copy-done.5
  100.8 0.2 copy-done.6
  101.0 0.0 copy-start.7
  101.0 0.0 copy-start.8
  101.0 0.0 copy-start.9
  101.0 2.1 %fusion.16 = (bf16[4,257,128]{2,0,1:T(4,128)(2,1)}, f32[4,257,128]{2,0,1:T(4,128)}, f32[4,257,128]{2,0,1:T(4,128)}, f32[4,257,128]{2,0,1:T(4,128)}) fusion(f32[4,257,128]{2,0,1:T(4,128)S(1)} %copy-done, f32[1,4,128]{2,1,0:T(4,128)S(1)} %bitcast.51, f32[256,4,128]{2,1,0:T(4,128)S(1)} %reshape.41, f32[4,257,128]{2,0,1:T(4,128)S(1)} %copy-done.5, ...), kind=kLoop, calls=%fused_computation.27 | loop fusion | flops 2105344 | bytes 3947520 | tf_op jit(solution)/shard_map/convert_element_type | solution.py:1270
  103.1 0.0 copy-start.3
  103.1 0.6 fusion.4
  103.7 0.0 copy-done.7
  103.7 0.0 copy-done.8
  103.8 0.0 copy-done.9
  103.8 1.1 %fusion.14 = (bf16[108,256]{1,0:T(8,128)(2,1)}, f32[108,256]{1,0:T(8,128)}, f32[108,256]{1,0:T(8,128)}, f32[108,256]{1,0:T(8,128)}) fusion(f32[108,256]{1,0:T(8,128)S(1)} %copy-done.7, f32[108,256]{1,0:T(8,128)S(1)} %copy-done.8, f32[108,256]{1,0:T(8,128)S(1)} %copy-done.9, f32[64,256]{1,0:T(8,128)S(1)} %fusion.4, f32[64,896]{1,0:T(8,128)S(1)} %bitcast.49), kind=kOutput, calls=%fused_computation.26 | convolution fusion | flops 21648384 | bytes 829440 | tf_op jit(solution)/shard_map/dot_general | solution.py:1310
  104.9 0.0 copy-done.3
  104.9 0.0 copy-start.2
  104.9 1.3 %copy.37 = bf16[8,16,64,64]{3,2,1,0:T(8,128)(2,1)} copy(bf16[8,16,64,64]{3,2,1,0:T(8,128)(2,1)S(1)} %copy-done.3) | data formatting | bytes 2097152
  106.2 1.6 %copy-done.2 = f32[8,16,64,64]{3,2,1,0:T(8,128)S(1)} copy-done((f32[8,16,64,64]{3,2,1,0:T(8,128)S(1)}, f32[8,16,64,64]{3,2,1,0:T(8,128)}, u32[]{:S(2)}) %copy-start.2) | copy-done | bytes 2097176
  107.8 2.0 %copy.38 = f32[8,16,64,64]{3,2,1,0:T(8,128)} copy(f32[8,16,64,64]{3,2,1,0:T(8,128)S(1)} %copy-done.2) | data formatting | bytes 4194304
  (2 shorter events, 0.1 us)
Async XLA Ops:
  1.3 94.0 %copy-start.1 = (f32[4032,64]{0,1:T(8,128)S(1)}, f32[4032,64]{0,1:T(8,128)}, u32[]{:S(2)}) copy-start(f32[4032,64]{0,1:T(8,128)} %param.21) | copy-start | bytes 3096580
  95.3 4.4 %copy-start.4 = (f32[8,8,896]{2,1,0:T(8,128)S(1)}, f32[8,8,896]{2,1,0:T(8,128)}, u32[]{:S(2)}) copy-start(f32[8,8,896]{2,1,0:T(8,128)} %get-tuple-element.21) | copy-start | bytes 688132
  99.6 1.0 copy-start
  99.6 1.2 %copy-start.5 = (f32[4,257,128]{2,0,1:T(4,128)S(1)}, f32[4,257,128]{2,0,1:T(4,128)}, u32[]{:S(2)}) copy-start(f32[4,257,128]{2,0,1:T(4,128)} %param.26) | copy-start | bytes 1579012
  99.6 1.4 %copy-start.6 = (f32[4,257,128]{2,0,1:T(4,128)S(1)}, f32[4,257,128]{2,0,1:T(4,128)}, u32[]{:S(2)}) copy-start(f32[4,257,128]{2,0,1:T(4,128)} %param.25) | copy-start | bytes 1579012
  101.0 2.7 %copy-start.7 = (f32[108,256]{1,0:T(8,128)S(1)}, f32[108,256]{1,0:T(8,128)}, u32[]{:S(2)}) copy-start(f32[108,256]{1,0:T(8,128)} %tab_ref.1) | copy-start | bytes 331780
  101.0 2.8 %copy-start.8 = (f32[108,256]{1,0:T(8,128)S(1)}, f32[108,256]{1,0:T(8,128)}, u32[]{:S(2)}) copy-start(f32[108,256]{1,0:T(8,128)} %param.29) | copy-start | bytes 331780
  101.0 2.8 %copy-start.9 = (f32[108,256]{1,0:T(8,128)S(1)}, f32[108,256]{1,0:T(8,128)}, u32[]{:S(2)}) copy-start(f32[108,256]{1,0:T(8,128)} %param.28) | copy-start | bytes 331780
  103.1 1.8 %copy-start.3 = (bf16[8,16,64,64]{3,2,1,0:T(8,128)(2,1)S(1)}, bf16[8,16,64,64]{3,2,1,0:T(8,128)(2,1)}, u32[]{:S(2)}) copy-start(bf16[8,16,64,64]{3,2,1,0:T(8,128)(2,1)} %get-tuple-element.48) | copy-start | bytes 3145732
  104.9 2.9 %copy-start.2 = (f32[8,16,64,64]{3,2,1,0:T(8,128)S(1)}, f32[8,16,64,64]{3,2,1,0:T(8,128)}, u32[]{:S(2)}) copy-start(f32[8,16,64,64]{3,2,1,0:T(8,128)} %get-tuple-element.49) | copy-start | bytes 6291460

commit v3 on v2

--- a/solution.py
+++ b/solution.py
@@ -558,7 +558,7 @@
         return put_row(total, f, full_sum(both)), put_row(square, f, full_sum(both * both))
 
     zero_rows = jnp.zeros((frames, 128), F32)
-    sums = lax.fori_loop(0, frames, load_x, (zero_rows, zero_rows))
+    sums = lax.fori_loop(0, frames, load_x, (zero_rows, zero_rows), unroll=4)
     stat_start(0, jnp.concatenate(sums, axis=0))
     g_copy = pltpu.make_async_copy(cot_hbm, raw, local_sem.at[1])
     g_copy.start()
@@ -728,7 +728,7 @@
         xs[f, rows + 3] = jnp.concatenate([low[2:3], zero], axis=-1)[0].astype(BF16)
         return carry
 
-    lax.fori_loop(0, frames, load_x_halo, 0)
+    lax.fori_loop(0, frames, load_x_halo, 0, unroll=4)
     norm_forward(0, stat_total(0), False)
 
     def first_layer(f, carry):
@@ -743,7 +743,7 @@
         own = out[1 : rows + 1]
         return put_row(total, f, full_sum(own)), put_row(square, f, full_sum(own * own))
 
-    sums = lax.fori_loop(0, frames, first_layer, (zero_rows, zero_rows))
+    sums = lax.fori_loop(0, frames, first_layer, (zero_rows, zero_rows), unroll=4)
     stat_start(1, jnp.concatenate(sums, axis=0))
 
     g_copy.wait()
@@ -771,7 +771,7 @@
         gsa[f] = dot_nn(window(eg, f, 1, rows + 2), wsb[...]).reshape(rows + 2, cols, 256)
         return carry
 
-    lax.fori_loop(0, frames, load_g, 0)
+    lax.fori_loop(0, frames, load_g, 0, unroll=4)
 
     norm_forward(1, stat_total(1), False)
 
@@ -789,7 +789,7 @@
         put_e(esk, f, 1, skip)
         return carry
 
-    lax.fori_loop(0, frames, second_layer, 0)
+    lax.fori_loop(0, frames, second_layer, 0, unroll=4)
 
     def down_window(f):
         return jnp.concatenate(
@@ -809,7 +809,7 @@
         border(hout, 1, hf, d)
         return put_row(total, hf, coarse_sum(d)), put_row(square, hf, coarse_sum(d * d))
 
-    sums = lax.fori_loop(0, half, down_layer, (zero_coarse, zero_coarse))
+    sums = lax.fori_loop(0, half, down_layer, (zero_coarse, zero_coarse), unroll=4)
     stat_start(2, jnp.concatenate(list(sums) + pad_rows, axis=0))
     halo_start(d_halo)
 
@@ -826,7 +826,7 @@
         border(hout, 0, hf, back)
         return carry
 
-    lax.fori_loop(0, half, coarse_gradient, 0)
+    lax.fori_loop(0, half, coarse_gradient, 0, unroll=4)
     halo_start(g_h4_halo)
 
     def put_half(index, value):
@@ -845,7 +845,7 @@
             acc[0, :, 0:1024] += dot_tn(g, window(e, f, start, rows))
             return carry
 
-        lax.fori_loop(0, frames, add, 0)
+        lax.fori_loop(0, frames, add, 0, unroll=4)
         for t in range(3):
             u = []
             for dq in range(2):
@@ -867,7 +867,7 @@
             acc[0, 0:128, :] += dot_tn(g, coarse_window(ec, hf))
             return carry
 
-        lax.fori_loop(0, half, add, 0)
+        lax.fori_loop(0, half, add, 0, unroll=4)
         for a in range(3):
             for j in range(3):
                 lanes = pl.ds((a * 3 + j) * 128, 128)
@@ -882,7 +882,7 @@
             acc[1, 0:128, 0:768] += dot_tn(g, down_window(hf + half))
             return carry
 
-        lax.fori_loop(0, half, add, 0)
+        lax.fori_loop(0, half, add, 0, unroll=4)
         for a in range(3):
             near = acc[0, 0:64, pl.ds(a * 256, 128)] + acc[1, 64:128, pl.ds(a * 256, 128)]
             far = (
@@ -901,7 +901,7 @@
             acc[1] += dot_tn(own_pixels(eg, hf + half, 2, rows), v)
             return carry
 
-        lax.fori_loop(0, half, add, 0)
+        lax.fori_loop(0, half, add, 0, unroll=4)
 
         def block(dr, dq, i, j):
             r = (dr * 2 + dq) * 64
@@ -933,7 +933,7 @@
         border(hout, 2, hf, out)
         return put_row(total, hf, coarse_sum(out)), put_row(square, hf, coarse_sum(out * out))
 
-    sums = lax.fori_loop(0, half, third_layer, (zero_coarse, zero_coarse))
+    sums = lax.fori_loop(0, half, third_layer, (zero_coarse, zero_coarse), unroll=4)
     stat_start(3, jnp.concatenate(list(sums) + pad_rows, axis=0))
     halo_start(c3_halo)
     fine_kernel_grad(lambda t, s: 45 + (t * 3 + s) * 2, esk, 2, eg, 2)
@@ -957,7 +957,7 @@
         xhat = v[1 : rows + 1] * param(3, RSTD, hf) + param(3, NMR, hf)
         return put_row(shift, hf, coarse_sum(own)), put_row(scale, hf, coarse_sum(own * xhat))
 
-    sums = lax.fori_loop(0, half, fourth_layer, (zero_coarse, zero_coarse))
+    sums = lax.fori_loop(0, half, fourth_layer, (zero_coarse, zero_coarse), unroll=4)
     stat_start(4, jnp.concatenate(list(sums) + pad_rows, axis=0))
 
     def coarse_output(hf, carry):
@@ -968,7 +968,7 @@
         put_ec(ecy, hf, jnp.concatenate([edge, y, edge], axis=0))
         return carry
 
-    lax.fori_loop(0, half, coarse_output, 0)
+    lax.fori_loop(0, half, coarse_output, 0, unroll=4)
     halo_start(y_halo)
     coarse_kernel_grad(stacked(4), ec4, ecg)
 
@@ -992,7 +992,7 @@
         xhat = v * param(2, RSTD, hf) + param(2, NMR, hf)
         return put_row(shift, hf, coarse_sum(own)), put_row(scale, hf, coarse_sum(own * xhat))
 
-    sums = lax.fori_loop(0, half, third_back, (zero_coarse, zero_coarse))
+    sums = lax.fori_loop(0, half, third_back, (zero_coarse, zero_coarse), unroll=4)
     stat_start(5, jnp.concatenate(list(sums) + pad_rows, axis=0))
     halo_start(g_h3_halo)
 
@@ -1025,7 +1025,7 @@
             result_copy(f).start()
         return carry
 
-    lax.fori_loop(0, half, merge, 0)
+    lax.fori_loop(0, half, merge, 0, unroll=4)
     coarse_kernel_grad(stacked(3), ec3, ecg3)
     up_kernel_grad()
     gather_start(0)
@@ -1061,7 +1061,7 @@
             put_e(eg2, f, 0, jnp.where(block_mask(total.shape, 1), total, 0.0))
         return carry
 
-    lax.fori_loop(0, half, down_back, 0)
+    lax.fori_loop(0, half, down_back, 0, unroll=4)
 
     def second_back(f, carry):
         shift, scale = carry
@@ -1076,7 +1076,7 @@
         xhat = v * wide(1, RSTD, f) + wide(1, NMR, f)
         return put_row(shift, f, full_sum(own)), put_row(scale, f, full_sum(own * xhat))
 
-    sums = lax.fori_loop(0, frames, second_back, (zero_rows, zero_rows))
+    sums = lax.fori_loop(0, frames, second_back, (zero_rows, zero_rows), unroll=4)
     stat_start(6, jnp.concatenate(sums, axis=0))
     halo_start(g_h2_halo)
     down_kernel_grad(stacked(2))
@@ -1108,7 +1108,7 @@
         return put_row(shift, f, full_sum(own)), put_row(scale, f, full_sum(own * xhat))
 
     pack_start(0)
-    sums = lax.fori_loop(0, frames, first_back, (zero_rows, zero_rows))
+    sums = lax.fori_loop(0, frames, first_back, (zero_rows, zero_rows), unroll=4)
     stat_start(7, jnp.concatenate(sums, axis=0))
     gather_spread(0)
     gather_space(1)
@@ -1140,7 +1140,7 @@
         frames_copy(f).start()
         return carry
 
-    lax.fori_loop(0, frames, frames_back, 0)
+    lax.fori_loop(0, frames, frames_back, 0, unroll=4)
     gather_space(2)
     gather_all(1)
     gather_spread(2)

time: 110 us -> 103 us (0.936)
  Pallas kernels: 93.9 us -> 86.7 us
    pallas_call x1, Pallas kernels: 93.9 us -> 86.7 us  [run_step(): pl.pallas_call(functools.partial(step_kernel, nd, n), out_shape=(jax.Shap...]
where the time goes in v3:
time: 103 us
  Pallas kernels  86.7 us (84%)
  other arithmetic  6.48 us (6%)
  local copies, waits for them, and re-layouts  5.69 us (6%)
  matrix products  2.33 us (2%)
  between operations  1.39 us (1%)
    pallas_call x1, Pallas kernels, run_step(): pl.pallas_call(functools.partial(step_kernel, nd, n), out_shape=(jax.Shap...  86.7 us
    unnamed x22, local copies, waits for them, and re-layouts  5.47 us
    transpose x1, other arithmetic, local(): conv_out = [v.T for v in adamw(cw, conv_moment.T, conv_square.T, grad_t,...  4.36 us
    convert_element_type x1, other arithmetic, adamw(): return (moment_new, square_new, weight_new, weight_new.astype(BF16))  2.09 us

profile of v3, /device:TPU:0, one launch (start us, length us, event | category | flops | bytes accessed | tf_op | source)
XLA Modules:
  0.0 102.6 jit_solution(2471996859332964222)
XLA Ops:
  1.3 0.0 copy-start.1
  1.3 86.7 %step.1 = (bf16[8,16,64,64]{3,2,1,0:T(8,128)(2,1)}, f32[8,16,64,64]{3,2,1,0:T(8,128)}, bf16[64,4096]{1,0:T(8,128)(2,1)}, f32[8,8,896]{2,1,0:T(8,128)}) custom-call(bf16[8,16,64,64]{3,2,1,0:T(8,128)(2,1)} %x_hbm.1, bf16[8,16,64,64]{3,2,1,0:T(8,128)(2,1)} %cot_hbm.1, s32[8]{0:T(128)} %act_ref.1, s32[8]{0:T(128)} %noise_ref.1, s32[8]{0:T(128)} %game_ref.1, ...), custom_call_target="tpu_custom_call" | custom-call | tf_op jit(solution)/shard_map/step/pallas_call | solution.py:1244
  88.0 0.0 copy-done.1
  88.0 0.0 copy-start.4
  88.0 4.4 %convert_bitcast_fusion = (bf16[4032,64]{0,1:T(8,128)(2,1)}, f32[64,4032]{1,0:T(8,128)}, f32[4032,64]{0,1:T(8,128)}, f32[4032,64]{0,1:T(8,128)}) fusion(f32[4032,64]{0,1:T(8,128)} %param.23, bf16[64,4096]{1,0:T(8,128)(2,1)} %get-tuple-element.20, f32[4032,64]{0,1:T(8,128)} %param.22, f32[4032,64]{0,1:T(8,128)S(1)} %copy-done.1), kind=kLoop, calls=%fused_computation.14 | loop fusion | flops 4128768 | bytes 7225344 | tf_op jit(solution)/shard_map/transpose | solution.py:1298
  92.4 0.0 copy-start
  92.4 0.0 copy-start.5
  92.4 0.0 copy-start.6
  92.4 0.0 copy-done.4
  92.5 0.6 fusion.8
  93.1 0.2 reshape.41
  93.3 0.2 copy-done
  93.5 0.2 copy-done.5
  93.6 0.2 copy-done.6
  93.8 0.0 copy-start.7
  93.8 0.0 copy-start.8
  93.8 0.0 copy-start.9
  93.8 2.1 %fusion.16 = (bf16[4,257,128]{2,0,1:T(4,128)(2,1)}, f32[4,257,128]{2,0,1:T(4,128)}, f32[4,257,128]{2,0,1:T(4,128)}, f32[4,257,128]{2,0,1:T(4,128)}) fusion(f32[4,257,128]{2,0,1:T(4,128)S(1)} %copy-done, f32[1,4,128]{2,1,0:T(4,128)S(1)} %bitcast.51, f32[256,4,128]{2,1,0:T(4,128)S(1)} %reshape.41, f32[4,257,128]{2,0,1:T(4,128)S(1)} %copy-done.5, ...), kind=kLoop, calls=%fused_computation.27 | loop fusion | flops 2105344 | bytes 3947520 | tf_op jit(solution)/shard_map/convert_element_type | solution.py:1270
  95.9 0.0 copy-start.3
  95.9 0.6 fusion.4
  96.5 0.0 copy-done.7
  96.5 0.0 copy-done.8
  96.5 0.0 copy-done.9
  96.5 1.1 %fusion.14 = (bf16[108,256]{1,0:T(8,128)(2,1)}, f32[108,256]{1,0:T(8,128)}, f32[108,256]{1,0:T(8,128)}, f32[108,256]{1,0:T(8,128)}) fusion(f32[108,256]{1,0:T(8,128)S(1)} %copy-done.7, f32[108,256]{1,0:T(8,128)S(1)} %copy-done.8, f32[108,256]{1,0:T(8,128)S(1)} %copy-done.9, f32[64,256]{1,0:T(8,128)S(1)} %fusion.4, f32[64,896]{1,0:T(8,128)S(1)} %bitcast.49), kind=kOutput, calls=%fused_computation.26 | convolution fusion | flops 21648384 | bytes 829440 | tf_op jit(solution)/shard_map/dot_general | solution.py:1310
  97.7 0.0 copy-done.3
  97.7 0.0 copy-start.2
  97.7 1.3 %copy.37 = bf16[8,16,64,64]{3,2,1,0:T(8,128)(2,1)} copy(bf16[8,16,64,64]{3,2,1,0:T(8,128)(2,1)S(1)} %copy-done.3) | data formatting | bytes 2097152
  99.0 1.6 %copy-done.2 = f32[8,16,64,64]{3,2,1,0:T(8,128)S(1)} copy-done((f32[8,16,64,64]{3,2,1,0:T(8,128)S(1)}, f32[8,16,64,64]{3,2,1,0:T(8,128)}, u32[]{:S(2)}) %copy-start.2) | copy-done | bytes 2097176
  100.6 2.0 %copy.38 = f32[8,16,64,64]{3,2,1,0:T(8,128)} copy(f32[8,16,64,64]{3,2,1,0:T(8,128)S(1)} %copy-done.2) | data formatting | bytes 4194304
  (2 shorter events, 0.1 us)
Async XLA Ops:
  1.3 86.7 %copy-start.1 = (f32[4032,64]{0,1:T(8,128)S(1)}, f32[4032,64]{0,1:T(8,128)}, u32[]{:S(2)}) copy-start(f32[4032,64]{0,1:T(8,128)} %param.21) | copy-start | bytes 3096580
  88.0 4.4 %copy-start.4 = (f32[8,8,896]{2,1,0:T(8,128)S(1)}, f32[8,8,896]{2,1,0:T(8,128)}, u32[]{:S(2)}) copy-start(f32[8,8,896]{2,1,0:T(8,128)} %get-tuple-element.21) | copy-start | bytes 688132
  92.4 1.0 %copy-start = (f32[4,257,128]{2,0,1:T(4,128)S(1)}, f32[4,257,128]{2,0,1:T(4,128)}, u32[]{:S(2)}) copy-start(f32[4,257,128]{2,0,1:T(4,128)} %param.24) | copy-start | bytes 1579012
  92.4 1.2 %copy-start.5 = (f32[4,257,128]{2,0,1:T(4,128)S(1)}, f32[4,257,128]{2,0,1:T(4,128)}, u32[]{:S(2)}) copy-start(f32[4,257,128]{2,0,1:T(4,128)} %param.26) | copy-start | bytes 1579012
  92.4 1.4 %copy-start.6 = (f32[4,257,128]{2,0,1:T(4,128)S(1)}, f32[4,257,128]{2,0,1:T(4,128)}, u32[]{:S(2)}) copy-start(f32[4,257,128]{2,0,1:T(4,128)} %param.25) | copy-start | bytes 1579012
  93.8 2.7 %copy-start.7 = (f32[108,256]{1,0:T(8,128)S(1)}, f32[108,256]{1,0:T(8,128)}, u32[]{:S(2)}) copy-start(f32[108,256]{1,0:T(8,128)} %tab_ref.1) | copy-start | bytes 331780
  93.8 2.8 %copy-start.8 = (f32[108,256]{1,0:T(8,128)S(1)}, f32[108,256]{1,0:T(8,128)}, u32[]{:S(2)}) copy-start(f32[108,256]{1,0:T(8,128)} %param.29) | copy-start | bytes 331780
  93.8 2.8 %copy-start.9 = (f32[108,256]{1,0:T(8,128)S(1)}, f32[108,256]{1,0:T(8,128)}, u32[]{:S(2)}) copy-start(f32[108,256]{1,0:T(8,128)} %param.28) | copy-start | bytes 331780
  95.9 1.8 %copy-start.3 = (bf16[8,16,64,64]{3,2,1,0:T(8,128)(2,1)S(1)}, bf16[8,16,64,64]{3,2,1,0:T(8,128)(2,1)}, u32[]{:S(2)}) copy-start(bf16[8,16,64,64]{3,2,1,0:T(8,128)(2,1)} %get-tuple-element.48) | copy-start | bytes 3145732
  97.7 2.9 %copy-start.2 = (f32[8,16,64,64]{3,2,1,0:T(8,128)S(1)}, f32[8,16,64,64]{3,2,1,0:T(8,128)}, u32[]{:S(2)}) copy-start(f32[8,16,64,64]{3,2,1,0:T(8,128)} %get-tuple-element.49) | copy-start | bytes 6291460

commit v4 on v3

--- a/solution.py
+++ b/solution.py
@@ -74,28 +74,23 @@
     cw_ref,
     nm_hbm,
     tab_ref,
-    res_hbm,
-    fg_hbm,
-    gout_ref,
-    packs,
+    io_hbm,
+    par_hbm,
     raw,
-    xh,
     tmp,
-    fst,
     xs,
+    gs,
     e1,
     e2,
     esk,
     eg,
-    eg2,
     c1,
     gsa,
     gz,
     dv,
     c3,
     gh4,
-    gz4,
-    gz3,
+    gzc,
     gco,
     ec3,
     ec4,
@@ -133,6 +128,7 @@
     zbuf,
     zfull,
     gall,
+    packs,
     local_sem,
     out_sem,
     fg_sem,
@@ -157,6 +153,17 @@
     owned = rows * cols
     ext = (rows + 2) * cols
 
+    x_copy = pltpu.make_async_copy(x_hbm, raw, local_sem.at[0])
+    x_copy.start()
+    g_copy = pltpu.make_async_copy(cot_hbm, raw, local_sem.at[1])
+    map_copies = [
+        pltpu.make_async_copy(nm_hbm.at[pl.ds(0, 256), k], nmv.at[k], local_sem.at[2 + k])
+        for k in range(4)
+    ]
+    map_copies.append(pltpu.make_async_copy(nm_hbm.at[256], nmb, local_sem.at[6]))
+    for copy in map_copies:
+        copy.start()
+
     barrier = pltpu.get_barrier_semaphore()
     for off in range(1, n):
         pl.semaphore_signal(
@@ -172,17 +179,6 @@
             device_id={"dp": lax.rem(dp + off, nd)},
             device_id_type=MESH,
         )
-
-    x_copy = pltpu.make_async_copy(x_hbm, raw, local_sem.at[0])
-    x_copy.start()
-    map_copies = [
-        pltpu.make_async_copy(nm_hbm.at[pl.ds(0, 256), k], nmv.at[k], local_sem.at[2 + k])
-        for k in range(4)
-    ]
-    map_copies.append(pltpu.make_async_copy(nm_hbm.at[256], nmb, local_sem.at[6]))
-    for copy in map_copies:
-        copy.start()
-    pl.semaphore_wait(barrier, n + nd - 2)
 
     def halo_copies(k, first, last, to_up, to_down):
         up = pltpu.make_async_remote_copy(
@@ -255,23 +251,21 @@
             stat_copy(k, off, me).wait_send()
         return total
 
-    x_halo = halo_copies(
-        0, x_hbm.at[:, pl.ds(0, 3)], x_hbm.at[:, pl.ds(strip - 3, 3)], xh.at[0, 1], xh.at[0, 0]
-    )
-    g_halo = halo_copies(
-        1, cot_hbm.at[:, pl.ds(0, 3)], cot_hbm.at[:, pl.ds(strip - 3, 3)], xh.at[1, 1], xh.at[1, 0]
-    )
-    for side in range(2):
-
-        @pl.when((me == 0) if side == 0 else (me == n - 1))
-        def _():
-            for which in range(2):
-                xh[which, side] = jnp.zeros(xh.shape[2:], BF16)
-            for which in range(hal.shape[0]):
-                hal[which, side] = jnp.zeros(hal.shape[2:], BF16)
-            hfull[side] = jnp.zeros(hfull.shape[1:], BF16)
-
-    halo_start(x_halo)
+    def wide_halos(k, v):
+        both = halo_copies(
+            k, v.at[:, 2], v.at[:, rows + 1], v.at[:, rows + 2], v.at[:, 1]
+        )
+        third = halo_copies(
+            k + 1,
+            v.at[:, 3, :, pl.ds(0, 128)],
+            v.at[:, rows, :, pl.ds(128, 128)],
+            v.at[:, rows + 3, :, pl.ds(0, 128)],
+            v.at[:, 0, :, pl.ds(128, 128)],
+        )
+        return both, third
+
+    x_halos = wide_halos(0, xs)
+    g_halos = wide_halos(8, gs)
 
     def coarse_halo(k):
         return halo_copies(
@@ -559,10 +553,31 @@
 
     zero_rows = jnp.zeros((frames, 128), F32)
     sums = lax.fori_loop(0, frames, load_x, (zero_rows, zero_rows), unroll=4)
+    g_copy.start()
+    pl.semaphore_wait(barrier, n + nd - 2)
     stat_start(0, jnp.concatenate(sums, axis=0))
-    g_copy = pltpu.make_async_copy(cot_hbm, raw, local_sem.at[1])
-    g_copy.start()
-    halo_start(g_halo)
+    for copies in x_halos:
+        halo_start(copies)
+
+    @pl.when(me == 0)
+    def _():
+        for v in (xs, gs):
+            v[:, 0:2] = jnp.zeros((frames, 2, cols, 256), BF16)
+        for which in range(hal.shape[0]):
+            hal[which, 0] = jnp.zeros(hal.shape[2:], BF16)
+        hfull[0] = jnp.zeros(hfull.shape[1:], BF16)
+
+    @pl.when(me == n - 1)
+    def _():
+        for v in (xs, gs):
+            v[:, rows + 2 : rows + 4] = jnp.zeros((frames, 2, cols, 256), BF16)
+        for which in range(hal.shape[0]):
+            hal[which, 1] = jnp.zeros(hal.shape[2:], BF16)
+        hfull[1] = jnp.zeros(hfull.shape[1:], BF16)
+
+    for v in (xs, gs):
+        v[:, 0, :, 0:128] = jnp.zeros((frames, cols, 128), BF16)
+        v[:, rows + 3, :, 128:256] = jnp.zeros((frames, cols, 128), BF16)
 
     def conditioning():
         entry = lax.broadcasted_iota(jnp.int32, (frames, 128), 1)
@@ -596,6 +611,20 @@
 
     conditioning()
 
+    g_copy.wait()
+
+    def load_cotangent(f, carry):
+        live = jnp.where(f < live_ref[0], 1.0, 0.0)
+        even, odd = pair_halves(paired(raw[f]))
+        both = jnp.concatenate([even, odd], axis=-1)
+        gs[f, 2 : 2 + rows] = (both * live).astype(BF16)
+        return carry
+
+    lax.fori_loop(0, frames, load_cotangent, 0, unroll=4)
+    for copies in g_halos:
+        halo_start(copies)
+
+
     def tap(index):
         first = (index // 2) * 128
         last = min(first + 128, cw_ref.shape[1])
@@ -716,19 +745,8 @@
     coarse_weights(stacked(3), w3f, w3b)
     coarse_weights(stacked(4), w4f, w4b)
 
-    halo_wait(x_halo)
-
-    def load_x_halo(f, carry):
-        zero = jnp.zeros((1, cols, 128), F32)
-        top = paired(xh[0, 0, f])
-        low = paired(xh[0, 1, f])
-        xs[f, 0] = jnp.concatenate([zero, top[0:1]], axis=-1)[0].astype(BF16)
-        xs[f, 1] = jnp.concatenate([top[1:2], top[2:3]], axis=-1)[0].astype(BF16)
-        xs[f, rows + 2] = jnp.concatenate([low[0:1], low[1:2]], axis=-1)[0].astype(BF16)
-        xs[f, rows + 3] = jnp.concatenate([low[2:3], zero], axis=-1)[0].astype(BF16)
-        return carry
-
-    lax.fori_loop(0, frames, load_x_halo, 0, unroll=4)
+    for copies in x_halos:
+        halo_wait(copies)
     norm_forward(0, stat_total(0), False)
 
     def first_layer(f, carry):
@@ -746,28 +764,12 @@
     sums = lax.fori_loop(0, frames, first_layer, (zero_rows, zero_rows), unroll=4)
     stat_start(1, jnp.concatenate(sums, axis=0))
 
-    g_copy.wait()
-    halo_wait(g_halo)
+    for copies in g_halos:
+        halo_wait(copies)
 
     def load_g(f, carry):
-        live = jnp.where(f < live_ref[0], 1.0, 0.0)
-        even, odd = pair_halves(paired(raw[f]))
-        own = jnp.concatenate([even, odd], axis=-1)
-        zero = jnp.zeros((1, cols, 128), F32)
-        top = paired(xh[1, 0, f])
-        low = paired(xh[1, 1, f])
-        g = jnp.concatenate(
-            [
-                jnp.concatenate([zero, top[0:1]], axis=-1),
-                jnp.concatenate([top[1:2], top[2:3]], axis=-1),
-                own,
-                jnp.concatenate([low[0:1], low[1:2]], axis=-1),
-                jnp.concatenate([low[2:3], zero], axis=-1),
-            ],
-            axis=0,
-        )
-        g = jnp.where(block_mask(g.shape, 2), g * live, 0.0)
-        put_e(eg, f, 0, g)
+        g = gs[f].astype(F32)
+        put_e(eg, f, 0, jnp.where(block_mask(g.shape, 2), g, 0.0))
         gsa[f] = dot_nn(window(eg, f, 1, rows + 2), wsb[...]).reshape(rows + 2, cols, 256)
         return carry
 
@@ -952,7 +954,7 @@
         h = z * gate
         put_ec(ec4, hf, jnp.where(block_mask(h.shape, 1), h, 0.0))
         g = gh4[hf] * (gate + h * (1.0 - gate))
-        gz4[hf] = g
+        gzc[hf] = g
         own = g[1 : rows + 1]
         xhat = v[1 : rows + 1] * param(3, RSTD, hf) + param(3, NMR, hf)
         return put_row(shift, hf, coarse_sum(own)), put_row(scale, hf, coarse_sum(own * xhat))
@@ -977,7 +979,7 @@
     def third_back(hf, carry):
         shift, scale = carry
         g = (
-            gz4[hf] * param(3, ALPHA, hf)
+            gzc[hf] * param(3, ALPHA, hf)
             + c3[hf] * param(3, COEF, hf)
             + param(3, BIAS, hf)
         )
@@ -988,7 +990,7 @@
         z = v * param(2, ALPHA, hf) + param(2, BETA, hf)
         gate = logistic(z)
         own = back * (gate + z * gate * (1.0 - gate))
-        gz3[hf, 1 : rows + 1] = own
+        gzc[hf, 1 : rows + 1] = own
         xhat = v * param(2, RSTD, hf) + param(2, NMR, hf)
         return put_row(shift, hf, coarse_sum(own)), put_row(scale, hf, coarse_sum(own * xhat))
 
@@ -999,13 +1001,7 @@
     halo_wait(y_halo)
 
     def result_copy(f):
-        return pltpu.make_async_copy(raw.at[f], res_hbm.at[f], out_sem.at[f])
-
-    def unpair(lo, hi):
-        count = lo.shape[0]
-        both = jnp.stack([lo, hi], axis=1).reshape(count * 2, cols, 128)
-        tmp[0 : 2 * count, pl.ds(0, cols, stride=2), :] = both
-        tmp[0 : 2 * count, pl.ds(1, cols, stride=2), :] = swap(both)
+        return pltpu.make_async_copy(gz.at[f, pl.ds(1, rows)], io_hbm.at[f], out_sem.at[f])
 
     def merge(hf, carry):
         for side, row in ((0, 0), (1, rows + 1)):
@@ -1019,9 +1015,7 @@
         for hi in range(2):
             f = hf + hi * half
             out = dot_nt(window(esk, f, 2, rows), wsf[...]) + both[:, hi * 256 : hi * 256 + 256]
-            out = out.reshape(rows, cols, 256)
-            unpair(out[:, :, 0:128], out[:, :, 128:256])
-            raw[f] = tmp[:, :, 0:64].astype(BF16)
+            gz[f, 1 : rows + 1] = out.reshape(rows, cols, 256)
             result_copy(f).start()
         return carry
 
@@ -1038,10 +1032,10 @@
             v = dv[hf, row]
             z = v * param(2, ALPHA, hf) + param(2, BETA, hf)
             gate = logistic(z)
-            gz3[hf, row] = hal[4, side, hf].astype(F32) * (gate + z * gate * (1.0 - gate))
+            gzc[hf, row] = hal[4, side, hf].astype(F32) * (gate + z * gate * (1.0 - gate))
         g = (
             gco[hf]
-            + gz3[hf] * param(2, ALPHA, hf)
+            + gzc[hf] * param(2, ALPHA, hf)
             + dv[hf] * param(2, COEF, hf)
             + param(2, BIAS, hf)
         )
@@ -1058,14 +1052,14 @@
             f = hf + hi * half
             total = gsa[f] + back[:, :, hi * 256 : hi * 256 + 256]
             gsa[f] = total
-            put_e(eg2, f, 0, jnp.where(block_mask(total.shape, 1), total, 0.0))
+            put_e(eg, f, 0, jnp.where(block_mask(total.shape, 1), total, 0.0))
         return carry
 
     lax.fori_loop(0, half, down_back, 0, unroll=4)
 
     def second_back(f, carry):
         shift, scale = carry
-        back = dot_nn(window(eg2, f, 1, rows), w2b[...]).reshape(rows, cols, 256)
+        back = dot_nn(window(eg, f, 1, rows), w2b[...]).reshape(rows, cols, 256)
         hfout[0, f] = back[0, :, 0:128].astype(BF16)
         hfout[1, f] = back[rows - 1, :, 128:256].astype(BF16)
         v = c1[f, 1 : rows + 1]
@@ -1076,11 +1070,13 @@
         xhat = v * wide(1, RSTD, f) + wide(1, NMR, f)
         return put_row(shift, f, full_sum(own)), put_row(scale, f, full_sum(own * xhat))
 
+    for f in range(frames):
+        result_copy(f).wait()
     sums = lax.fori_loop(0, frames, second_back, (zero_rows, zero_rows), unroll=4)
     stat_start(6, jnp.concatenate(sums, axis=0))
     halo_start(g_h2_halo)
     down_kernel_grad(stacked(2))
-    fine_kernel_grad(stacked(1), e2, 2, eg2, 1)
+    fine_kernel_grad(stacked(1), e2, 2, eg, 1)
     gather_start(1)
     gather_space(0)
     halo_wait(g_h2_halo)
@@ -1118,49 +1114,72 @@
     pack_start(1)
     gather_all(0)
     gather_spread(1)
+    gather_space(2)
 
     def frames_copy(f):
-        slot = lax.rem(f, 2)
-        return pltpu.make_async_copy(fst.at[slot], fg_hbm.at[f], fg_sem.at[slot])
+        return pltpu.make_async_copy(
+            gz.at[f, pl.ds(1, rows)], io_hbm.at[frames + f], fg_sem.at[f]
+        )
 
     def frames_back(f, carry):
-        g = (
+        gz[f, 1 : rows + 1] = (
             gsa[f, 1 : rows + 1]
             + gz[f, 1 : rows + 1] * wide(0, ALPHA, f)
             + xs[f, 2 : rows + 2].astype(F32) * wide(0, COEF, f)
             + wide(0, BIAS, f)
         )
-        unpair(g[:, :, 0:128], g[:, :, 128:256])
-
-        @pl.when(f >= 2)
-        def _():
-            frames_copy(f - 2).wait()
-
-        fst[lax.rem(f, 2)] = tmp[:, :, 0:64]
         frames_copy(f).start()
         return carry
 
-    lax.fori_loop(0, frames, frames_back, 0, unroll=4)
-    gather_space(2)
+    lax.fori_loop(0, half, frames_back, 0, unroll=4)
     gather_all(1)
     gather_spread(2)
+    lax.fori_loop(half, frames, frames_back, 0, unroll=4)
     gather_all(2)
-    for stage in range(3):
-        gather_finish(stage)
     for off in range(1, nd):
         for which in range(2):
             pack_copy(which, off, dp_before(off)).wait_recv()
             pack_copy(which, off, dp).wait_send()
-    for slot in range(slots):
-        for owner in range(nd):
-            lane = (slot * nd + owner) * 128
-            gout_ref[:, lane : lane + 128] = gall[owner, slot]
-
-    frames_copy(frames - 2).wait()
-    frames_copy(frames - 1).wait()
+    total_frames = nd * frames
+    every = packs[...].reshape(total_frames, 896)
+    embedded, hot = every[:, 512:768], every[:, 768:896]
+    g_embed = 0.0
+    for k in range(4):
+        dmod = every[:, k * 128 : (k + 1) * 128]
+        acc[1, :, k * 128 : k * 128 + 128] = lax.dot_general(
+            embedded, dmod, (((0,), (0,)), ((), ())), precision=HIGH, preferred_element_type=F32
+        )
+        lane = 512 + k % 2 * 128
+        acc[1, 128 + k // 2 : 129 + k // 2, lane : lane + 128] = jnp.sum(
+            dmod, axis=0, keepdims=True
+        )
+        g_embed = g_embed + lax.dot_general(
+            dmod, nmv[k], (((1,), (1,)), ((), ())), precision=HIGH, preferred_element_type=F32
+        )
+    acc[1, 0:128, 512:768] = lax.dot_general(
+        hot, g_embed, (((0,), (0,)), ((), ())), precision=HIGH, preferred_element_type=F32
+    )
+
+    def par_copy(e):
+        return pltpu.make_async_copy(
+            acc.at[e // 4, :, pl.ds(e % 4 * 256, 256)], par_hbm.at[e], local_sem.at[e]
+        )
+
+    for e in range(4, 7):
+        par_copy(e).start()
+    for stage in range(3):
+        gather_finish(stage)
+    for tile in range(32):
+        row, lane = tile // 2 % 4 * 64, tile // 8 * 256 + tile % 2 * 128
+        acc[0, row : row + 64, lane : lane + 128] = gall[tile % nd, tile // nd].astype(F32)
+    for e in range(4):
+        par_copy(e).start()
+
+    for e in range(7):
+        par_copy(e).wait()
     for f in range(frames):
-        result_copy(f).wait()
-    for copies in (x_halo, g_halo, g_h4_halo, d_halo, c3_halo, y_halo, g_h3_halo, g_h2_halo):
+        frames_copy(f).wait()
+    for copies in (*x_halos, *g_halos, g_h4_halo, d_halo, c3_halo, y_halo, g_h3_halo, g_h2_halo):
         halo_finish(copies)
 
 
@@ -1172,19 +1191,16 @@
     coarse_e = (half, rows + 2, cols, 384)
     scratch = [
         VM((count, strip, breadth, 64), BF16),
-        VM((2, 2, count, 3, breadth, 64), BF16),
         VM((strip, breadth, 128), F32),
-        VM((2, strip, breadth, 64), F32),
+        VM((count, rows + 4, cols, 256), BF16),
         VM((count, rows + 4, cols, 256), BF16),
         VM(fine, BF16),
         VM(fine, BF16),
         VM(fine, BF16),
         VM(fine, BF16),
-        VM((count, rows + 2, cols, 512), BF16),
         VM((count, rows + 2, cols, 256), F32),
         VM((count, rows + 2, cols, 256), F32),
         VM((count, rows + 2, cols, 256), F32),
-        VM(coarse, F32),
         VM(coarse, F32),
         VM(coarse, F32),
         VM(coarse, F32),
@@ -1226,13 +1242,14 @@
         VM((n, 32 // nd, 64 // n, 128), F32),
         VM((n, 32 // nd, 64 // n, 128), F32),
         VM((nd, 32 // nd, 64, 128), BF16),
+        VM((nd, count, 896), F32),
         pltpu.SemaphoreType.DMA((7,)),
         pltpu.SemaphoreType.DMA((count,)),
-        pltpu.SemaphoreType.DMA((2,)),
+        pltpu.SemaphoreType.DMA((count,)),
         pltpu.SemaphoreType.DMA((8, n - 1)),
         pltpu.SemaphoreType.DMA((8, n - 1)),
-        pltpu.SemaphoreType.DMA((8, 2)),
-        pltpu.SemaphoreType.DMA((8, 2)),
+        pltpu.SemaphoreType.DMA((10, 2)),
+        pltpu.SemaphoreType.DMA((10, 2)),
         pltpu.SemaphoreType.DMA((4, 2, nd - 1)),
         pltpu.SemaphoreType.DMA((4, 2, nd - 1)),
         pltpu.SemaphoreType.DMA((3, 2, n - 1)),
@@ -1240,20 +1257,18 @@
     ]
     smem = pl.BlockSpec(memory_space=pltpu.SMEM)
     vmem = pl.BlockSpec(memory_space=pltpu.VMEM)
-    hbm = pl.BlockSpec(memory_space=pl.ANY)
+    hbm = pl.BlockSpec(memory_space=pltpu.HBM)
     return pl.pallas_call(
         functools.partial(step_kernel, nd, n),
         out_shape=(
-            jax.ShapeDtypeStruct(frames.shape, BF16),
-            jax.ShapeDtypeStruct(frames.shape, F32),
-            jax.ShapeDtypeStruct((64, 4096), BF16),
-            jax.ShapeDtypeStruct((nd, count, 896), F32),
+            jax.ShapeDtypeStruct((2 * count, rows, cols, 256), F32),
+            jax.ShapeDtypeStruct((7, 256, 256), F32),
         ),
         in_specs=[hbm, hbm, smem, smem, smem, smem, vmem, hbm, vmem],
-        out_specs=(hbm, hbm, vmem, vmem),
+        out_specs=(hbm, hbm),
         scratch_shapes=scratch,
         compiler_params=pltpu.CompilerParams(
-            collective_id=0, has_side_effects=True, vmem_limit_bytes=62 * 1024 * 1024
+            collective_id=0, has_side_effects=True, vmem_limit_bytes=55 * 1024 * 1024
         ),
         name="step",
     )(frames, cotangent, actions, noise_ids, games, live_counts, cw, nm, table)
@@ -1268,6 +1283,142 @@
     fixed_v = square_new / fix_two
     weight_new = weight - rate * (fixed_m / (jnp.sqrt(fixed_v) + ADAM_EPS) + DECAY * weight)
     return (moment_new, square_new, weight_new, weight_new.astype(BF16))
+
+
+def finish_kernel(
+    io_hbm,
+    par_hbm,
+    cw,
+    cm,
+    cv,
+    nm,
+    nmo,
+    nsq,
+    tab,
+    tmo,
+    tsq,
+    res_out,
+    fg_out,
+    *refs,
+):
+    outs, refs = refs[:12], refs[12:]
+    stages, refs = refs[:12], refs[12:]
+    io, par, tmp, rs, fs, gmap, in_sem, pin_sem, fg_sem, out_sem, par_sem = refs
+    frames, rows, cols = rs.shape[0], io.shape[1], io.shape[2]
+
+    def frame_in(f):
+        return pltpu.make_async_copy(io_hbm.at[f], io.at[f], in_sem.at[f])
+
+    def par_in(e):
+        return pltpu.make_async_copy(par_hbm.at[e], par.at[e], pin_sem.at[e])
+
+    for e in range(7):
+        par_in(e).start()
+    for f in range(2 * frames):
+        frame_in((f + frames) % (2 * frames)).start()
+    out_copies = [
+        pltpu.make_async_copy(stages[i], outs[i], par_sem.at[i]) for i in range(12)
+    ]
+
+    def update(first, at, weight, moment, square, grad, rate):
+        new = adamw(weight, moment, square, grad, rate)
+        for i in range(4):
+            stages[first + i][at] = new[i]
+
+    wide = cw.shape[1]
+    for c in range(16):
+        if c % 4 == 0:
+            par_in(c // 4).wait()
+        lanes = slice(c * 256, min(c * 256 + 256, wide))
+        at = (slice(None), lanes)
+        grad = par[c // 4, c % 4 * 64 : c % 4 * 64 + 64, 0 : lanes.stop - lanes.start]
+        update(0, at, cw[at], cm[at], cv[at], grad, 0.05)
+    for i in range(4):
+        out_copies[i].start()
+
+    def unpair(v):
+        both = jnp.stack([v[:, :, 0:128], v[:, :, 128:256]], axis=1).reshape(rows * 2, cols, 128)
+        tmp[:, pl.ds(0, cols, stride=2), :] = both
+        tmp[:, pl.ds(1, cols, stride=2), :] = swap(both)
+        return tmp[:, :, 0:64]
+
+    def frame_copies(f):
+        return (
+            pltpu.make_async_copy(fs.at[f], fg_out.at[f], fg_sem.at[f]),
+            pltpu.make_async_copy(rs.at[f], res_out.at[f], out_sem.at[f]),
+        )
+
+    def put_frames(f, carry):
+        frame_in(frames + f).wait()
+        fs[f] = unpair(io[frames + f])
+        frame_copies(f)[0].start()
+        return carry
+
+    lax.fori_loop(0, frames, put_frames, 0)
+
+    def put_result(f, carry):
+        frame_in(f).wait()
+        rs[f] = unpair(io[f]).astype(BF16)
+        frame_copies(f)[1].start()
+        return carry
+
+    lax.fori_loop(0, frames, put_result, 0)
+
+    for e in range(4, 7):
+        par_in(e).wait()
+    for k in range(4):
+        lane = k % 2 * 128
+        gmap[0:256, k, :] = par[4 + k // 2, :, lane : lane + 128]
+        gmap[256, k : k + 1, :] = par[6, 128 + k // 2 : 129 + k // 2, lane : lane + 128]
+    at = slice(None)
+    update(4, at, nm[...], nmo[...], nsq[...], gmap[...], 0.04)
+    for i in range(4, 8):
+        out_copies[i].start()
+    update(8, at, tab[...], tmo[...], tsq[...], par[6, 0 : tab.shape[0]], 0.5)
+    for i in range(8, 12):
+        out_copies[i].start()
+    for f in range(frames):
+        for copy in frame_copies(f):
+            copy.wait()
+    for copy in out_copies:
+        copy.wait()
+
+
+def run_finish(shape, io, par, conv, norm, table):
+    count, strip, breadth, _ = shape
+    hbm = pl.BlockSpec(memory_space=pl.ANY)
+    vmem = pl.BlockSpec(memory_space=pltpu.VMEM)
+    params = [
+        jax.ShapeDtypeStruct(v[0].shape, dtype)
+        for v in (conv, norm, table)
+        for dtype in (F32, F32, F32, BF16)
+    ]
+    return pl.pallas_call(
+        finish_kernel,
+        out_shape=(
+            jax.ShapeDtypeStruct(shape, BF16),
+            jax.ShapeDtypeStruct(shape, F32),
+            *params,
+        ),
+        in_specs=[hbm, hbm] + [vmem] * 9,
+        out_specs=(hbm,) * 14,
+        scratch_shapes=[VM(v.shape, v.dtype) for v in params]
+        + [
+            VM(io.shape, F32),
+            VM(par.shape, F32),
+            VM((strip, breadth, 128), F32),
+            VM(shape, BF16),
+            VM(shape, F32),
+            VM(norm[0].shape, F32),
+            pltpu.SemaphoreType.DMA((2 * count,)),
+            pltpu.SemaphoreType.DMA((7,)),
+            pltpu.SemaphoreType.DMA((count,)),
+            pltpu.SemaphoreType.DMA((count,)),
+            pltpu.SemaphoreType.DMA((12,)),
+        ],
+        compiler_params=pltpu.CompilerParams(vmem_limit_bytes=48 * 1024 * 1024),
+        name="finish",
+    )(io, par, *conv, *norm, *table)
 
 
 def local(
@@ -1289,27 +1440,28 @@
     table_moment,
     table_square,
 ):
-    cw = conv_weight.T
-    nm = jnp.transpose(norm_map, (1, 0, 2))
-    result, frames_grad, grads, packs = run_step(
-        nd, ns, frames, cotangent, actions, noise_ids, games, live_counts, cw, nm, emb_table
+    conv = [v.T for v in (conv_weight, conv_moment, conv_square)]
+    norm = [jnp.transpose(v, (1, 0, 2)) for v in (norm_map, norm_moment, norm_square)]
+    table = (emb_table, table_moment, table_square)
+    io, par = run_step(
+        nd,
+        ns,
+        frames,
+        cotangent,
+        actions,
+        noise_ids,
+        games,
+        live_counts,
+        conv[0],
+        norm[0],
+        emb_table,
     )
-    grad_t = grads[:, : conv_weight.shape[0]].astype(F32)
-    conv_out = [v.T for v in adamw(cw, conv_moment.T, conv_square.T, grad_t, 0.05)]
-    packs = packs.reshape(-1, 896)
-    dmods = packs[:, 0:512]
-    embedded = packs[:, 512:768]
-    hot = packs[:, 768 : 768 + emb_table.shape[0]]
-    top = jnp.dot(embedded.T, dmods, precision=HIGH).reshape(256, 4, 128)
-    last = jnp.sum(dmods, axis=0).reshape(1, 4, 128)
-    grad_map = jnp.concatenate([top, last], axis=0).transpose(1, 0, 2)
-    norm_out = adamw(norm_map, norm_moment, norm_square, grad_map, 0.04)
-    g_embed = jnp.dot(
-        dmods, norm_map[:, :-1].transpose(0, 2, 1).reshape(512, 256), precision=HIGH
+    result, frames_grad, *new = run_finish(
+        frames.shape, io, par, conv, norm, table
     )
-    grad_table = jnp.dot(hot.T, g_embed, precision=HIGH)
-    table_out = adamw(emb_table, table_moment, table_square, grad_table, 0.5)
-    return (result, frames_grad, *conv_out, *norm_out, *table_out)
+    conv_out = [v.T for v in new[0:4]]
+    norm_out = [jnp.transpose(v, (1, 0, 2)) for v in new[4:8]]
+    return (result, frames_grad, *conv_out, *norm_out, *new[8:12])
 
 
 def solution(mesh):

time: 103 us -> 87 us (0.84)
  other arithmetic: 6.48 us -> 0 us
  local copies, waits for them, and re-layouts: 5.69 us -> 0.04 us
  matrix products: 2.33 us -> 0 us
  Pallas kernels: 86.7 us -> 85.1 us
    pallas_call x1, Pallas kernels: 86.7 us -> 76.2 us  [run_step(): pl.pallas_call(functools.partial(step_kernel, nd, n), out_shape=(jax.Shap...]
    pallas_call x0 -> x1, Pallas kernels: none -> 8.89 us  [run_finish(): pl.pallas_call(finish_kernel, out_shape=(jax.ShapeDtypeStruct(shape, BF16...]
    unnamed x22 -> x18, local copies, waits for them, and re-layouts: 5.47 us -> 0.04 us
    transpose x1 -> x0, other arithmetic: 4.36 us -> none  [local(): conv_out = [v.T for v in adamw(cw, conv_moment.T, conv_square.T, grad_t,...]
    dot_general x3 -> x0, matrix products: 2.33 us -> none  [the longest x1 1.11 us: local(): grad_table = jnp.dot(hot.T, g_embed, precision=HIGH)]
    convert_element_type x1 -> x0, other arithmetic: 2.09 us -> none  [adamw(): return (moment_new, square_new, weight_new, weight_new.astype(BF16))]
where the time goes in v4:
time: 87 us; the launch traced here: 86.8 us
  Pallas kernels  85.1 us (98%)
  between operations  1.63 us (2%)
    pallas_call x1, Pallas kernels, run_step(): pl.pallas_call(functools.partial(step_kernel, nd, n), out_shape=(jax.Shap...  76.2 us
    pallas_call x1, Pallas kernels, run_finish(): pl.pallas_call(finish_kernel, out_shape=(jax.ShapeDtypeStruct(shape, BF16...  8.89 us

profile of v4, /device:TPU:0, one launch (start us, length us, event | category | flops | bytes accessed | tf_op | source)
XLA Modules:
  0.0 86.8 jit_solution(15486500631156723954)
XLA Ops:
  1.3 0.0 copy-start
  1.3 0.0 copy-start.1
  1.3 0.0 copy-start.2
  1.3 0.0 copy-start.3
  1.3 0.0 copy-start.4
  1.3 0.0 copy-start.5
  1.4 0.0 copy-start.6
  1.4 0.0 copy-start.7
  1.4 0.0 copy-start.8
  1.4 76.2 %step.1 = (f32[16,8,32,256]{3,2,1,0:T(8,128)}, f32[7,256,256]{2,1,0:T(8,128)}) custom-call(bf16[8,16,64,64]{3,2,1,0:T(8,128)(2,1)} %x_hbm.1, bf16[8,16,64,64]{3,2,1,0:T(8,128)(2,1)} %cot_hbm.1, s32[8]{0:T(128)} %act_ref.1, s32[8]{0:T(128)} %noise_ref.1, s32[8]{0:T(128)} %game_ref.1, s32[1]{0:T(128)S(6)} %copy.29.live_ref, f32[64,4032]{1,0:T(8,128)} %bitcast.14, ...), custom_call_target="tpu_custom_call" | custom-call | tf_op jit(solution)/shard_map/step/pallas_call | solution.py:1261
  77.6 0.0 copy-done
  77.7 0.0 copy-done.1
  77.7 0.0 copy-done.2
  77.7 0.0 copy-done.3
  77.7 0.0 copy-done.4
  77.7 0.0 copy-done.5
  77.7 0.0 copy-done.6
  77.7 0.0 copy-done.7
  77.7 0.0 copy-done.8
  77.7 8.9 %finish.1 = (bf16[8,16,64,64]{3,2,1,0:T(8,128)(2,1)}, f32[8,16,64,64]{3,2,1,0:T(8,128)}, f32[64,4032]{1,0:T(8,128)}, f32[64,4032]{1,0:T(8,128)}, f32[64,4032]{1,...) custom-call(f32[16,8,32,256]{3,2,1,0:T(8,128)} %get-tuple-element.30, ...), custom_call_target="tpu_custom_call" | custom-call | tf_op jit(solution)/shard_map/finish/pallas_call | solution.py:1396
Async XLA Ops:
  1.3 76.3 %copy-start = (f32[4032,64]{0,1:T(8,128)S(1)}, f32[4032,64]{0,1:T(8,128)}, u32[]{:S(2)}) copy-start(f32[4032,64]{0,1:T(8,128)} %param.21) | copy-start | bytes 3096580
  1.3 76.3 %copy-start.1 = (f32[4,257,128]{2,0,1:T(4,128)S(1)}, f32[4,257,128]{2,0,1:T(4,128)}, u32[]{:S(2)}) copy-start(f32[4,257,128]{2,0,1:T(4,128)} %param.24) | copy-start | bytes 1579012
  1.3 76.3 %copy-start.2 = (f32[4032,64]{0,1:T(8,128)S(1)}, f32[4032,64]{0,1:T(8,128)}, u32[]{:S(2)}) copy-start(f32[4032,64]{0,1:T(8,128)} %param.22) | copy-start | bytes 3096580
  1.3 76.3 %copy-start.3 = (f32[4032,64]{0,1:T(8,128)S(1)}, f32[4032,64]{0,1:T(8,128)}, u32[]{:S(2)}) copy-start(f32[4032,64]{0,1:T(8,128)} %param.23) | copy-start | bytes 3096580
  1.3 76.3 %copy-start.4 = (f32[4,257,128]{2,0,1:T(4,128)S(1)}, f32[4,257,128]{2,0,1:T(4,128)}, u32[]{:S(2)}) copy-start(f32[4,257,128]{2,0,1:T(4,128)} %param.25) | copy-start | bytes 1579012
  1.3 76.3 %copy-start.5 = (f32[4,257,128]{2,0,1:T(4,128)S(1)}, f32[4,257,128]{2,0,1:T(4,128)}, u32[]{:S(2)}) copy-start(f32[4,257,128]{2,0,1:T(4,128)} %param.26) | copy-start | bytes 1579012
  1.4 76.3 %copy-start.6 = (f32[108,256]{1,0:T(8,128)S(1)}, f32[108,256]{1,0:T(8,128)}, u32[]{:S(2)}) copy-start(f32[108,256]{1,0:T(8,128)} %tab.1) | copy-start | bytes 331780
  1.4 76.3 %copy-start.7 = (f32[108,256]{1,0:T(8,128)S(1)}, f32[108,256]{1,0:T(8,128)}, u32[]{:S(2)}) copy-start(f32[108,256]{1,0:T(8,128)} %tmo.1) | copy-start | bytes 331780
  1.4 76.3 %copy-start.8 = (f32[108,256]{1,0:T(8,128)S(1)}, f32[108,256]{1,0:T(8,128)}, u32[]{:S(2)}) copy-start(f32[108,256]{1,0:T(8,128)} %tsq.1) | copy-start | bytes 331780

commit v5 on v4

--- a/solution.py
+++ b/solution.py
@@ -127,6 +127,7 @@
     part,
     zbuf,
     zfull,
+    zwhole,
     gall,
     packs,
     local_sem,
@@ -226,12 +227,12 @@
         def _():
             copies[1].wait_send()
 
-    def stat_copy(k, off, slot):
+    def stat_copy(k, off, slots):
         return pltpu.make_async_remote_copy(
-            src_ref=stat.at[k, slot],
-            dst_ref=stat.at[k, slot],
-            send_sem=stat_send.at[k, off - 1],
-            recv_sem=stat_recv.at[k, off - 1],
+            src_ref=stat.at[k, slots],
+            dst_ref=stat.at[k, slots],
+            send_sem=stat_send.at[k],
+            recv_sem=stat_recv.at[k],
             device_id={"space": lax.rem(me + off, n)},
             device_id_type=MESH,
         )
@@ -242,13 +243,12 @@
             stat_copy(k, off, me).start()
 
     def stat_total(k):
-        for off in range(1, n):
-            stat_copy(k, off, lax.rem(me + n - off, n)).wait_recv()
+        peers = stat_copy(k, 1, pl.ds(0, n - 1))
+        peers.wait_recv()
         total = stat[k, 0]
         for i in range(1, n):
             total = total + stat[k, i]
-        for off in range(1, n):
-            stat_copy(k, off, me).wait_send()
+        peers.wait_send()
         return total
 
     def wide_halos(k, v):
@@ -419,128 +419,115 @@
 
     slots = 32 // nd
     share = 64 // n
-    first_slots = [
-        [i for i in range(slots) if i * nd >= 16],
-        [i for i in range(slots) if 8 <= i * nd < 16],
-        [0],
-    ]
-
-    def dp_before(off):
-        return lax.rem(dp + nd - off, nd)
-
-    def dp_after(off):
-        return lax.rem(dp + off, nd)
-
-    def sp_before(off):
-        return lax.rem(me + n - off, n)
-
-    def sp_after(off):
-        return lax.rem(me + off, n)
-
-    def stage_slots(stage):
-        chosen = first_slots[stage]
-        return pl.ds(chosen[0], len(chosen))
-
-    def dp_copy(stage, phase, src, dst, off):
+    stage_slots = [pl.ds(1, slots - 1), pl.ds(0, 1)]
+
+    def dp_copy(which, src, dst, off):
         return pltpu.make_async_remote_copy(
             src_ref=src,
             dst_ref=dst,
-            send_sem=dp_send.at[stage, phase, off - 1],
-            recv_sem=dp_recv.at[stage, phase, off - 1],
-            device_id={"dp": dp_after(off)},
+            send_sem=dp_send.at[which],
+            recv_sem=dp_recv.at[which],
+            device_id={"dp": lax.rem(dp + off, nd)},
             device_id_type=MESH,
         )
 
-    def sp_copy(stage, phase, src, dst, off):
+    def sp_copy(which, src, dst, off):
         return pltpu.make_async_remote_copy(
             src_ref=src,
             dst_ref=dst,
-            send_sem=sp_send.at[stage, phase, off - 1],
-            recv_sem=sp_recv.at[stage, phase, off - 1],
-            device_id={"space": sp_after(off)},
+            send_sem=sp_send.at[which],
+            recv_sem=sp_recv.at[which],
+            device_id={"space": lax.rem(me + off, n)},
             device_id_type=MESH,
         )
 
-    def first_copy(stage, off, owner, slot):
-        where = stage_slots(stage)
-        return dp_copy(stage, 0, gt_ref.at[where, owner], rbuf.at[slot, where], off)
-
-    def second_copy(stage, off, row, slot):
-        where = stage_slots(stage)
-        return sp_copy(stage, 0, part.at[row, where], zbuf.at[slot, where], off)
-
-    def third_copy(stage, off, slot):
-        where = stage_slots(stage)
-        return sp_copy(stage, 1, zfull.at[slot, where], zfull.at[slot, where], off)
-
-    def fourth_copy(stage, off, slot):
-        where = stage_slots(stage)
-        return dp_copy(stage, 1, gall.at[slot, where], gall.at[slot, where], off)
-
-    def pack_copy(which, off, slot):
+    dp_peers, sp_peers = pl.ds(0, nd - 1), pl.ds(0, n - 1)
+
+    def first_all(stage):
+        where = stage_slots[stage]
+        return dp_copy(stage, rbuf.at[dp_peers, where], rbuf.at[dp_peers, where], 1)
+
+    def last_all(stage):
+        where = stage_slots[stage]
+        return dp_copy(2 + stage, gall.at[dp_peers, where], gall.at[dp_peers, where], 1)
+
+    def pack_all(which):
         lanes = pl.ds(0, 128) if which else pl.ds(128, 768)
-        return dp_copy(3, which, packs.at[slot, :, lanes], packs.at[slot, :, lanes], off)
+        ref = packs.at[dp_peers, :, lanes]
+        return dp_copy(4 + which, ref, ref, 1)
+
+    def space_all(which):
+        where = stage_slots[1 if which == 2 else 0]
+        ref = zwhole.at[sp_peers] if which == 2 else zbuf.at[sp_peers, where]
+        return sp_copy(which, ref, ref, 1)
 
     def pack_start(which):
+        lanes = pl.ds(0, 128) if which else pl.ds(128, 768)
         for off in range(1, nd):
-            pack_copy(which, off, dp).start()
+            ref = packs.at[dp, :, lanes]
+            dp_copy(4 + which, ref, ref, off).start()
 
     def gather_start(stage):
-        if not first_slots[stage]:
-            return
+        where = stage_slots[stage]
         for off in range(1, nd):
-            first_copy(stage, off, dp_after(off), dp).start()
-
-    def gather_space(stage):
-        if not first_slots[stage]:
-            return
-        where = stage_slots(stage)
-        for off in range(1, nd):
-            first_copy(stage, off, dp, dp_before(off)).wait_recv()
+            owner = lax.rem(dp + off, nd)
+            dp_copy(stage, gt_ref.at[where, owner], rbuf.at[dp, where], off).start()
+
+    def gather_dp(stage):
+        where = stage_slots[stage]
+        first_all(stage).wait_recv()
         rbuf[dp, where] = gt_ref[where, dp]
         total = rbuf[0, where].astype(F32)
         for i in range(1, nd):
             total = total + rbuf[i, where].astype(F32)
+        return total
+
+    def gather_space(stage):
+        where = stage_slots[stage]
+        total = gather_dp(stage)
+        if stage == 1:
+            zwhole[me] = total[0]
+            for off in range(1, n):
+                sp_copy(2, zwhole.at[me], zwhole.at[me], off).start()
+            return
         for z in range(n):
             part[z, where] = total[:, z * share : (z + 1) * share]
         for off in range(1, n):
-            second_copy(stage, off, sp_after(off), me).start()
-
-    def gather_spread(stage):
-        if not first_slots[stage]:
-            return
-        where = stage_slots(stage)
-        for off in range(1, n):
-            second_copy(stage, off, me, sp_before(off)).wait_recv()
+            row = lax.rem(me + off, n)
+            sp_copy(0, part.at[row, where], zbuf.at[me, where], off).start()
+
+    def gather_spread():
+        where = stage_slots[0]
+        space_all(0).wait_recv()
         zbuf[me, where] = part[me, where]
         total = zbuf[0, where]
         for i in range(1, n):
             total = total + zbuf[i, where]
         zfull[me, where] = total
         for off in range(1, n):
-            third_copy(stage, off, me).start()
+            sp_copy(1, zfull.at[me, where], zfull.at[me, where], off).start()
 
     def gather_all(stage):
-        if not first_slots[stage]:
-            return
-        where = stage_slots(stage)
-        for off in range(1, n):
-            third_copy(stage, off, sp_before(off)).wait_recv()
-        whole = jnp.concatenate([zfull[z, where] for z in range(n)], axis=1)
-        gall[dp, where] = whole.astype(BF16)
+        where = stage_slots[stage]
+        if stage == 1:
+            space_all(2).wait_recv()
+            total = zwhole[0]
+            for i in range(1, n):
+                total = total + zwhole[i]
+            gall[dp, 0] = total.astype(BF16)
+        else:
+            space_all(1).wait_recv()
+            whole = jnp.concatenate([zfull[z, where] for z in range(n)], axis=1)
+            gall[dp, where] = whole.astype(BF16)
         for off in range(1, nd):
-            fourth_copy(stage, off, dp).start()
+            dp_copy(2 + stage, gall.at[dp, where], gall.at[dp, where], off).start()
 
     def gather_finish(stage):
-        if not first_slots[stage]:
-            return
-        for off in range(1, nd):
-            fourth_copy(stage, off, dp_before(off)).wait_recv()
-            first_copy(stage, off, dp_after(off), dp).wait_send()
-            fourth_copy(stage, off, dp).wait_send()
-        for off in range(1, n):
-            second_copy(stage, off, sp_after(off), me).wait_send()
-            third_copy(stage, off, me).wait_send()
+        last_all(stage).wait_recv()
+        first_all(stage).wait_send()
+        last_all(stage).wait_send()
+        for which in (2,) if stage else (0, 1):
+            space_all(which).wait_send()
 
     x_copy.wait()
 
@@ -938,6 +925,16 @@
     sums = lax.fori_loop(0, half, third_layer, (zero_coarse, zero_coarse), unroll=4)
     stat_start(3, jnp.concatenate(list(sums) + pad_rows, axis=0))
     halo_start(c3_halo)
+
+    def result_copy(f):
+        return pltpu.make_async_copy(gz.at[f, pl.ds(1, rows)], io_hbm.at[f], out_sem.at[f])
+
+    def merge_skip(f, carry):
+        out = dot_nt(window(esk, f, 2, rows), wsf[...])
+        gz[f, 1 : rows + 1] = out.reshape(rows, cols, 256)
+        return carry
+
+    lax.fori_loop(0, half, merge_skip, 0, unroll=4)
     fine_kernel_grad(lambda t, s: 45 + (t * 3 + s) * 2, esk, 2, eg, 2)
 
     halo_wait(c3_halo)
@@ -973,6 +970,7 @@
     lax.fori_loop(0, half, coarse_output, 0, unroll=4)
     halo_start(y_halo)
     coarse_kernel_grad(stacked(4), ec4, ecg)
+    lax.fori_loop(half, frames, merge_skip, 0, unroll=4)
 
     norm_backward(3, stat_total(4), True)
 
@@ -999,9 +997,6 @@
     halo_start(g_h3_halo)
 
     halo_wait(y_halo)
-
-    def result_copy(f):
-        return pltpu.make_async_copy(gz.at[f, pl.ds(1, rows)], io_hbm.at[f], out_sem.at[f])
 
     def merge(hf, carry):
         for side, row in ((0, 0), (1, rows + 1)):
@@ -1014,15 +1009,14 @@
         both = dot_nt(coarse_window(ecy, hf), wup[...])
         for hi in range(2):
             f = hf + hi * half
-            out = dot_nt(window(esk, f, 2, rows), wsf[...]) + both[:, hi * 256 : hi * 256 + 256]
-            gz[f, 1 : rows + 1] = out.reshape(rows, cols, 256)
+            up = both[:, hi * 256 : hi * 256 + 256].reshape(rows, cols, 256)
+            gz[f, 1 : rows + 1] = gz[f, 1 : rows + 1] + up
             result_copy(f).start()
         return carry
 
     lax.fori_loop(0, half, merge, 0, unroll=4)
     coarse_kernel_grad(stacked(3), ec3, ecg3)
     up_kernel_grad()
-    gather_start(0)
 
     halo_wait(g_h3_halo)
     norm_backward(2, stat_total(5), True)
@@ -1077,13 +1071,11 @@
     halo_start(g_h2_halo)
     down_kernel_grad(stacked(2))
     fine_kernel_grad(stacked(1), e2, 2, eg, 1)
-    gather_start(1)
-    gather_space(0)
+    gather_start(0)
     halo_wait(g_h2_halo)
     norm_backward(1, stat_total(6), False)
 
-    def first_back(f, carry):
-        shift, scale = carry
+    def first_gradient(f, carry):
         for side, row in ((0, 0), (1, rows + 1)):
             v = c1[f, row]
             lanes = slice(128, 256) if side == 0 else slice(0, 128)
@@ -1094,6 +1086,15 @@
             gz[f, row] = jnp.concatenate([blank, g] if side == 0 else [g, blank], axis=-1)
         g = gz[f] * wide(1, ALPHA, f) + c1[f] * wide(1, COEF, f) + wide(1, BIAS, f)
         put_e(eg, f, 0, jnp.where(block_mask(g.shape, 1), g, 0.0))
+        return carry
+
+    lax.fori_loop(0, frames, first_gradient, 0, unroll=4)
+    fine_kernel_grad(stacked(0), e1, 2, eg, 1)
+    gather_start(1)
+    gather_space(0)
+
+    def first_back(f, carry):
+        shift, scale = carry
         back = dot_nn(window(eg, f, 1, rows), w1b[...]).reshape(rows, cols, 256)
         v = xs[f, 2 : rows + 2].astype(F32)
         z = v * wide(0, ALPHA, f) + wide(0, BETA, f)
@@ -1106,15 +1107,11 @@
     pack_start(0)
     sums = lax.fori_loop(0, frames, first_back, (zero_rows, zero_rows), unroll=4)
     stat_start(7, jnp.concatenate(sums, axis=0))
-    gather_spread(0)
+    gather_spread()
     gather_space(1)
-    fine_kernel_grad(stacked(0), e1, 2, eg, 1)
-    gather_start(2)
     norm_backward(0, stat_total(7), False)
     pack_start(1)
     gather_all(0)
-    gather_spread(1)
-    gather_space(2)
 
     def frames_copy(f):
         return pltpu.make_async_copy(
@@ -1133,13 +1130,10 @@
 
     lax.fori_loop(0, half, frames_back, 0, unroll=4)
     gather_all(1)
-    gather_spread(2)
     lax.fori_loop(half, frames, frames_back, 0, unroll=4)
-    gather_all(2)
-    for off in range(1, nd):
-        for which in range(2):
-            pack_copy(which, off, dp_before(off)).wait_recv()
-            pack_copy(which, off, dp).wait_send()
+    for which in range(2):
+        pack_all(which).wait_recv()
+        pack_all(which).wait_send()
     total_frames = nd * frames
     every = packs[...].reshape(total_frames, 896)
     embedded, hot = every[:, 512:768], every[:, 768:896]
@@ -1167,7 +1161,7 @@
 
     for e in range(4, 7):
         par_copy(e).start()
-    for stage in range(3):
+    for stage in range(2):
         gather_finish(stage)
     for tile in range(32):
         row, lane = tile // 2 % 4 * 64, tile // 8 * 256 + tile % 2 * 128
@@ -1241,19 +1235,20 @@
         VM((n, 32 // nd, 64 // n, 128), F32),
         VM((n, 32 // nd, 64 // n, 128), F32),
         VM((n, 32 // nd, 64 // n, 128), F32),
+        VM((n, 64, 128), F32),
         VM((nd, 32 // nd, 64, 128), BF16),
         VM((nd, count, 896), F32),
         pltpu.SemaphoreType.DMA((7,)),
         pltpu.SemaphoreType.DMA((count,)),
         pltpu.SemaphoreType.DMA((count,)),
-        pltpu.SemaphoreType.DMA((8, n - 1)),
-        pltpu.SemaphoreType.DMA((8, n - 1)),
+        pltpu.SemaphoreType.DMA((8,)),
+        pltpu.SemaphoreType.DMA((8,)),
         pltpu.SemaphoreType.DMA((10, 2)),
         pltpu.SemaphoreType.DMA((10, 2)),
-        pltpu.SemaphoreType.DMA((4, 2, nd - 1)),
-        pltpu.SemaphoreType.DMA((4, 2, nd - 1)),
-        pltpu.SemaphoreType.DMA((3, 2, n - 1)),
-        pltpu.SemaphoreType.DMA((3, 2, n - 1)),
+        pltpu.SemaphoreType.DMA((6,)),
+        pltpu.SemaphoreType.DMA((6,)),
+        pltpu.SemaphoreType.DMA((3,)),
+        pltpu.SemaphoreType.DMA((3,)),
     ]
     smem = pl.BlockSpec(memory_space=pltpu.SMEM)
     vmem = pl.BlockSpec(memory_space=pltpu.VMEM)

time: 87 us -> 83.4 us (0.959)
  Pallas kernels: 85.1 us -> 81.6 us
    pallas_call x1, Pallas kernels: 76.2 us -> 72.7 us  [run_step(): pl.pallas_call(functools.partial(step_kernel, nd, n), out_shape=(jax.Shap...]
where the time goes in v5:
time: 83.4 us; the launch traced here: 83.2 us
  Pallas kernels  81.6 us (98%)
  between operations  1.63 us (2%)
    pallas_call x1, Pallas kernels, run_step(): pl.pallas_call(functools.partial(step_kernel, nd, n), out_shape=(jax.Shap...  72.7 us
    pallas_call x1, Pallas kernels, run_finish(): pl.pallas_call(finish_kernel, out_shape=(jax.ShapeDtypeStruct(shape, BF16...  8.89 us

profile of v5, /device:TPU:0, one launch (start us, length us, event | category | flops | bytes accessed | tf_op | source)
XLA Modules:
  0.0 83.2 jit_solution(2384015324224581072)
XLA Ops:
  1.3 0.0 copy-start
  1.3 0.0 copy-start.1
  1.3 0.0 copy-start.2
  1.3 0.0 copy-start.3
  1.3 0.0 copy-start.4
  1.3 0.0 copy-start.5
  1.4 0.0 copy-start.6
  1.4 0.0 copy-start.7
  1.4 0.0 copy-start.8
  1.4 72.7 %step.1 = (f32[16,8,32,256]{3,2,1,0:T(8,128)}, f32[7,256,256]{2,1,0:T(8,128)}) custom-call(bf16[8,16,64,64]{3,2,1,0:T(8,128)(2,1)} %x_hbm.1, bf16[8,16,64,64]{3,2,1,0:T(8,128)(2,1)} %cot_hbm.1, s32[8]{0:T(128)} %act_ref.1, s32[8]{0:T(128)} %noise_ref.1, s32[8]{0:T(128)} %game_ref.1, s32[1]{0:T(128)S(6)} %copy.29.live_ref, f32[64,4032]{1,0:T(8,128)} %bitcast.14, ...), custom_call_target="tpu_custom_call" | custom-call | tf_op jit(solution)/shard_map/step/pallas_call | solution.py:1256
  74.1 0.0 copy-done
  74.1 0.0 copy-done.1
  74.1 0.0 copy-done.2
  74.1 0.0 copy-done.3
  74.1 0.0 copy-done.4
  74.1 0.0 copy-done.5
  74.1 0.0 copy-done.6
  74.1 0.0 copy-done.7
  74.1 0.0 copy-done.8
  74.1 8.9 %finish.1 = (bf16[8,16,64,64]{3,2,1,0:T(8,128)(2,1)}, f32[8,16,64,64]{3,2,1,0:T(8,128)}, f32[64,4032]{1,0:T(8,128)}, f32[64,4032]{1,0:T(8,128)}, f32[64,4032]{1,...) custom-call(f32[16,8,32,256]{3,2,1,0:T(8,128)} %get-tuple-element.30, ...), custom_call_target="tpu_custom_call" | custom-call | tf_op jit(solution)/shard_map/finish/pallas_call | solution.py:1391
Async XLA Ops:
  1.3 72.8 %copy-start = (f32[4032,64]{0,1:T(8,128)S(1)}, f32[4032,64]{0,1:T(8,128)}, u32[]{:S(2)}) copy-start(f32[4032,64]{0,1:T(8,128)} %param.21) | copy-start | bytes 3096580
  1.3 72.8 %copy-start.1 = (f32[4,257,128]{2,0,1:T(4,128)S(1)}, f32[4,257,128]{2,0,1:T(4,128)}, u32[]{:S(2)}) copy-start(f32[4,257,128]{2,0,1:T(4,128)} %param.24) | copy-start | bytes 1579012
  1.3 72.8 %copy-start.2 = (f32[4032,64]{0,1:T(8,128)S(1)}, f32[4032,64]{0,1:T(8,128)}, u32[]{:S(2)}) copy-start(f32[4032,64]{0,1:T(8,128)} %param.22) | copy-start | bytes 3096580
  1.3 72.8 %copy-start.3 = (f32[4032,64]{0,1:T(8,128)S(1)}, f32[4032,64]{0,1:T(8,128)}, u32[]{:S(2)}) copy-start(f32[4032,64]{0,1:T(8,128)} %param.23) | copy-start | bytes 3096580
  1.3 72.8 %copy-start.4 = (f32[4,257,128]{2,0,1:T(4,128)S(1)}, f32[4,257,128]{2,0,1:T(4,128)}, u32[]{:S(2)}) copy-start(f32[4,257,128]{2,0,1:T(4,128)} %param.25) | copy-start | bytes 1579012
  1.3 72.8 %copy-start.5 = (f32[4,257,128]{2,0,1:T(4,128)S(1)}, f32[4,257,128]{2,0,1:T(4,128)}, u32[]{:S(2)}) copy-start(f32[4,257,128]{2,0,1:T(4,128)} %param.26) | copy-start | bytes 1579012
  1.4 72.8 %copy-start.6 = (f32[108,256]{1,0:T(8,128)S(1)}, f32[108,256]{1,0:T(8,128)}, u32[]{:S(2)}) copy-start(f32[108,256]{1,0:T(8,128)} %tab.1) | copy-start | bytes 331780
  1.4 72.8 %copy-start.7 = (f32[108,256]{1,0:T(8,128)S(1)}, f32[108,256]{1,0:T(8,128)}, u32[]{:S(2)}) copy-start(f32[108,256]{1,0:T(8,128)} %tmo.1) | copy-start | bytes 331780
  1.4 72.8 %copy-start.8 = (f32[108,256]{1,0:T(8,128)S(1)}, f32[108,256]{1,0:T(8,128)}, u32[]{:S(2)}) copy-start(f32[108,256]{1,0:T(8,128)} %tsq.1) | copy-start | bytes 331780

commit v6 on v5

--- a/solution.py
+++ b/solution.py
@@ -71,12 +71,14 @@
     noise_ref,
     game_ref,
     live_ref,
-    cw_ref,
+    cw_hbm,
     nm_hbm,
-    tab_ref,
+    tab_hbm,
     io_hbm,
     par_hbm,
     raw,
+    cw_ref,
+    tab_ref,
     tmp,
     xs,
     gs,
@@ -162,6 +164,9 @@
         for k in range(4)
     ]
     map_copies.append(pltpu.make_async_copy(nm_hbm.at[256], nmb, local_sem.at[6]))
+    map_copies.append(pltpu.make_async_copy(tab_hbm, tab_ref, local_sem.at[7]))
+    weight_copy = pltpu.make_async_copy(cw_hbm, cw_ref, local_sem.at[8])
+    weight_copy.start()
     for copy in map_copies:
         copy.start()
 
@@ -419,7 +424,9 @@
 
     slots = 32 // nd
     share = 64 // n
-    stage_slots = [pl.ds(1, slots - 1), pl.ds(0, 1)]
+    early = max(1, 16 // nd)
+    stages = (0, 1, 2) if early > 1 else (0, 2)
+    stage_slots = [pl.ds(early, slots - early), pl.ds(1, 1), pl.ds(0, 1)]
 
     def dp_copy(which, src, dst, off):
         return pltpu.make_async_remote_copy(
@@ -444,51 +451,54 @@
     dp_peers, sp_peers = pl.ds(0, nd - 1), pl.ds(0, n - 1)
 
     def first_all(stage):
-        where = stage_slots[stage]
-        return dp_copy(stage, rbuf.at[dp_peers, where], rbuf.at[dp_peers, where], 1)
+        ref = rbuf.at[dp_peers, stage_slots[stage]]
+        return dp_copy(stage, ref, ref, 1)
 
     def last_all(stage):
-        where = stage_slots[stage]
-        return dp_copy(2 + stage, gall.at[dp_peers, where], gall.at[dp_peers, where], 1)
+        ref = gall.at[dp_peers, stage_slots[stage]]
+        return dp_copy(3 + stage, ref, ref, 1)
+
+    def pack_lanes(which):
+        return pl.ds(0, 128) if which else pl.ds(128, 768)
 
     def pack_all(which):
-        lanes = pl.ds(0, 128) if which else pl.ds(128, 768)
-        ref = packs.at[dp_peers, :, lanes]
-        return dp_copy(4 + which, ref, ref, 1)
+        ref = packs.at[dp_peers, :, pack_lanes(which)]
+        return dp_copy(6 + which, ref, ref, 1)
+
+    def pack_start(which):
+        ref = packs.at[dp, :, pack_lanes(which)]
+        for off in range(1, nd):
+            dp_copy(6 + which, ref, ref, off).start()
 
     def space_all(which):
-        where = stage_slots[1 if which == 2 else 0]
-        ref = zwhole.at[sp_peers] if which == 2 else zbuf.at[sp_peers, where]
+        if which >= 2:
+            ref = zwhole.at[which - 2, sp_peers]
+        else:
+            ref = zbuf.at[sp_peers, stage_slots[0]]
         return sp_copy(which, ref, ref, 1)
 
-    def pack_start(which):
-        lanes = pl.ds(0, 128) if which else pl.ds(128, 768)
-        for off in range(1, nd):
-            ref = packs.at[dp, :, lanes]
-            dp_copy(4 + which, ref, ref, off).start()
-
     def gather_start(stage):
+        if stage not in stages:
+            return
         where = stage_slots[stage]
         for off in range(1, nd):
             owner = lax.rem(dp + off, nd)
             dp_copy(stage, gt_ref.at[where, owner], rbuf.at[dp, where], off).start()
 
-    def gather_dp(stage):
+    def gather_space(stage):
+        if stage not in stages:
+            return
         where = stage_slots[stage]
         first_all(stage).wait_recv()
         rbuf[dp, where] = gt_ref[where, dp]
         total = rbuf[0, where].astype(F32)
         for i in range(1, nd):
             total = total + rbuf[i, where].astype(F32)
-        return total
-
-    def gather_space(stage):
-        where = stage_slots[stage]
-        total = gather_dp(stage)
-        if stage == 1:
-            zwhole[me] = total[0]
+        if stage > 0:
+            zwhole[stage - 1, me] = total[0]
+            ref = zwhole.at[stage - 1, me]
             for off in range(1, n):
-                sp_copy(2, zwhole.at[me], zwhole.at[me], off).start()
+                sp_copy(stage + 1, ref, ref, off).start()
             return
         for z in range(n):
             part[z, where] = total[:, z * share : (z + 1) * share]
@@ -508,25 +518,27 @@
             sp_copy(1, zfull.at[me, where], zfull.at[me, where], off).start()
 
     def gather_all(stage):
+        if stage not in stages:
+            return
         where = stage_slots[stage]
-        if stage == 1:
-            space_all(2).wait_recv()
-            total = zwhole[0]
+        if stage > 0:
+            space_all(stage + 1).wait_recv()
+            total = zwhole[stage - 1, 0]
             for i in range(1, n):
-                total = total + zwhole[i]
-            gall[dp, 0] = total.astype(BF16)
+                total = total + zwhole[stage - 1, i]
+            gall[dp, where] = total[None].astype(BF16)
         else:
             space_all(1).wait_recv()
             whole = jnp.concatenate([zfull[z, where] for z in range(n)], axis=1)
             gall[dp, where] = whole.astype(BF16)
         for off in range(1, nd):
-            dp_copy(2 + stage, gall.at[dp, where], gall.at[dp, where], off).start()
+            dp_copy(3 + stage, gall.at[dp, where], gall.at[dp, where], off).start()
 
     def gather_finish(stage):
         last_all(stage).wait_recv()
         first_all(stage).wait_send()
         last_all(stage).wait_send()
-        for which in (2,) if stage else (0, 1):
+        for which in (stage + 1,) if stage > 0 else (0, 1):
             space_all(which).wait_send()
 
     x_copy.wait()
@@ -577,14 +589,14 @@
                 | (entry == game_ref[f] + ACTIONS + NOISE_LEVELS)
             )
             hot = jnp.where((row == f) & hit, 1.0, hot)
+        for copy in map_copies:
+            copy.wait()
         table_rows = tab_ref.shape[0]
         tabp[...] = jnp.zeros(tabp.shape, F32)
         tabp[0:table_rows, :] = tab_ref[...]
         embedded = dot_high(hot, tabp[...])
         packs[dp, :, 512:768] = embedded
         packs[dp, :, 768:896] = hot
-        for copy in map_copies:
-            copy.wait()
         for k in range(4):
             mod = dot_high(embedded, nmv[k]) + nmb[k : k + 1, :]
             scale = join(mod, swap(mod)) + 1.0
@@ -724,6 +736,7 @@
     def stacked(k):
         return lambda t, s: k * 9 + t * 3 + s
 
+    weight_copy.wait()
     fine_weights(stacked(0), w1f, w1b)
     fine_weights(stacked(1), w2f, w2b)
     fine_weights(lambda t, s: 45 + (t * 3 + s) * 2, wsf, wsb)
@@ -1017,6 +1030,7 @@
     lax.fori_loop(0, half, merge, 0, unroll=4)
     coarse_kernel_grad(stacked(3), ec3, ecg3)
     up_kernel_grad()
+    gather_start(0)
 
     halo_wait(g_h3_halo)
     norm_backward(2, stat_total(5), True)
@@ -1070,8 +1084,10 @@
     stat_start(6, jnp.concatenate(sums, axis=0))
     halo_start(g_h2_halo)
     down_kernel_grad(stacked(2))
+    gather_space(0)
     fine_kernel_grad(stacked(1), e2, 2, eg, 1)
-    gather_start(0)
+    gather_start(1)
+    gather_spread()
     halo_wait(g_h2_halo)
     norm_backward(1, stat_total(6), False)
 
@@ -1090,8 +1106,9 @@
 
     lax.fori_loop(0, frames, first_gradient, 0, unroll=4)
     fine_kernel_grad(stacked(0), e1, 2, eg, 1)
-    gather_start(1)
-    gather_space(0)
+    gather_start(2)
+    gather_all(0)
+    gather_space(1)
 
     def first_back(f, carry):
         shift, scale = carry
@@ -1107,11 +1124,11 @@
     pack_start(0)
     sums = lax.fori_loop(0, frames, first_back, (zero_rows, zero_rows), unroll=4)
     stat_start(7, jnp.concatenate(sums, axis=0))
-    gather_spread()
-    gather_space(1)
+    gather_all(1)
+    gather_space(2)
     norm_backward(0, stat_total(7), False)
     pack_start(1)
-    gather_all(0)
+    gather_all(2)
 
     def frames_copy(f):
         return pltpu.make_async_copy(
@@ -1128,9 +1145,7 @@
         frames_copy(f).start()
         return carry
 
-    lax.fori_loop(0, half, frames_back, 0, unroll=4)
-    gather_all(1)
-    lax.fori_loop(half, frames, frames_back, 0, unroll=4)
+    lax.fori_loop(0, frames, frames_back, 0, unroll=4)
     for which in range(2):
         pack_all(which).wait_recv()
         pack_all(which).wait_send()
@@ -1161,7 +1176,7 @@
 
     for e in range(4, 7):
         par_copy(e).start()
-    for stage in range(2):
+    for stage in stages:
         gather_finish(stage)
     for tile in range(32):
         row, lane = tile // 2 % 4 * 64, tile // 8 * 256 + tile % 2 * 128
@@ -1185,6 +1200,8 @@
     coarse_e = (half, rows + 2, cols, 384)
     scratch = [
         VM((count, strip, breadth, 64), BF16),
+        VM(cw.shape, F32),
+        VM(table.shape, F32),
         VM((strip, breadth, 128), F32),
         VM((count, rows + 4, cols, 256), BF16),
         VM((count, rows + 4, cols, 256), BF16),
@@ -1235,20 +1252,20 @@
         VM((n, 32 // nd, 64 // n, 128), F32),
         VM((n, 32 // nd, 64 // n, 128), F32),
         VM((n, 32 // nd, 64 // n, 128), F32),
-        VM((n, 64, 128), F32),
+        VM((2, n, 64, 128), F32),
         VM((nd, 32 // nd, 64, 128), BF16),
         VM((nd, count, 896), F32),
-        pltpu.SemaphoreType.DMA((7,)),
+        pltpu.SemaphoreType.DMA((9,)),
         pltpu.SemaphoreType.DMA((count,)),
         pltpu.SemaphoreType.DMA((count,)),
         pltpu.SemaphoreType.DMA((8,)),
         pltpu.SemaphoreType.DMA((8,)),
         pltpu.SemaphoreType.DMA((10, 2)),
         pltpu.SemaphoreType.DMA((10, 2)),
-        pltpu.SemaphoreType.DMA((6,)),
-        pltpu.SemaphoreType.DMA((6,)),
-        pltpu.SemaphoreType.DMA((3,)),
-        pltpu.SemaphoreType.DMA((3,)),
+        pltpu.SemaphoreType.DMA((8,)),
+        pltpu.SemaphoreType.DMA((8,)),
+        pltpu.SemaphoreType.DMA((4,)),
+        pltpu.SemaphoreType.DMA((4,)),
     ]
     smem = pl.BlockSpec(memory_space=pltpu.SMEM)
     vmem = pl.BlockSpec(memory_space=pltpu.VMEM)
@@ -1259,7 +1276,7 @@
             jax.ShapeDtypeStruct((2 * count, rows, cols, 256), F32),
             jax.ShapeDtypeStruct((7, 256, 256), F32),
         ),
-        in_specs=[hbm, hbm, smem, smem, smem, smem, vmem, hbm, vmem],
+        in_specs=[hbm, hbm, smem, smem, smem, smem, hbm, hbm, hbm],
         out_specs=(hbm, hbm),
         scratch_shapes=scratch,
         compiler_params=pltpu.CompilerParams(

time: 83.4 us -> 82 us (0.983)
  Pallas kernels: 81.6 us -> 80.2 us
    pallas_call x1, Pallas kernels: 72.7 us -> 71.3 us  [run_step(): pl.pallas_call(functools.partial(step_kernel, nd, n), out_shape=(jax.Shap...]
where the time goes in v6:
time: 82 us; the launch traced here: 81.8 us
  Pallas kernels  80.2 us (98%)
  between operations  1.63 us (2%)
    pallas_call x1, Pallas kernels, run_step(): pl.pallas_call(functools.partial(step_kernel, nd, n), out_shape=(jax.Shap...  71.3 us
    pallas_call x1, Pallas kernels, run_finish(): pl.pallas_call(finish_kernel, out_shape=(jax.ShapeDtypeStruct(shape, BF16...  8.89 us

profile of v6, /device:TPU:0, one launch (start us, length us, event | category | flops | bytes accessed | tf_op | source)
XLA Modules:
  0.0 81.8 jit_solution(1439969584104240684)
XLA Ops:
  1.3 0.0 copy-start
  1.3 0.0 copy-start.1
  1.3 0.0 copy-start.2
  1.3 0.0 copy-start.3
  1.3 0.0 copy-start.4
  1.3 0.0 copy-start.5
  1.4 0.0 copy-start.6
  1.4 0.0 copy-start.7
  1.4 0.0 copy-start.8
  1.4 71.3 %step.1 = (f32[16,8,32,256]{3,2,1,0:T(8,128)}, f32[7,256,256]{2,1,0:T(8,128)}) custom-call(bf16[8,16,64,64]{3,2,1,0:T(8,128)(2,1)} %x_hbm.1, bf16[8,16,64,64]{3,2,1,0:T(8,128)(2,1)} %cot_hbm.1, s32[8]{0:T(128)} %act_ref.1, s32[8]{0:T(128)} %noise_ref.1, s32[8]{0:T(128)} %game_ref.1, s32[1]{0:T(128)S(6)} %copy.29.live_ref, f32[64,4032]{1,0:T(8,128)} %bitcast.14, ...), custom_call_target="tpu_custom_call" | custom-call | tf_op jit(solution)/shard_map/step/pallas_call | solution.py:1273
  72.7 0.0 copy-done
  72.7 0.0 copy-done.1
  72.7 0.0 copy-done.2
  72.7 0.0 copy-done.3
  72.7 0.0 copy-done.4
  72.7 0.0 copy-done.5
  72.7 0.0 copy-done.6
  72.7 0.0 copy-done.7
  72.7 0.0 copy-done.8
  72.8 8.9 %finish.1 = (bf16[8,16,64,64]{3,2,1,0:T(8,128)(2,1)}, f32[8,16,64,64]{3,2,1,0:T(8,128)}, f32[64,4032]{1,0:T(8,128)}, f32[64,4032]{1,0:T(8,128)}, f32[64,4032]{1,...) custom-call(f32[16,8,32,256]{3,2,1,0:T(8,128)} %get-tuple-element.30, ...), custom_call_target="tpu_custom_call" | custom-call | tf_op jit(solution)/shard_map/finish/pallas_call | solution.py:1408
Async XLA Ops:
  1.3 71.4 %copy-start = (f32[4032,64]{0,1:T(8,128)S(1)}, f32[4032,64]{0,1:T(8,128)}, u32[]{:S(2)}) copy-start(f32[4032,64]{0,1:T(8,128)} %param.21) | copy-start | bytes 3096580
  1.3 71.4 %copy-start.1 = (f32[4,257,128]{2,0,1:T(4,128)S(1)}, f32[4,257,128]{2,0,1:T(4,128)}, u32[]{:S(2)}) copy-start(f32[4,257,128]{2,0,1:T(4,128)} %param.24) | copy-start | bytes 1579012
  1.3 71.4 %copy-start.2 = (f32[4032,64]{0,1:T(8,128)S(1)}, f32[4032,64]{0,1:T(8,128)}, u32[]{:S(2)}) copy-start(f32[4032,64]{0,1:T(8,128)} %param.22) | copy-start | bytes 3096580
  1.3 71.4 %copy-start.3 = (f32[4032,64]{0,1:T(8,128)S(1)}, f32[4032,64]{0,1:T(8,128)}, u32[]{:S(2)}) copy-start(f32[4032,64]{0,1:T(8,128)} %param.23) | copy-start | bytes 3096580
  1.3 71.4 %copy-start.4 = (f32[4,257,128]{2,0,1:T(4,128)S(1)}, f32[4,257,128]{2,0,1:T(4,128)}, u32[]{:S(2)}) copy-start(f32[4,257,128]{2,0,1:T(4,128)} %param.25) | copy-start | bytes 1579012
  1.3 71.4 %copy-start.5 = (f32[4,257,128]{2,0,1:T(4,128)S(1)}, f32[4,257,128]{2,0,1:T(4,128)}, u32[]{:S(2)}) copy-start(f32[4,257,128]{2,0,1:T(4,128)} %param.26) | copy-start | bytes 1579012
  1.4 71.4 %copy-start.6 = (f32[108,256]{1,0:T(8,128)S(1)}, f32[108,256]{1,0:T(8,128)}, u32[]{:S(2)}) copy-start(f32[108,256]{1,0:T(8,128)} %tab.1) | copy-start | bytes 331780
  1.4 71.4 %copy-start.7 = (f32[108,256]{1,0:T(8,128)S(1)}, f32[108,256]{1,0:T(8,128)}, u32[]{:S(2)}) copy-start(f32[108,256]{1,0:T(8,128)} %tmo.1) | copy-start | bytes 331780
  1.4 71.4 %copy-start.8 = (f32[108,256]{1,0:T(8,128)S(1)}, f32[108,256]{1,0:T(8,128)}, u32[]{:S(2)}) copy-start(f32[108,256]{1,0:T(8,128)} %tsq.1) | copy-start | bytes 331780

commit v7 on v6

--- a/solution.py
+++ b/solution.py
@@ -67,15 +67,20 @@
     n,
     x_hbm,
     cot_hbm,
-    act_ref,
-    noise_ref,
-    game_ref,
-    live_ref,
+    act_hbm,
+    noise_hbm,
+    game_hbm,
+    live_hbm,
     cw_hbm,
     nm_hbm,
     tab_hbm,
     io_hbm,
     par_hbm,
+    gall_hbm,
+    act_ref,
+    noise_ref,
+    game_ref,
+    live_ref,
     raw,
     cw_ref,
     tab_ref,
@@ -130,7 +135,7 @@
     zbuf,
     zfull,
     zwhole,
-    gall,
+    gown,
     packs,
     local_sem,
     out_sem,
@@ -143,6 +148,7 @@
     dp_recv,
     sp_send,
     sp_recv,
+    own_sem,
 ):
     frames, strip = raw.shape[0], raw.shape[1]
     breadth = raw.shape[2]
@@ -165,6 +171,9 @@
     ]
     map_copies.append(pltpu.make_async_copy(nm_hbm.at[256], nmb, local_sem.at[6]))
     map_copies.append(pltpu.make_async_copy(tab_hbm, tab_ref, local_sem.at[7]))
+    ids = ((act_hbm, act_ref), (noise_hbm, noise_ref), (game_hbm, game_ref), (live_hbm, live_ref))
+    for i, (there, here) in enumerate(ids):
+        map_copies.append(pltpu.make_async_copy(there, here, local_sem.at[9 + i]))
     weight_copy = pltpu.make_async_copy(cw_hbm, cw_ref, local_sem.at[8])
     weight_copy.start()
     for copy in map_copies:
@@ -455,7 +464,7 @@
         return dp_copy(stage, ref, ref, 1)
 
     def last_all(stage):
-        ref = gall.at[dp_peers, stage_slots[stage]]
+        ref = gall_hbm.at[dp_peers, stage_slots[stage]]
         return dp_copy(3 + stage, ref, ref, 1)
 
     def pack_lanes(which):
@@ -517,6 +526,10 @@
         for off in range(1, n):
             sp_copy(1, zfull.at[me, where], zfull.at[me, where], off).start()
 
+    def own_copy(stage):
+        where = stage_slots[stage]
+        return pltpu.make_async_copy(gown.at[where], gall_hbm.at[dp, where], own_sem.at[stage])
+
     def gather_all(stage):
         if stage not in stages:
             return
@@ -526,18 +539,20 @@
             total = zwhole[stage - 1, 0]
             for i in range(1, n):
                 total = total + zwhole[stage - 1, i]
-            gall[dp, where] = total[None].astype(BF16)
+            gown[where] = total[None].astype(BF16)
         else:
             space_all(1).wait_recv()
             whole = jnp.concatenate([zfull[z, where] for z in range(n)], axis=1)
-            gall[dp, where] = whole.astype(BF16)
+            gown[where] = whole.astype(BF16)
         for off in range(1, nd):
-            dp_copy(3 + stage, gall.at[dp, where], gall.at[dp, where], off).start()
+            dp_copy(3 + stage, gown.at[where], gall_hbm.at[dp, where], off).start()
+        own_copy(stage).start()
 
     def gather_finish(stage):
         last_all(stage).wait_recv()
         first_all(stage).wait_send()
         last_all(stage).wait_send()
+        own_copy(stage).wait()
         for which in (stage + 1,) if stage > 0 else (0, 1):
             space_all(which).wait_send()
 
@@ -582,6 +597,8 @@
         entry = lax.broadcasted_iota(jnp.int32, (frames, 128), 1)
         row = lax.broadcasted_iota(jnp.int32, (frames, 128), 0)
         hot = jnp.zeros((frames, 128), F32)
+        for copy in map_copies:
+            copy.wait()
         for f in range(frames):
             hit = (
                 (entry == act_ref[f])
@@ -589,8 +606,6 @@
                 | (entry == game_ref[f] + ACTIONS + NOISE_LEVELS)
             )
             hot = jnp.where((row == f) & hit, 1.0, hot)
-        for copy in map_copies:
-            copy.wait()
         table_rows = tab_ref.shape[0]
         tabp[...] = jnp.zeros(tabp.shape, F32)
         tabp[0:table_rows, :] = tab_ref[...]
@@ -1171,20 +1186,15 @@
 
     def par_copy(e):
         return pltpu.make_async_copy(
-            acc.at[e // 4, :, pl.ds(e % 4 * 256, 256)], par_hbm.at[e], local_sem.at[e]
-        )
-
-    for e in range(4, 7):
+            acc.at[1, :, pl.ds(e * 256, 256)], par_hbm.at[e], local_sem.at[e]
+        )
+
+    for e in range(3):
         par_copy(e).start()
     for stage in stages:
         gather_finish(stage)
-    for tile in range(32):
-        row, lane = tile // 2 % 4 * 64, tile // 8 * 256 + tile % 2 * 128
-        acc[0, row : row + 64, lane : lane + 128] = gall[tile % nd, tile // nd].astype(F32)
-    for e in range(4):
-        par_copy(e).start()
-
-    for e in range(7):
+
+    for e in range(3):
         par_copy(e).wait()
     for f in range(frames):
         frames_copy(f).wait()
@@ -1199,6 +1209,10 @@
     coarse = (half, rows + 2, cols, 128)
     coarse_e = (half, rows + 2, cols, 384)
     scratch = [
+        pltpu.SMEM(actions.shape, jnp.int32),
+        pltpu.SMEM(noise_ids.shape, jnp.int32),
+        pltpu.SMEM(games.shape, jnp.int32),
+        pltpu.SMEM(live_counts.shape, jnp.int32),
         VM((count, strip, breadth, 64), BF16),
         VM(cw.shape, F32),
         VM(table.shape, F32),
@@ -1253,9 +1267,9 @@
         VM((n, 32 // nd, 64 // n, 128), F32),
         VM((n, 32 // nd, 64 // n, 128), F32),
         VM((2, n, 64, 128), F32),
-        VM((nd, 32 // nd, 64, 128), BF16),
+        VM((32 // nd, 64, 128), BF16),
         VM((nd, count, 896), F32),
-        pltpu.SemaphoreType.DMA((9,)),
+        pltpu.SemaphoreType.DMA((13,)),
         pltpu.SemaphoreType.DMA((count,)),
         pltpu.SemaphoreType.DMA((count,)),
         pltpu.SemaphoreType.DMA((8,)),
@@ -1266,18 +1280,18 @@
         pltpu.SemaphoreType.DMA((8,)),
         pltpu.SemaphoreType.DMA((4,)),
         pltpu.SemaphoreType.DMA((4,)),
+        pltpu.SemaphoreType.DMA((3,)),
     ]
-    smem = pl.BlockSpec(memory_space=pltpu.SMEM)
-    vmem = pl.BlockSpec(memory_space=pltpu.VMEM)
     hbm = pl.BlockSpec(memory_space=pltpu.HBM)
     return pl.pallas_call(
         functools.partial(step_kernel, nd, n),
         out_shape=(
             jax.ShapeDtypeStruct((2 * count, rows, cols, 256), F32),
-            jax.ShapeDtypeStruct((7, 256, 256), F32),
+            jax.ShapeDtypeStruct((8, 256, 256), F32),
+            jax.ShapeDtypeStruct((4 * nd, 32 // nd, 64, 128), BF16),
         ),
-        in_specs=[hbm, hbm, smem, smem, smem, smem, hbm, hbm, hbm],
-        out_specs=(hbm, hbm),
+        in_specs=[hbm] * 9,
+        out_specs=(hbm, hbm, hbm),
         scratch_shapes=scratch,
         compiler_params=pltpu.CompilerParams(
             collective_id=0, has_side_effects=True, vmem_limit_bytes=55 * 1024 * 1024
@@ -1300,6 +1314,7 @@
 def finish_kernel(
     io_hbm,
     par_hbm,
+    gall_hbm,
     cw,
     cm,
     cv,
@@ -1315,7 +1330,7 @@
 ):
     outs, refs = refs[:12], refs[12:]
     stages, refs = refs[:12], refs[12:]
-    io, par, tmp, rs, fs, gmap, in_sem, pin_sem, fg_sem, out_sem, par_sem = refs
+    io, par, gall, tmp, rs, fs, gmap, in_sem, pin_sem, fg_sem, out_sem, par_sem = refs
     frames, rows, cols = rs.shape[0], io.shape[1], io.shape[2]
 
     def frame_in(f):
@@ -1324,7 +1339,11 @@
     def par_in(e):
         return pltpu.make_async_copy(par_hbm.at[e], par.at[e], pin_sem.at[e])
 
-    for e in range(7):
+    gall_in = pltpu.make_async_copy(
+        gall_hbm.at[pl.ds(0, gall.shape[0])], gall, pin_sem.at[3]
+    )
+    gall_in.start()
+    for e in range(3):
         par_in(e).start()
     for f in range(2 * frames):
         frame_in((f + frames) % (2 * frames)).start()
@@ -1338,12 +1357,12 @@
             stages[first + i][at] = new[i]
 
     wide = cw.shape[1]
-    for c in range(16):
-        if c % 4 == 0:
-            par_in(c // 4).wait()
-        lanes = slice(c * 256, min(c * 256 + 256, wide))
+    gall_in.wait()
+    for tile in range(32):
+        lanes = slice(tile * 128, min(tile * 128 + 128, wide))
         at = (slice(None), lanes)
-        grad = par[c // 4, c % 4 * 64 : c % 4 * 64 + 64, 0 : lanes.stop - lanes.start]
+        owner, slot = tile % gall.shape[0], tile // gall.shape[0]
+        grad = gall[owner, slot, :, 0 : lanes.stop - lanes.start].astype(F32)
         update(0, at, cw[at], cm[at], cv[at], grad, 0.05)
     for i in range(4):
         out_copies[i].start()
@@ -1376,17 +1395,17 @@
 
     lax.fori_loop(0, frames, put_result, 0)
 
-    for e in range(4, 7):
+    for e in range(3):
         par_in(e).wait()
     for k in range(4):
         lane = k % 2 * 128
-        gmap[0:256, k, :] = par[4 + k // 2, :, lane : lane + 128]
-        gmap[256, k : k + 1, :] = par[6, 128 + k // 2 : 129 + k // 2, lane : lane + 128]
+        gmap[0:256, k, :] = par[k // 2, :, lane : lane + 128]
+        gmap[256, k : k + 1, :] = par[2, 128 + k // 2 : 129 + k // 2, lane : lane + 128]
     at = slice(None)
     update(4, at, nm[...], nmo[...], nsq[...], gmap[...], 0.04)
     for i in range(4, 8):
         out_copies[i].start()
-    update(8, at, tab[...], tmo[...], tsq[...], par[6, 0 : tab.shape[0]], 0.5)
+    update(8, at, tab[...], tmo[...], tsq[...], par[2, 0 : tab.shape[0]], 0.5)
     for i in range(8, 12):
         out_copies[i].start()
     for f in range(frames):
@@ -1396,7 +1415,7 @@
         copy.wait()
 
 
-def run_finish(shape, io, par, conv, norm, table):
+def run_finish(shape, io, par, gall, conv, norm, table):
     count, strip, breadth, _ = shape
     hbm = pl.BlockSpec(memory_space=pl.ANY)
     vmem = pl.BlockSpec(memory_space=pltpu.VMEM)
@@ -1412,25 +1431,26 @@
             jax.ShapeDtypeStruct(shape, F32),
             *params,
         ),
-        in_specs=[hbm, hbm] + [vmem] * 9,
+        in_specs=[hbm] * 3 + [vmem] * 9,
         out_specs=(hbm,) * 14,
         scratch_shapes=[VM(v.shape, v.dtype) for v in params]
         + [
             VM(io.shape, F32),
-            VM(par.shape, F32),
+            VM((3,) + par.shape[1:], F32),
+            VM((gall.shape[0] // 4,) + gall.shape[1:], BF16),
             VM((strip, breadth, 128), F32),
             VM(shape, BF16),
             VM(shape, F32),
             VM(norm[0].shape, F32),
             pltpu.SemaphoreType.DMA((2 * count,)),
-            pltpu.SemaphoreType.DMA((7,)),
+            pltpu.SemaphoreType.DMA((4,)),
             pltpu.SemaphoreType.DMA((count,)),
             pltpu.SemaphoreType.DMA((count,)),
             pltpu.SemaphoreType.DMA((12,)),
         ],
         compiler_params=pltpu.CompilerParams(vmem_limit_bytes=48 * 1024 * 1024),
         name="finish",
-    )(io, par, *conv, *norm, *table)
+    )(io, par, gall, *conv, *norm, *table)
 
 
 def local(
@@ -1455,7 +1475,7 @@
     conv = [v.T for v in (conv_weight, conv_moment, conv_square)]
     norm = [jnp.transpose(v, (1, 0, 2)) for v in (norm_map, norm_moment, norm_square)]
     table = (emb_table, table_moment, table_square)
-    io, par = run_step(
+    io, par, gall = run_step(
         nd,
         ns,
         frames,
@@ -1469,7 +1489,7 @@
         emb_table,
     )
     result, frames_grad, *new = run_finish(
-        frames.shape, io, par, conv, norm, table
+        frames.shape, io, par, gall, conv, norm, table
     )
     conv_out = [v.T for v in new[0:4]]
     norm_out = [jnp.transpose(v, (1, 0, 2)) for v in new[4:8]]

time: 82 us -> 80.6 us (0.983)
  Pallas kernels: 80.2 us -> 78.8 us
    pallas_call x1, Pallas kernels: 71.3 us -> 69.4 us  [run_step(): pl.pallas_call(functools.partial(step_kernel, nd, n), out_shape=(jax.Shap...]
where the time goes in v7:
time: 80.6 us; the launch traced here: 80.4 us
  Pallas kernels  78.8 us (98%)
  between operations  1.63 us (2%)
    pallas_call x1, Pallas kernels, run_step(): pl.pallas_call(functools.partial(step_kernel, nd, n), out_shape=(jax.Shap...  69.4 us
    pallas_call x1, Pallas kernels, run_finish(): pl.pallas_call(finish_kernel, out_shape=(jax.ShapeDtypeStruct(shape, BF16...  9.37 us

profile of v7, /device:TPU:0, one launch (start us, length us, event | category | flops | bytes accessed | tf_op | source)
XLA Modules:
  0.0 80.4 jit_solution(800745135197986341)
XLA Ops:
  1.3 0.0 copy-start
  1.3 0.0 copy-start.1
  1.3 0.0 copy-start.2
  1.3 0.0 copy-start.3
  1.3 0.0 copy-start.4
  1.3 0.0 copy-start.5
  1.4 0.0 copy-start.6
  1.4 0.0 copy-start.7
  1.4 0.0 copy-start.8
  1.4 69.4 %step.1 = (f32[16,8,32,256]{3,2,1,0:T(8,128)}, f32[8,256,256]{2,1,0:T(8,128)}, bf16[32,4,64,128]{3,2,1,0:T(8,128)(2,1)}) custom-call(bf16[8,16,64,64]{3,2,1,0:T(8,128)(2,1)} %x_hbm.1, bf16[8,16,64,64]{3,2,1,0:T(8,128)(2,1)} %cot_hbm.1, s32[8]{0:T(128)} %act_hbm.1, s32[8]{0:T(128)} %noise_hbm.1, s32[8]{0:T(128)} %game_hbm.1, s32[1]{0:T(128)S(6)} %copy.29.live_hbm, ...), custom_call_target="tpu_custom_call" | custom-call | tf_op jit(solution)/shard_map/step/pallas_call | solution.py:1286
  70.8 0.0 copy-done
  70.8 0.0 copy-done.1
  70.8 0.0 copy-done.2
  70.8 0.0 copy-done.3
  70.8 0.0 copy-done.4
  70.8 0.0 copy-done.5
  70.8 0.0 copy-done.6
  70.9 0.0 copy-done.7
  70.9 0.0 copy-done.8
  70.9 9.4 %finish.1 = (bf16[8,16,64,64]{3,2,1,0:T(8,128)(2,1)}, f32[8,16,64,64]{3,2,1,0:T(8,128)}, f32[64,4032]{1,0:T(8,128)}, f32[64,4032]{1,0:T(8,128)}, f32[64,4032]{1,...) custom-call(f32[16,8,32,256]{3,2,1,0:T(8,128)} %get-tuple-element.31, ...), custom_call_target="tpu_custom_call" | custom-call | tf_op jit(solution)/shard_map/finish/pallas_call | solution.py:1427
Async XLA Ops:
  1.3 69.5 %copy-start = (f32[4032,64]{0,1:T(8,128)S(1)}, f32[4032,64]{0,1:T(8,128)}, u32[]{:S(2)}) copy-start(f32[4032,64]{0,1:T(8,128)} %param.21) | copy-start | bytes 3096580
  1.3 69.5 %copy-start.1 = (f32[4,257,128]{2,0,1:T(4,128)S(1)}, f32[4,257,128]{2,0,1:T(4,128)}, u32[]{:S(2)}) copy-start(f32[4,257,128]{2,0,1:T(4,128)} %param.24) | copy-start | bytes 1579012
  1.3 69.5 %copy-start.2 = (f32[4032,64]{0,1:T(8,128)S(1)}, f32[4032,64]{0,1:T(8,128)}, u32[]{:S(2)}) copy-start(f32[4032,64]{0,1:T(8,128)} %param.22) | copy-start | bytes 3096580
  1.3 69.5 %copy-start.3 = (f32[4032,64]{0,1:T(8,128)S(1)}, f32[4032,64]{0,1:T(8,128)}, u32[]{:S(2)}) copy-start(f32[4032,64]{0,1:T(8,128)} %param.23) | copy-start | bytes 3096580
  1.3 69.5 %copy-start.4 = (f32[4,257,128]{2,0,1:T(4,128)S(1)}, f32[4,257,128]{2,0,1:T(4,128)}, u32[]{:S(2)}) copy-start(f32[4,257,128]{2,0,1:T(4,128)} %param.25) | copy-start | bytes 1579012
  1.3 69.5 %copy-start.5 = (f32[4,257,128]{2,0,1:T(4,128)S(1)}, f32[4,257,128]{2,0,1:T(4,128)}, u32[]{:S(2)}) copy-start(f32[4,257,128]{2,0,1:T(4,128)} %param.26) | copy-start | bytes 1579012
  1.4 69.5 %copy-start.6 = (f32[108,256]{1,0:T(8,128)S(1)}, f32[108,256]{1,0:T(8,128)}, u32[]{:S(2)}) copy-start(f32[108,256]{1,0:T(8,128)} %tab.1) | copy-start | bytes 331780
  1.4 69.5 %copy-start.7 = (f32[108,256]{1,0:T(8,128)S(1)}, f32[108,256]{1,0:T(8,128)}, u32[]{:S(2)}) copy-start(f32[108,256]{1,0:T(8,128)} %tmo.1) | copy-start | bytes 331780
  1.4 69.5 %copy-start.8 = (f32[108,256]{1,0:T(8,128)S(1)}, f32[108,256]{1,0:T(8,128)}, u32[]{:S(2)}) copy-start(f32[108,256]{1,0:T(8,128)} %tsq.1) | copy-start | bytes 331780

commit v8 on v7

--- a/solution.py
+++ b/solution.py
@@ -162,8 +162,14 @@
     owned = rows * cols
     ext = (rows + 2) * cols
 
-    x_copy = pltpu.make_async_copy(x_hbm, raw, local_sem.at[0])
-    x_copy.start()
+    x_copies = []
+    for piece in range(2):
+        at = pl.ds(piece * half, half)
+        x_copies.append(
+            pltpu.make_async_copy(x_hbm.at[at], raw.at[at], local_sem.at[13 * piece])
+        )
+    for copy in x_copies:
+        copy.start()
     g_copy = pltpu.make_async_copy(cot_hbm, raw, local_sem.at[1])
     map_copies = [
         pltpu.make_async_copy(nm_hbm.at[pl.ds(0, 256), k], nmv.at[k], local_sem.at[2 + k])
@@ -556,8 +562,6 @@
         for which in (stage + 1,) if stage > 0 else (0, 1):
             space_all(which).wait_send()
 
-    x_copy.wait()
-
     def load_x(f, carry):
         total, square = carry
         even, odd = pair_halves(paired(raw[f]))
@@ -566,7 +570,10 @@
         return put_row(total, f, full_sum(both)), put_row(square, f, full_sum(both * both))
 
     zero_rows = jnp.zeros((frames, 128), F32)
-    sums = lax.fori_loop(0, frames, load_x, (zero_rows, zero_rows), unroll=4)
+    sums = (zero_rows, zero_rows)
+    for piece in range(2):
+        x_copies[piece].wait()
+        sums = lax.fori_loop(piece * half, piece * half + half, load_x, sums, unroll=4)
     g_copy.start()
     pl.semaphore_wait(barrier, n + nd - 2)
     stat_start(0, jnp.concatenate(sums, axis=0))
@@ -1269,7 +1276,7 @@
         VM((2, n, 64, 128), F32),
         VM((32 // nd, 64, 128), BF16),
         VM((nd, count, 896), F32),
-        pltpu.SemaphoreType.DMA((13,)),
+        pltpu.SemaphoreType.DMA((14,)),
         pltpu.SemaphoreType.DMA((count,)),
         pltpu.SemaphoreType.DMA((count,)),
         pltpu.SemaphoreType.DMA((8,)),

time: 80.6 us -> 80.1 us (level)
  no operation moved by 1% of the time
where the time goes in v8:
time: 80.1 us; the launch traced here: 80 us
  Pallas kernels  78.3 us (98%)
  between operations  1.63 us (2%)
    pallas_call x1, Pallas kernels, run_step(): pl.pallas_call(functools.partial(step_kernel, nd, n), out_shape=(jax.Shap...  68.9 us
    pallas_call x1, Pallas kernels, run_finish(): pl.pallas_call(finish_kernel, out_shape=(jax.ShapeDtypeStruct(shape, BF16...  9.37 us

profile of v8, /device:TPU:0, one launch (start us, length us, event | category | flops | bytes accessed | tf_op | source)
XLA Modules:
  0.0 80.0 jit_solution(15170135207391694978)
XLA Ops:
  1.3 0.0 copy-start
  1.3 0.0 copy-start.1
  1.3 0.0 copy-start.2
  1.3 0.0 copy-start.3
  1.3 0.0 copy-start.4
  1.3 0.0 copy-start.5
  1.4 0.0 copy-start.6
  1.4 0.0 copy-start.7
  1.4 0.0 copy-start.8
  1.4 68.9 %step.1 = (f32[16,8,32,256]{3,2,1,0:T(8,128)}, f32[8,256,256]{2,1,0:T(8,128)}, bf16[32,4,64,128]{3,2,1,0:T(8,128)(2,1)}) custom-call(bf16[8,16,64,64]{3,2,1,0:T(8,128)(2,1)} %x_hbm.1, bf16[8,16,64,64]{3,2,1,0:T(8,128)(2,1)} %cot_hbm.1, s32[8]{0:T(128)} %act_hbm.1, s32[8]{0:T(128)} %noise_hbm.1, s32[8]{0:T(128)} %game_hbm.1, s32[1]{0:T(128)S(6)} %copy.29.live_hbm, ...), custom_call_target="tpu_custom_call" | custom-call | tf_op jit(solution)/shard_map/step/pallas_call | solution.py:1293
  70.3 0.0 copy-done
  70.3 0.0 copy-done.1
  70.4 0.0 copy-done.2
  70.4 0.0 copy-done.3
  70.4 0.0 copy-done.4
  70.4 0.0 copy-done.5
  70.4 0.0 copy-done.6
  70.4 0.0 copy-done.7
  70.4 0.0 copy-done.8
  70.4 9.4 %finish.1 = (bf16[8,16,64,64]{3,2,1,0:T(8,128)(2,1)}, f32[8,16,64,64]{3,2,1,0:T(8,128)}, f32[64,4032]{1,0:T(8,128)}, f32[64,4032]{1,0:T(8,128)}, f32[64,4032]{1,...) custom-call(f32[16,8,32,256]{3,2,1,0:T(8,128)} %get-tuple-element.31, ...), custom_call_target="tpu_custom_call" | custom-call | tf_op jit(solution)/shard_map/finish/pallas_call | solution.py:1434
Async XLA Ops:
  1.3 69.0 %copy-start = (f32[4032,64]{0,1:T(8,128)S(1)}, f32[4032,64]{0,1:T(8,128)}, u32[]{:S(2)}) copy-start(f32[4032,64]{0,1:T(8,128)} %param.21) | copy-start | bytes 3096580
  1.3 69.0 %copy-start.1 = (f32[4,257,128]{2,0,1:T(4,128)S(1)}, f32[4,257,128]{2,0,1:T(4,128)}, u32[]{:S(2)}) copy-start(f32[4,257,128]{2,0,1:T(4,128)} %param.24) | copy-start | bytes 1579012
  1.3 69.0 %copy-start.2 = (f32[4032,64]{0,1:T(8,128)S(1)}, f32[4032,64]{0,1:T(8,128)}, u32[]{:S(2)}) copy-start(f32[4032,64]{0,1:T(8,128)} %param.22) | copy-start | bytes 3096580
  1.3 69.0 %copy-start.3 = (f32[4032,64]{0,1:T(8,128)S(1)}, f32[4032,64]{0,1:T(8,128)}, u32[]{:S(2)}) copy-start(f32[4032,64]{0,1:T(8,128)} %param.23) | copy-start | bytes 3096580
  1.3 69.0 %copy-start.4 = (f32[4,257,128]{2,0,1:T(4,128)S(1)}, f32[4,257,128]{2,0,1:T(4,128)}, u32[]{:S(2)}) copy-start(f32[4,257,128]{2,0,1:T(4,128)} %param.25) | copy-start | bytes 1579012
  1.3 69.0 %copy-start.5 = (f32[4,257,128]{2,0,1:T(4,128)S(1)}, f32[4,257,128]{2,0,1:T(4,128)}, u32[]{:S(2)}) copy-start(f32[4,257,128]{2,0,1:T(4,128)} %param.26) | copy-start | bytes 1579012
  1.4 69.0 %copy-start.6 = (f32[108,256]{1,0:T(8,128)S(1)}, f32[108,256]{1,0:T(8,128)}, u32[]{:S(2)}) copy-start(f32[108,256]{1,0:T(8,128)} %tab.1) | copy-start | bytes 331780
  1.4 69.0 %copy-start.7 = (f32[108,256]{1,0:T(8,128)S(1)}, f32[108,256]{1,0:T(8,128)}, u32[]{:S(2)}) copy-start(f32[108,256]{1,0:T(8,128)} %tmo.1) | copy-start | bytes 331780
  1.4 69.0 %copy-start.8 = (f32[108,256]{1,0:T(8,128)S(1)}, f32[108,256]{1,0:T(8,128)}, u32[]{:S(2)}) copy-start(f32[108,256]{1,0:T(8,128)} %tsq.1) | copy-start | bytes 331780
